TPU v7x, 128 devices: a whole 4x4x4 slice. The times are simulated.
128 devices in a mesh: lon: 32 (over x_hi, z, y), lat: 4 (over x_lo, core).
Axes of the slice: x: 4 (x_hi: 2, x_lo: 2; x = x_hi * 2 + x_lo), y: 4, z: 4, core: 2. Of those that a mesh axis runs over, the one named last changes fastest.
Arguments:
- right_side: float32 [20, 1024, 4096], P(None, 'lat', 'lon'), may hold values from -6 to 6
- helmholtz: float32 [20, 1024, 4096], P(None, 'lat', 'lon'), may hold values from 0.3 to 3
- coupling: float32 [19, 1024, 4096], P(None, 'lat', 'lon'), may hold values from 1 to 10
Outputs:
- solution: float32 [20, 1024, 4096], P(None, 'lat', 'lon')
- residual: float32 [20, 1024, 4096], P(None, 'lat', 'lon')
All inputs are finite; a program needn't handle non-finite values.
Results may differ from a plain program's by a relative error of at most 0.0003.
Values sent between devices are 32-bit elements; how exact they have to be, the bound alone decides.
No kernel may reach another device: no remote copies, remote signals or barrier semaphores. Data moves between devices by JAX's collectives and lax.ppermute only.
A program may use at most 128 MiB of HBM per device.

v0:
```python
import math

import jax
import jax.numpy as jnp
from jax import lax
from jax.sharding import PartitionSpec as P

ITERS = 3


def with_halo(block, sides, width, periodic):
    for axis, dim in sides:
        count = lax.axis_size(axis)
        forward = [(i, i + 1) for i in range(count - 1)]
        if periodic:
            forward.append((count - 1, 0))
        backward = [(target, source) for source, target in forward]
        low = lax.ppermute(
            lax.slice_in_dim(block, block.shape[dim] - width, None, axis=dim), axis, forward
        )
        high = lax.ppermute(lax.slice_in_dim(block, 0, width, axis=dim), axis, backward)
        block = jnp.concatenate([low, block, high], axis=dim)
    return block


def passed_along(x, axis, by):
    devices = lax.axis_size(axis)
    return lax.ppermute(x, axis, [(i, (i + by) % devices) for i in range(devices)])


def cosines(rows, total_rows):
    latitude = -0.5 * math.pi + (rows + 0.5) * (math.pi / total_rows)
    return jnp.maximum(jnp.cos(latitude), 0.5)


def factors(helmholtz, coupling, cosine, north_face, south_face, lon_coeff):
    zero_level = jnp.zeros_like(coupling[:1])
    vertical_sum = jnp.concatenate([coupling, zero_level], 0) + jnp.concatenate(
        [zero_level, coupling], 0
    )
    diagonal = (
        cosine * helmholtz
        + 2.0 * lon_coeff / cosine
        + north_face
        + south_face
        + cosine * vertical_sum
    )
    offdiag = -cosine * coupling
    levels = diagonal.shape[0]
    inverse = []
    ratios = []
    pivot = diagonal[0]
    for layer in range(levels):
        if layer > 0:
            pivot = diagonal[layer] - offdiag[layer - 1] * ratios[layer - 1]
        inverse.append(1.0 / pivot)
        if layer < levels - 1:
            ratios.append(offdiag[layer] * (1.0 / pivot))
    return (offdiag, inverse, ratios)


def solve_lines(values, offdiag, inverse, ratios):
    levels = len(inverse)
    forward = [values[0] * inverse[0]]
    for layer in range(1, levels):
        forward.append((values[layer] - offdiag[layer - 1] * forward[layer - 1]) * inverse[layer])
    result = [None] * levels
    result[levels - 1] = forward[levels - 1]
    for layer in range(levels - 2, -1, -1):
        result[layer] = forward[layer] - ratios[layer] * result[layer + 1]
    return jnp.stack(result)


def combine(
    field,
    east_cells,
    west_cells,
    north_cells,
    south_cells,
    helmholtz,
    coupling,
    cosine,
    north_face,
    south_face,
    lon_coeff,
):
    zero_level = jnp.zeros_like(field[:1])
    vertical_flux = coupling * (field[:-1] - field[1:])
    vertical = jnp.concatenate([vertical_flux, zero_level], 0) - jnp.concatenate(
        [zero_level, vertical_flux], 0
    )
    result = cosine * helmholtz * field + lon_coeff / cosine * (
        2.0 * field - east_cells - west_cells
    )
    result = result + north_face * (field - north_cells) + south_face * (field - south_cells)
    return result + cosine * vertical


def operate(field, helmholtz, coupling, cosine, north_face, south_face, lon_coeff):
    lon_count = lax.axis_size("lon")
    lat_count = lax.axis_size("lat")
    lat_place = lax.axis_index("lat")
    widened = with_halo(field, (("lon", 2),), 1, True)
    east_cells = widened[:, :, 2:]
    west_cells = widened[:, :, :-2]
    heightened = with_halo(field, (("lat", 1),), 1, False)
    polar_rows = jnp.stack([field[:, 0, :], field[:, -1, :]])
    far_rows = passed_along(polar_rows, "lon", lon_count // 2)
    north_edge = jnp.where(lat_place == lat_count - 1, far_rows[1], heightened[:, -1, :])
    south_edge = jnp.where(lat_place == 0, far_rows[0], heightened[:, 0, :])
    north_cells = jnp.concatenate([heightened[:, 2:-1, :], north_edge[:, None, :]], 1)
    south_cells = jnp.concatenate([south_edge[:, None, :], heightened[:, 1:-2, :]], 1)
    return combine(
        field,
        east_cells,
        west_cells,
        north_cells,
        south_cells,
        helmholtz,
        coupling,
        cosine,
        north_face,
        south_face,
        lon_coeff,
    )


def energy_total(smooth_field, smooth_image):
    return lax.psum(jnp.sum(smooth_field * smooth_image), ("lon", "lat"))


def on_device(right_side, helmholtz, coupling):
    lat_rows = right_side.shape[1]
    lon_cells = right_side.shape[2]
    total_lat = lat_rows * lax.axis_size("lat")
    total_lon = lon_cells * lax.axis_size("lon")
    rows = (lax.axis_index("lat") * lat_rows + jnp.arange(lat_rows)).astype(jnp.float32)
    cosine = cosines(rows, total_lat)
    below = cosines(jnp.maximum(rows - 1.0, 0.0), total_lat)
    above = cosines(jnp.minimum(rows + 1.0, total_lat - 1.0), total_lat)
    south_face = ((cosine + below) * 0.5).reshape(1, -1, 1)
    north_face = ((cosine + above) * 0.5).reshape(1, -1, 1)
    cosine = cosine.reshape(1, -1, 1)
    lon_coeff = (total_lon / (2.0 * total_lat)) ** 2
    offdiag, inverse, ratios = factors(
        helmholtz, coupling, cosine, north_face, south_face, lon_coeff
    )

    def apply_operator(field):
        return operate(field, helmholtz, coupling, cosine, north_face, south_face, lon_coeff)

    def smooth(values):
        return solve_lines(values, offdiag, inverse, ratios)

    solution = jnp.zeros_like(right_side)
    residual = right_side
    smoothed = smooth(residual)
    image_smooth = apply_operator(smoothed)
    energy = energy_total(smoothed, image_smooth)
    direction = smoothed
    image_dir = image_smooth
    for iteration in range(ITERS):
        back_image = smooth(image_dir)
        curvature = lax.psum(jnp.sum(image_dir * back_image), ("lon", "lat"))
        step_length = energy / curvature
        solution = solution + step_length * direction
        residual = residual - step_length * image_dir
        smoothed = smoothed - step_length * back_image
        if iteration < ITERS - 1:
            image_smooth = apply_operator(smoothed)
            energy_next = energy_total(smoothed, image_smooth)
            step_ratio = energy_next / energy
            direction = smoothed + step_ratio * direction
            image_dir = image_smooth + step_ratio * image_dir
            energy = energy_next
    return (solution, residual)


def solution(mesh):
    in_specs = (P(None, "lat", "lon"), P(None, "lat", "lon"), P(None, "lat", "lon"))
    out_specs = (P(None, "lat", "lon"), P(None, "lat", "lon"))
    return jax.shard_map(
        on_device, mesh=mesh, in_specs=in_specs, out_specs=out_specs, check_vma=False
    )
```

profile of v0, /device:TPU:0, one launch (start us, length us, event | category | flops | bytes accessed | tf_op | source)
XLA Modules:
  0.0 527.5 jit_solution(9977972734995392593)
XLA Ops:
  0.8 2.2 broadcast_multiply_fusion
  3.1 3.6 multiply_add_fusion.3
  6.7 2.0 subtract_multiply_fusion.2
  14.0 1.9 collective-permute-start.4
  17.7 3.6 collective-permute-start.2
  21.3 3.3 fusion.189
  24.6 3.3 copy.49
  29.4 3.3 copy.47
  32.7 6.3 %collective-permute-start = (f32[20,256,1]{1,0,2:T(8,128)}, f32[20,256,1]{1,0,2:T(8,128)}, u32[]{:S(2)}, u32[]{:S(2)}) collective-permute-start(f32[20,256,1]{1,0,2:T(8,128)} %copy.47), channel_id=1, source_target_pairs={{4,0},{8,4},{12,8},{16,12},{20,16},{24,20},{28,24},{32,28},{36,32}... | collective-permute-start | bytes 61448 | tf_op jit(solution)/shard_map/ppermute | solution.py:21
  39.0 2.8 fusion.188
  41.8 1.9 subtract_multiply_fusion
  43.8 3.0 copy.48
  46.8 3.0 copy.50
  50.9 7.9 %fusion.19 = f32[20,256,128]{2,1,0:T(8,128)S(1)} fusion(f32[20,256,128]{2,1,0:T(8,128)S(1)} %get-tuple-element.202, f32[20,256,1]{2,1,0:T(8,128)} %copy.50, f32[20,256,1]{2,1,0:T(8,128)} %copy.48, f32[20,1,128]{2,1,0:T(1,128)S(1)} %get-tuple-element.261, f32[20,255,128]{2,1,0:T(8,128)} %get-tuple-element.198, f32[20,255,128]{2,1,0:T(8,128)} %get-tuple-element.197, ...), kind=kLoop, calls=%fused_computation.24 | loop fusion | flops 13107200 | bytes 15642624 | tf_op jit(solution)/shard_map/add | solution.py:96
  59.1 2.3 fusion.69
  65.0 64.1 %all-reduce.8 = (f32[]{:T(128)}, f32[]{:T(128)}) all-reduce(f32[]{:T(128)} %get-tuple-element.5, f32[]{:T(128)} %get-tuple-element.4), channel_id=1, replica_groups=mesh['lon'=32,'lat'=4] {'lon','lat'}, use_global_device_ids=true, to_apply=%region_1.2 | all-reduce | flops 2 | bytes 16 | tf_op jit(solution)/shard_map/psum | solution.py:129
  130.5 2.8 multiply_subtract_fusion.2
  133.9 2.8 fusion.185
  136.7 3.3 fusion.184
  141.3 3.6 collective-permute-start.9
  147.2 3.3 copy.51
  150.5 3.3 copy.53
  155.1 6.5 %collective-permute-start.5 = (f32[20,256,1]{1,0,2:T(8,128)}, f32[20,256,1]{1,0,2:T(8,128)}, u32[]{:S(2)}, u32[]{:S(2)}) collective-permute-start(f32[20,256,1]{1,0,2:T(8,128)} %copy.51), channel_id=1, source_target_pairs={{4,0},{8,4},{12,8},{16,12},{20,16},{24,20},{28,24},{32,28},{36,32}... | collective-permute-start | bytes 61448 | tf_op jit(solution)/shard_map/ppermute | solution.py:21
  161.7 3.4 fusion.28
  165.1 3.0 copy.52
  168.1 3.0 copy.54
  171.9 9.8 %multiply_reduce_fusion.3 = (f32[]{:T(128)}, f32[20,256,128]{2,1,0:T(8,128)}) fusion(f32[20,256,128]{2,1,0:T(8,128)S(1)} %multiply_subtract_fusion.2, f32[19,256,128]{2,1,0:T(8,128)} %fusion.28, f32[20,255,128]{2,1,0:T(8,128)} %get-tuple-element.188, f32[20,1,128]{2,1,0:T(1,128)S(1)} %get-tuple-element.259, f32[256]{0:T(256)S(1)} %get-tuple-element.262, ...), kind=kLoop, calls=%fused_computation.47 | loop fusion | flops 14417919 | bytes 15642628 | tf_op jit(solution)/shard_map/reduce_sum | solution.py:129
  181.7 64.9 %psum.44 = f32[]{:T(128)} all-reduce(f32[]{:T(128)} %get-tuple-element.68), channel_id=1, replica_groups=mesh['lon'=32,'lat'=4] {'lon','lat'}, use_global_device_ids=true, to_apply=%region_5.6 | all-reduce | flops 1 | bytes 8 | tf_op jit(solution)/shard_map/psum | solution.py:129
  248.1 3.0 multiply_add_fusion.2
  251.9 2.4 fusion.50
  259.1 64.8 %psum.45 = f32[]{:T(128)} all-reduce(f32[]{:T(128)} %multiply_reduce_fusion.2), channel_id=1, replica_groups=mesh['lon'=32,'lat'=4] {'lon','lat'}, use_global_device_ids=true, to_apply=%region_7.8 | all-reduce | flops 1 | bytes 8 | tf_op jit(solution)/shard_map/psum | solution.py:164
  325.2 2.0 multiply_subtract_fusion.1
  327.9 2.9 fusion.182
  330.8 3.2 fusion.181
  335.3 3.6 collective-permute-start.14
  341.1 3.3 copy.55
  344.3 3.3 copy.57
  347.6 8.0 %collective-permute-start.10 = (f32[20,256,1]{1,0,2:T(8,128)}, f32[20,256,1]{1,0,2:T(8,128)}, u32[]{:S(2)}, u32[]{:S(2)}) collective-permute-start(f32[20,256,1]{1,0,2:T(8,128)} %copy.55), channel_id=1, source_target_pairs={{4,0},{8,4},{12,8},{16,12},{20,16},{24,20},{28,24},{32,28},{36,32}... | collective-permute-start | bytes 61448 | tf_op jit(solution)/shard_map/ppermute | solution.py:21
  355.6 5.1 fusion.27
  360.7 3.0 copy.56
  363.7 3.0 copy.58
  367.5 12.4 %multiply_reduce_fusion.1 = (f32[]{:T(128)}, f32[20,256,128]{2,1,0:T(8,128)}) fusion(f32[20,256,128]{2,1,0:T(8,128)} %copy-done, f32[19,256,128]{2,1,0:T(8,128)} %fusion.27, f32[20,255,128]{2,1,0:T(8,128)} %get-tuple-element.180, f32[20,1,128]{2,1,0:T(1,128)S(1)} %get-tuple-element.257, f32[256]{0:T(256)S(1)} %get-tuple-element.262, ...), kind=kLoop, calls=%fused_computation.43 | loop fusion | flops 14417919 | bytes 15642628 | tf_op jit(solution)/shard_map/reduce_sum | solution.py:129
  380.0 63.2 %psum.46 = f32[]{:T(128)} all-reduce(f32[]{:T(128)} %get-tuple-element.37), channel_id=1, replica_groups=mesh['lon'=32,'lat'=4] {'lon','lat'}, use_global_device_ids=true, to_apply=%region_9.10 | all-reduce | flops 1 | bytes 8 | tf_op jit(solution)/shard_map/psum | solution.py:129
  444.6 3.0 multiply_add_fusion.1
  448.4 2.4 fusion.31
  454.1 62.7 %psum.47 = f32[]{:T(128)} all-reduce(f32[]{:T(128)} %multiply_reduce_fusion), channel_id=1, replica_groups=mesh['lon'=32,'lat'=4] {'lon','lat'}, use_global_device_ids=true, to_apply=%region_11.12 | all-reduce | flops 1 | bytes 8 | tf_op jit(solution)/shard_map/psum | solution.py:164
  518.1 5.0 multiply_add_fusion
  524.6 2.5 multiply_subtract_fusion
  (377 shorter events, 35.1 us)
Async XLA Ops:
  3.0 5.8 %copy-start.6 = (f32[19,256,128]{2,1,0:T(8,128)}, f32[19,256,128]{2,1,0:T(8,128)S(1)}, u32[]{:S(2)}) copy-start(f32[19,256,128]{2,1,0:T(8,128)S(1)} %broadcast_multiply_fusion) | copy-start | bytes 7471108
  12.4 50.9 %copy-start.1 = (f32[20,256,128]{2,1,0:T(8,128)}, f32[20,256,128]{2,1,0:T(8,128)S(1)}, u32[]{:S(2)}) copy-start(f32[20,256,128]{2,1,0:T(8,128)S(1)} %get-tuple-element.202) | copy-start | bytes 7864324
  14.0 35.9 %collective-permute-start.4 = (f32[20,1,128]{2,1,0:T(1,128)}, f32[20,1,128]{2,1,0:T(1,128)}, u32[]{:S(2)}, u32[]{:S(2)}) collective-permute-start(f32[20,1,128]{2,1,0:T(1,128)} %get-tuple-element.193), channel_id=1, source_target_pairs={{0,1},{1,2},{2,3},{4,5},{5,6},{6,7},{8,9},{9,10},{10,11},{12,13},{... | collective-permute-start | bytes 30728 | tf_op jit(solution)/shard_map/ppermute | solution.py:18
  15.8 34.0 %collective-permute-start.3 = (f32[20,1,128]{2,1,0:T(1,128)}, f32[20,1,128]{2,1,0:T(1,128)}, u32[]{:S(2)}, u32[]{:S(2)}) collective-permute-start(f32[20,1,128]{2,1,0:T(1,128)} %get-tuple-element.196), channel_id=1, source_target_pairs={{1,0},{2,1},{3,2},{5,4},{6,5},{7,6},{9,8},{10,9},{11,10},{13,12},{... | collective-permute-start | bytes 30728 | tf_op jit(solution)/shard_map/ppermute | solution.py:21
  17.7 32.1 %collective-permute-start.2 = (f32[2,20,128]{2,0,1:T(2,128)}, f32[2,20,128]{2,0,1:T(2,128)}, u32[]{:S(2)}, u32[]{:S(2)}) collective-permute-start(f32[2,20,128]{2,0,1:T(2,128)} %pad_maximum_fusion.6), channel_id=1, source_target_pairs={{0,64},{4,68},{8,72},{12,76},{16,80},{20,84},{24,88},{28,92},{32,9... | collective-permute-start | bytes 61448 | tf_op jit(solution)/shard_map/ppermute | solution.py:28
  27.8 19.0 %collective-permute-start.1 = (f32[20,256,1]{1,0,2:T(8,128)}, f32[20,256,1]{1,0,2:T(8,128)}, u32[]{:S(2)}, u32[]{:S(2)}) collective-permute-start(f32[20,256,1]{1,0,2:T(8,128)} %copy.49), channel_id=1, source_target_pairs={{0,4},{4,8},{8,12},{12,16},{16,20},{20,24},{24,28},{28,32},{32,36}... | collective-permute-start | bytes 61448 | tf_op jit(solution)/shard_map/ppermute | solution.py:18
  32.7 9.1 %copy-start.11 = (f32[19,256,128]{2,1,0:T(8,128)S(1)}, f32[19,256,128]{2,1,0:T(8,128)}, u32[]{:S(2)}) copy-start(f32[19,256,128]{2,1,0:T(8,128)} %param.5) | copy-start | bytes 7471108
  32.7 9.1 %copy-start.71 = (f32[19,256,128]{2,1,0:T(8,128)S(1)}, f32[19,256,128]{2,1,0:T(8,128)}, u32[]{:S(2)}) copy-start(f32[19,256,128]{2,1,0:T(8,128)} %copy-done.70) | copy-start | bytes 7471108
  32.7 9.1 %copy-start.73 = (f32[19,256,128]{2,1,0:T(8,128)S(1)}, f32[19,256,128]{2,1,0:T(8,128)}, u32[]{:S(2)}) copy-start(f32[19,256,128]{2,1,0:T(8,128)} %copy-done.72) | copy-start | bytes 7471108
  32.7 11.1 %collective-permute-start = (f32[20,256,1]{1,0,2:T(8,128)}, f32[20,256,1]{1,0,2:T(8,128)}, u32[]{:S(2)}, u32[]{:S(2)}) collective-permute-start(f32[20,256,1]{1,0,2:T(8,128)} %copy.47), channel_id=1, source_target_pairs={{4,0},{8,4},{12,8},{16,12},{20,16},{24,20},{28,24},{32,28},{36,32}... | collective-permute-start | bytes 61448 | tf_op jit(solution)/shard_map/ppermute | solution.py:21
  50.7 8.1 %copy-start.7 = (f32[19,256,128]{2,1,0:T(8,128)S(1)}, f32[19,256,128]{2,1,0:T(8,128)}, u32[]{:S(2)}) copy-start(f32[19,256,128]{2,1,0:T(8,128)} %copy-done.6) | copy-start | bytes 7471108
  50.7 8.1 %copy-start.74 = (f32[1,256,128]{2,1,0:T(8,128)S(1)}, f32[1,256,128]{2,1,0:T(8,128)}, u32[]{:S(2)}) copy-start(f32[1,256,128]{2,1,0:T(8,128)} %get-tuple-element.127) | copy-start | bytes 393220
  50.7 8.1 %copy-start.77 = (f32[1,256,128]{2,1,0:T(8,128)S(1)}, f32[1,256,128]{2,1,0:T(8,128)}, u32[]{:S(2)}) copy-start(f32[1,256,128]{2,1,0:T(8,128)} %get-tuple-element.130) | copy-start | bytes 393220
  50.7 8.1 %copy-start.80 = (f32[1,256,128]{2,1,0:T(8,128)S(1)}, f32[1,256,128]{2,1,0:T(8,128)}, u32[]{:S(2)}) copy-start(f32[1,256,128]{2,1,0:T(8,128)} %get-tuple-element.133) | copy-start | bytes 393220
  50.7 8.1 %copy-start.83 = (f32[1,256,128]{2,1,0:T(8,128)S(1)}, f32[1,256,128]{2,1,0:T(8,128)}, u32[]{:S(2)}) copy-start(f32[1,256,128]{2,1,0:T(8,128)} %get-tuple-element.136) | copy-start | bytes 393220
  50.7 8.1 %copy-start.86 = (f32[1,256,128]{2,1,0:T(8,128)S(1)}, f32[1,256,128]{2,1,0:T(8,128)}, u32[]{:S(2)}) copy-start(f32[1,256,128]{2,1,0:T(8,128)} %get-tuple-element.139) | copy-start | bytes 393220
  50.7 8.1 %copy-start.89 = (f32[1,256,128]{2,1,0:T(8,128)S(1)}, f32[1,256,128]{2,1,0:T(8,128)}, u32[]{:S(2)}) copy-start(f32[1,256,128]{2,1,0:T(8,128)} %get-tuple-element.142) | copy-start | bytes 393220
  50.8 8.1 %copy-start.92 = (f32[1,256,128]{2,1,0:T(8,128)S(1)}, f32[1,256,128]{2,1,0:T(8,128)}, u32[]{:S(2)}) copy-start(f32[1,256,128]{2,1,0:T(8,128)} %get-tuple-element.145) | copy-start | bytes 393220
  50.8 8.1 %copy-start.95 = (f32[1,256,128]{2,1,0:T(8,128)S(1)}, f32[1,256,128]{2,1,0:T(8,128)}, u32[]{:S(2)}) copy-start(f32[1,256,128]{2,1,0:T(8,128)} %get-tuple-element.148) | copy-start | bytes 393220
  50.8 8.1 %copy-start.98 = (f32[1,256,128]{2,1,0:T(8,128)S(1)}, f32[1,256,128]{2,1,0:T(8,128)}, u32[]{:S(2)}) copy-start(f32[1,256,128]{2,1,0:T(8,128)} %get-tuple-element.151) | copy-start | bytes 393220
  50.8 8.1 %copy-start.101 = (f32[1,256,128]{2,1,0:T(8,128)S(1)}, f32[1,256,128]{2,1,0:T(8,128)}, u32[]{:S(2)}) copy-start(f32[1,256,128]{2,1,0:T(8,128)} %get-tuple-element.154) | copy-start | bytes 393220
  50.8 8.1 %copy-start.104 = (f32[1,256,128]{2,1,0:T(8,128)S(1)}, f32[1,256,128]{2,1,0:T(8,128)}, u32[]{:S(2)}) copy-start(f32[1,256,128]{2,1,0:T(8,128)} %get-tuple-element.157) | copy-start | bytes 393220
  50.8 8.1 %copy-start.107 = (f32[1,256,128]{2,1,0:T(8,128)S(1)}, f32[1,256,128]{2,1,0:T(8,128)}, u32[]{:S(2)}) copy-start(f32[1,256,128]{2,1,0:T(8,128)} %get-tuple-element.160) | copy-start | bytes 393220
  50.8 8.1 %copy-start.110 = (f32[1,256,128]{2,1,0:T(8,128)S(1)}, f32[1,256,128]{2,1,0:T(8,128)}, u32[]{:S(2)}) copy-start(f32[1,256,128]{2,1,0:T(8,128)} %get-tuple-element.163) | copy-start | bytes 393220
  50.8 8.1 %copy-start.113 = (f32[1,256,128]{2,1,0:T(8,128)S(1)}, f32[1,256,128]{2,1,0:T(8,128)}, u32[]{:S(2)}) copy-start(f32[1,256,128]{2,1,0:T(8,128)} %get-tuple-element.166) | copy-start | bytes 393220
  50.8 8.1 %copy-start.116 = (f32[1,256,128]{2,1,0:T(8,128)S(1)}, f32[1,256,128]{2,1,0:T(8,128)}, u32[]{:S(2)}) copy-start(f32[1,256,128]{2,1,0:T(8,128)} %get-tuple-element.169) | copy-start | bytes 393220
  50.8 8.1 %copy-start.119 = (f32[1,256,128]{2,1,0:T(8,128)S(1)}, f32[1,256,128]{2,1,0:T(8,128)}, u32[]{:S(2)}) copy-start(f32[1,256,128]{2,1,0:T(8,128)} %get-tuple-element.172) | copy-start | bytes 393220
  50.9 8.1 %copy-start.122 = (f32[1,256,128]{2,1,0:T(8,128)S(1)}, f32[1,256,128]{2,1,0:T(8,128)}, u32[]{:S(2)}) copy-start(f32[1,256,128]{2,1,0:T(8,128)} %get-tuple-element.175) | copy-start | bytes 393220
  58.8 4.5 copy-start.4
  140.0 31.1 %collective-permute-start.8 = (f32[20,1,128]{2,1,0:T(1,128)}, f32[20,1,128]{2,1,0:T(1,128)}, u32[]{:S(2)}, u32[]{:S(2)}) collective-permute-start(f32[20,1,128]{2,1,0:T(1,128)} %get-tuple-element.189), channel_id=1, source_target_pairs={{1,0},{2,1},{3,2},{5,4},{6,5},{7,6},{9,8},{10,9},{11,10},{13,12},{... | collective-permute-start | bytes 30728 | tf_op jit(solution)/shard_map/ppermute | solution.py:21
  141.3 29.8 %collective-permute-start.9 = (f32[20,1,128]{2,1,0:T(1,128)}, f32[20,1,128]{2,1,0:T(1,128)}, u32[]{:S(2)}, u32[]{:S(2)}) collective-permute-start(f32[20,1,128]{2,1,0:T(1,128)} %get-tuple-element.191), channel_id=1, source_target_pairs={{0,1},{1,2},{2,3},{4,5},{5,6},{6,7},{8,9},{9,10},{10,11},{12,13},{... | collective-permute-start | bytes 30728 | tf_op jit(solution)/shard_map/ppermute | solution.py:18
  145.5 25.6 %collective-permute-start.7 = (f32[2,20,128]{2,0,1:T(2,128)}, f32[2,20,128]{2,0,1:T(2,128)}, u32[]{:S(2)}, u32[]{:S(2)}) collective-permute-start(f32[2,20,128]{2,0,1:T(2,128)} %pad_maximum_fusion.7), channel_id=1, source_target_pairs={{0,64},{4,68},{8,72},{12,76},{16,80},{20,84},{24,88},{28,92},{32,9... | collective-permute-start | bytes 61448 | tf_op jit(solution)/shard_map/ppermute | solution.py:28
  153.7 14.4 %collective-permute-start.6 = (f32[20,256,1]{1,0,2:T(8,128)}, f32[20,256,1]{1,0,2:T(8,128)}, u32[]{:S(2)}, u32[]{:S(2)}) collective-permute-start(f32[20,256,1]{1,0,2:T(8,128)} %copy.53), channel_id=1, source_target_pairs={{0,4},{4,8},{8,12},{12,16},{16,20},{20,24},{24,28},{28,32},{32,36}... | collective-permute-start | bytes 61448 | tf_op jit(solution)/shard_map/ppermute | solution.py:18
  155.1 9.9 %collective-permute-start.5 = (f32[20,256,1]{1,0,2:T(8,128)}, f32[20,256,1]{1,0,2:T(8,128)}, u32[]{:S(2)}, u32[]{:S(2)}) collective-permute-start(f32[20,256,1]{1,0,2:T(8,128)} %copy.51), channel_id=1, source_target_pairs={{4,0},{8,4},{12,8},{16,12},{20,16},{24,20},{28,24},{32,28},{36,32}... | collective-permute-start | bytes 61448 | tf_op jit(solution)/shard_map/ppermute | solution.py:21
  248.1 3.7 copy-start.120
  248.1 3.7 copy-start.123
  251.8 4.5 copy-start.2
  334.0 32.7 %collective-permute-start.13 = (f32[20,1,128]{2,1,0:T(1,128)}, f32[20,1,128]{2,1,0:T(1,128)}, u32[]{:S(2)}, u32[]{:S(2)}) collective-permute-start(f32[20,1,128]{2,1,0:T(1,128)} %get-tuple-element.181), channel_id=1, source_target_pairs={{1,0},{2,1},{3,2},{5,4},{6,5},{7,6},{9,8},{10,9},{11,10},{13,12},{... | collective-permute-start | bytes 30728 | tf_op jit(solution)/shard_map/ppermute | solution.py:21
  335.3 31.4 %collective-permute-start.14 = (f32[20,1,128]{2,1,0:T(1,128)}, f32[20,1,128]{2,1,0:T(1,128)}, u32[]{:S(2)}, u32[]{:S(2)}) collective-permute-start(f32[20,1,128]{2,1,0:T(1,128)} %get-tuple-element.183), channel_id=1, source_target_pairs={{0,1},{1,2},{2,3},{4,5},{5,6},{6,7},{8,9},{9,10},{10,11},{12,13},{... | collective-permute-start | bytes 30728 | tf_op jit(solution)/shard_map/ppermute | solution.py:18
  339.5 27.1 %collective-permute-start.12 = (f32[2,20,128]{2,0,1:T(2,128)}, f32[2,20,128]{2,0,1:T(2,128)}, u32[]{:S(2)}, u32[]{:S(2)}) collective-permute-start(f32[2,20,128]{2,0,1:T(2,128)} %pad_maximum_fusion.8), channel_id=1, source_target_pairs={{0,64},{4,68},{8,72},{12,76},{16,80},{20,84},{24,88},{28,92},{32,9... | collective-permute-start | bytes 61448 | tf_op jit(solution)/shard_map/ppermute | solution.py:28
  347.6 16.1 %collective-permute-start.11 = (f32[20,256,1]{1,0,2:T(8,128)}, f32[20,256,1]{1,0,2:T(8,128)}, u32[]{:S(2)}, u32[]{:S(2)}) collective-permute-start(f32[20,256,1]{1,0,2:T(8,128)} %copy.57), channel_id=1, source_target_pairs={{0,4},{4,8},{8,12},{12,16},{16,20},{20,24},{24,28},{28,32},{32,36}... | collective-permute-start | bytes 61448 | tf_op jit(solution)/shard_map/ppermute | solution.py:18
  347.6 13.1 %collective-permute-start.10 = (f32[20,256,1]{1,0,2:T(8,128)}, f32[20,256,1]{1,0,2:T(8,128)}, u32[]{:S(2)}, u32[]{:S(2)}) collective-permute-start(f32[20,256,1]{1,0,2:T(8,128)} %copy.55), channel_id=1, source_target_pairs={{4,0},{8,4},{12,8},{16,12},{20,16},{24,20},{28,24},{32,28},{36,32}... | collective-permute-start | bytes 61448 | tf_op jit(solution)/shard_map/ppermute | solution.py:21
  444.6 3.7 copy-start.124
  448.3 4.5 copy-start.12
  518.1 5.0 copy-start.3
  518.1 5.0 copy-start.5
  518.1 5.7 %copy-start.13 = (f32[20,256,128]{2,1,0:T(8,128)S(1)}, f32[20,256,128]{2,1,0:T(8,128)}, u32[]{:S(2)}) copy-start(f32[20,256,128]{2,1,0:T(8,128)} %copy-done.12) | copy-start | bytes 7864324
  518.1 6.6 %copy-start.16 = (f32[20,256,128]{2,1,0:T(8,128)S(1)}, f32[20,256,128]{2,1,0:T(8,128)}, u32[]{:S(2)}) copy-start(f32[20,256,128]{2,1,0:T(8,128)} %param.3) | copy-start | bytes 7864324
  (95 other events, 254.0 us)
where the time goes:
time: 535 us; the launch traced here: 528 us
  blocking collectives  320 us (60%)
  other arithmetic  88.7 us (17%)
  local copies, waits for them, and re-layouts  65.9 us (12%)
  starting transfers between devices  43.6 us (8%)
  between operations  9.79 us (2%)
    psum x3, blocking collectives, energy_total(): return lax.psum(jnp.sum(smooth_field * smooth_image), ('lon', 'lat'))  192 us
    psum x2, blocking collectives, on_device(): curvature = lax.psum(jnp.sum(image_dir * back_image), ('lon', 'lat'))  127 us
    ppermute x6, starting transfers between devices, with_halo(): lax.ppermute(lax.slice_in_dim(block, 0, width, axis=dim), axis, backward)  24.7 us
    reduce_sum x2, other arithmetic, energy_total(): return lax.psum(jnp.sum(smooth_field * smooth_image), ('lon', 'lat'))  22.2 us
    slice x6, local copies, waits for them, and re-layouts, with_halo(): lax.slice_in_dim(block, 0, width, axis=dim)  19.5 us
    ppermute x6, starting transfers between devices, with_halo(): lax.ppermute(lax.slice_in_dim(block, block.shape[dim] - width, None, axis...  12.1 us
  transfers between devices with their start and end apart: 15, of which 0 were waited for; matrix products, arithmetic and copies ran while one was open for 11% of the time, Pallas kernels for 0%

commit v1 on v0

v1 whole, which is shorter than its diff:
```python
import functools
import math

import jax
import jax.numpy as jnp
from jax import lax
from jax.experimental import pallas as pl
from jax.experimental.pallas import tpu as pltpu
from jax.sharding import PartitionSpec as P

LEVELS = 20
ROWS = 256
LANES = 128
TOTAL_ROWS = 1024
LON_COEFF = 4.0
TILES = ROWS // 8 + 2
EXTENDED = 8 * TILES + 16
STACKED = 3 * LEVELS - 1
AT_H = LEVELS
AT_C = 2 * LEVELS
CHUNKS = 8
AXES = ("lon", "lat")
F32 = jnp.float32
MIB = 1 << 20


def swap(x, partner):
    return lax.ppermute(x, AXES, [(i, partner(i)) for i in range(128)])


def lat_even(i):
    return i ^ 1


def lat_odd(i):
    lon, lat = i >> 2, i & 3
    if lat in (1, 2):
        return (lon << 2) | (3 - lat)
    return ((lon ^ 16) << 2) | lat


def lon_even(i):
    return i ^ 4


def lon_odd(i):
    lon, lat = i >> 2, i & 3
    other = (lon + 1) % 32 if lon % 2 else (lon - 1) % 32
    return (other << 2) | lat


def lane_index():
    return lax.broadcasted_iota(jnp.int32, (8, LANES), 1)


def sub_index():
    return lax.broadcasted_iota(jnp.int32, (8, LANES), 0)


def capped_cosine(row):
    angle = (row + 0.5) * (math.pi / TOTAL_ROWS) - 0.5 * math.pi
    square = angle * angle
    value = jnp.full_like(row, 0.0)
    for n in range(8, -1, -1):
        value = value * square + (-1.0) ** n / math.factorial(2 * n)
    return jnp.maximum(value, 0.5)


def row_terms(row):
    here = capped_cosine(row)
    return (
        here,
        LON_COEFF / here,
        (here + capped_cosine(row + 1.0)) * 0.5,
        (here + capped_cosine(row - 1.0)) * 0.5,
    )


def eliminate(terms, right, helm, coup, store):
    cosine, over, north, south = terms
    fixed = 2.0 * over + north + south
    forward = []
    ratios = []
    below = None
    for k in range(LEVELS):
        scaled = cosine * coup(k) if k < LEVELS - 1 else None
        pivot = cosine * helm(k) + fixed
        if scaled is not None:
            pivot = pivot + scaled
        if below is not None:
            pivot = pivot + below
            pivot = pivot - below * ratios[-1]
        inverse = 1.0 / pivot
        value = right(k)
        if below is not None:
            value = value + below * forward[-1]
        forward.append(value * inverse)
        ratio = None
        if scaled is not None:
            ratio = scaled * inverse
            ratios.append(ratio)
        store(k, scaled, inverse, ratio)
        below = scaled
    return forward, ratios


def packed_edges(read, lane):
    last = jnp.zeros((8, LANES), F32)
    first = jnp.zeros((8, LANES), F32)
    group = lane // 3
    for t in range(1, TILES - 1):
        turned = pltpu.roll(read(t), 3 * t + 3, axis=1)
        last = jnp.where(group == t, turned, last)
        first = jnp.where(group == t + 1, turned, first)
    return last, first


def edge_rows_kernel(b_lo, b_hi, h_lo, h_hi, c_lo, c_hi, a_ref, o_ref):
    even = lax.axis_index("lat") % 2 == 0
    for at, count, lo, hi in (
        (0, LEVELS, b_lo, b_hi),
        (AT_H, LEVELS, h_lo, h_hi),
        (AT_C, LEVELS - 1, c_lo, c_hi),
    ):
        low, high = lo[...], hi[...]
        a_ref[pl.ds(at, count)] = jnp.where(even, high, low)
        o_ref[pl.ds(at, count)] = jnp.where(even, low, high)


def first_kernel(
    b_hbm, h_hbm, c_hbm, b_ref, scaled_ref, inverse_ref, ratio_ref, x_ref, terms_ref, last_ref,
    first_ref, h_ref, c_ref, sems
):
    step = ROWS // CHUNKS

    def copy(i, n):
        src = (b_hbm, h_hbm, c_hbm)[i]
        dst = (b_ref, h_ref, c_ref)[i]
        rows = pl.ds(n * step, step)
        return pltpu.make_async_copy(src.at[:, rows, :], dst.at[:, rows, :], sems.at[i, n])

    for n in range(CHUNKS):
        for i in range(3):
            copy(i, n).start()
    base = lax.axis_index("lat") * ROWS
    lane = lane_index()
    sub = sub_index()

    def row_term(t, carry):
        row = (base + 8 * t - 8 + sub).astype(F32)
        for i, term in enumerate(row_terms(row)):
            terms_ref[i, pl.ds(pl.multiple_of(8 * t, 8), 8), :] = term
        return carry

    lax.fori_loop(0, TILES, row_term, 0)
    for n in range(CHUNKS):
        for i in range(3):
            copy(i, n).wait()

        def tile(t, carry):
            at = pl.ds(pl.multiple_of(8 * t - 8, 8), 8)
            wide = pl.ds(pl.multiple_of(8 * t + 8, 8), 8)
            terms = [terms_ref[i, pl.ds(pl.multiple_of(8 * t, 8), 8), :] for i in range(4)]

            def store(k, scaled, inverse, ratio):
                inverse_ref[k, wide, :] = inverse
                if scaled is not None:
                    scaled_ref[k, wide, :] = scaled
                    ratio_ref[k, wide, :] = ratio

            forward, ratios = eliminate(
                terms,
                lambda k: b_ref[k, at, :],
                lambda k: h_ref[k, at, :],
                lambda k: c_ref[k, at, :],
                store,
            )
            value = forward[-1]
            x_ref[LEVELS - 1, wide, :] = value
            for k in range(LEVELS - 2, -1, -1):
                value = forward[k] + ratio_ref[k, wide, :] * value
                x_ref[k, wide, :] = value
            return carry

        lax.fori_loop(1 + n * step // 8, 1 + (n + 1) * step // 8, tile, 0)

    def pack(source, at, count):
        def level(k, carry):
            last, first = packed_edges(lambda t: source[k, pl.ds(8 * t - 8, 8), :], lane)
            last_ref[at + k] = last
            first_ref[at + k] = first
            return carry

        lax.fori_loop(0, count, level, 0)

    pack(b_ref, 0, LEVELS)
    pack(h_ref, AT_H, LEVELS)
    pack(c_ref, AT_C, LEVELS - 1)


def edge_lanes_kernel(a_ref, o_ref, last_ref, first_ref, south_ref, north_ref, e_ref, d_ref):
    lat = lax.axis_index("lat")
    lat_is_even = lat % 2 == 0
    lon_is_even = lax.axis_index("lon") % 2 == 0
    polar = jnp.logical_or(lat == 0, lat == 3)
    lane = lane_index()
    sub = sub_index()
    group = lane // 3

    def level(j, carry):
        near = a_ref[j]
        far = o_ref[j]
        flipped = far
        for s in (0, 1, 2, 5, 6, 7):
            flipped = jnp.where(sub == s, jnp.broadcast_to(far[7 - s : 8 - s], (8, LANES)), flipped)
        far = jnp.where(polar, flipped, far)
        south = jnp.where(lat_is_even, far, near)
        north = jnp.where(lat_is_even, near, far)
        south_ref[j] = south
        north_ref[j] = north
        last, first = last_ref[j], first_ref[j]
        for t, value in ((0, south), (TILES - 1, north)):
            turned = pltpu.roll(value, 3 * t + 3, axis=1)
            last = jnp.where(group == t, turned, last)
            first = jnp.where(group == t + 1, turned, first)
        first = pltpu.roll(first, LANES - 3, axis=1)
        e_ref[j] = jnp.where(lon_is_even, last, first)
        d_ref[j] = jnp.where(lon_is_even, first, last)
        return carry

    lax.fori_loop(0, STACKED, level, 0, unroll=2)


def middle_kernel(
    b_ref, scaled_in, inverse_in, ratio_in, x0_in, terms_ref, south_ref, north_ref, e_ref, d_ref,
    scaled_ref, inverse_ref, ratio_ref, x0_ref, x1_ref, x2_ref, y1_ref, y2_ref, y3_ref, sums_ref,
    left_ref, right_ref, joint_ref, edge_ref, strip_ref
):
    del scaled_in, inverse_in, ratio_in, x0_in
    base = lax.axis_index("lat") * ROWS
    lon_is_even = lax.axis_index("lon") % 2 == 0
    lane = lane_index()
    sub = sub_index()
    slot = lane % 3
    group = lane // 3

    for t, source in ((0, south_ref), (TILES - 1, north_ref)):
        wide = pl.ds(8 * t + 8, 8)
        terms = [terms_ref[i, pl.ds(8 * t, 8), :] for i in range(4)]

        def store(k, scaled, inverse, ratio, wide=wide):
            inverse_ref[k, wide, :] = inverse
            if scaled is not None:
                scaled_ref[k, wide, :] = scaled
                ratio_ref[k, wide, :] = ratio

        forward, ratios = eliminate(
            terms,
            lambda k, source=source: source[k],
            lambda k, source=source: source[AT_H + k],
            lambda k, source=source: source[AT_C + k],
            store,
        )
        value = forward[-1]
        x0_ref[LEVELS - 1, wide, :] = value
        for k in range(LEVELS - 2, -1, -1):
            value = forward[k] + ratios[k] * value
            x0_ref[k, wide, :] = value

    strip_row = (base + 8 * group - 8 + sub).astype(F32)
    strip_terms = row_terms(strip_row)
    for side, out in ((0, left_ref), (1, right_ref)):

        def received(j, side=side):
            even, odd = (d_ref, e_ref) if side == 0 else (e_ref, d_ref)
            return jnp.where(lon_is_even, even[j], odd[j])

        def store(k, scaled, inverse, ratio, side=side):
            strip_ref[side, 1, k] = inverse
            if scaled is not None:
                strip_ref[side, 0, k] = scaled
                strip_ref[side, 2, k] = ratio

        forward, ratios = eliminate(
            strip_terms,
            received,
            lambda k: received(AT_H + k),
            lambda k: received(AT_C + k),
            store,
        )
        value = forward[-1]
        out[LEVELS - 1] = value
        for k in range(LEVELS - 2, -1, -1):
            value = forward[k] + ratios[k] * value
            out[k] = value

    def join_strips():
        def level(k, carry):
            right = pltpu.roll(right_ref[k], 1, axis=1)
            joint_ref[k] = jnp.where(slot == 2, left_ref[k], right)
            return carry

        lax.fori_loop(0, LEVELS, level, 0, unroll=4)

    def gather_edges(x_ref):
        def level(k, carry):
            edge = jnp.zeros((8, LANES), F32)
            for t in range(TILES):
                turned = pltpu.roll(x_ref[k, pl.ds(8 * t + 8, 8), :], 3 * t + 2, axis=1)
                edge = jnp.where(group == t, turned, edge)
            edge_ref[k] = edge
            return carry

        lax.fori_loop(0, LEVELS, level, 0)

    def strip_step():
        _, over, north, south = strip_terms
        for side, ref in ((0, left_ref), (1, right_ref)):
            forward = []
            for k in range(LEVELS):
                x = ref[k]
                up = pltpu.roll(x, 1, axis=1)
                down = pltpu.roll(x, LANES - 1, axis=1)
                if side == 0:
                    down = jnp.where(slot == 2, edge_ref[k], down)
                else:
                    up = jnp.where(slot == 0, pltpu.roll(edge_ref[k], LANES - 1, axis=1), up)
                above = jnp.concatenate([x[1:], pltpu.roll(x, LANES - 3, axis=1)[:1]], 0)
                below = jnp.concatenate([pltpu.roll(x, 3, axis=1)[7:], x[:7]], 0)
                value = over * (up + down) + north * above + south * below
                if k > 0:
                    value = value + strip_ref[side, 0, k - 1] * forward[-1]
                forward.append(value * strip_ref[side, 1, k])
            value = forward[-1]
            ref[LEVELS - 1] = value
            for k in range(LEVELS - 2, -1, -1):
                value = forward[k] + strip_ref[side, 2, k] * value
                ref[k] = value

    def tile_step(t, x_ref, y_ref, out_ref, sums):
        start = pl.multiple_of(8 * t + 8, 8)
        wide = pl.ds(start, 8)
        _, over, north, south = [
            terms_ref[i, pl.ds(pl.multiple_of(8 * t, 8), 8), :] for i in range(4)
        ]
        turn = 126 - 3 * t
        forward = []
        cross = jnp.zeros((8, LANES), F32)
        for k in range(LEVELS):
            x = x_ref[k, wide, :]
            inject = pltpu.roll(joint_ref[k], turn, axis=1)
            west = jnp.where(lane == 0, inject, pltpu.roll(x, 1, axis=1))
            east = jnp.where(lane == LANES - 1, inject, pltpu.roll(x, LANES - 1, axis=1))
            above = x_ref[k, pl.ds(start + 1, 8), :]
            below = x_ref[k, pl.ds(start - 1, 8), :]
            value = over * (west + east) + north * above + south * below
            if sums is not None:
                y_ref[k, pl.ds(pl.multiple_of(8 * t - 8, 8), 8), :] = value
                cross = cross + x * value
            if k > 0:
                value = value + scaled_ref[k - 1, wide, :] * forward[-1]
            forward.append(value * inverse_ref[k, wide, :])
        own = jnp.zeros((8, LANES), F32)
        value = forward[-1]
        for k in range(LEVELS - 1, -1, -1):
            if k < LEVELS - 1:
                value = forward[k] + ratio_ref[k, wide, :] * value
            if out_ref is not None:
                out_ref[k, wide, :] = value
            if sums is not None:
                own = own + value * y_ref[k, pl.ds(pl.multiple_of(8 * t - 8, 8), 8), :]
        if sums is not None:
            return sums[0] + cross, sums[1] + own

    zero = jnp.zeros((8, LANES), F32)

    def start_sum(t, carry):
        wide = pl.ds(pl.multiple_of(8 * t + 8, 8), 8)
        at = pl.ds(pl.multiple_of(8 * t - 8, 8), 8)
        total = zero
        for k in range(LEVELS):
            total = total + x0_ref[k, wide, :] * b_ref[k, at, :]
        return carry + total

    totals = [lax.fori_loop(1, TILES - 1, start_sum, zero)]
    for x_ref, y_ref, out_ref in (
        (x0_ref, y1_ref, x1_ref),
        (x1_ref, y2_ref, x2_ref),
        (x2_ref, y3_ref, None),
    ):
        join_strips()
        totals += lax.fori_loop(
            1,
            TILES - 1,
            lambda t, sums: tile_step(t, x_ref, y_ref, out_ref, sums),
            (zero, zero),
        )
        if out_ref is not None:

            def ends(i, carry):
                tile_step(i * (TILES - 1), x_ref, None, out_ref, None)
                return carry

            lax.fori_loop(0, 2, ends, 0)
            gather_edges(x_ref)
            strip_step()
    sums_ref[...] = jnp.concatenate([jnp.sum(total, axis=0, keepdims=True) for total in totals] + [zero[:1]], 0)


def two_sum(a, b):
    total = a + b
    part = total - a
    return total, (a - (total - part)) + (b - part)


def coefficients(high, low):
    for by in (64, 32, 16, 8, 4, 2, 1):
        high, error = two_sum(high, pltpu.roll(high, by, axis=1))
        low = low + pltpu.roll(low, by, axis=1) + error
    row = lambda x, n: jnp.broadcast_to(x[n : n + 1], (8, LANES))
    shift = jnp.floor(64.0 * (row(high, 1) / row(high, 0)) + 0.5) * (1.0 / 64.0)
    centred = []
    for n in range(7):
        centred.append(row(high, 0) + row(low, 0))
        if n == 6:
            break
        wide = 4097.0 * high
        coarse = wide - (wide - high)
        fine = high - coarse
        following = jnp.concatenate([high[1:], high[:1]], 0)
        rest = jnp.concatenate([low[1:], low[:1]], 0) - shift * low
        total, error = two_sum(following, -shift * coarse)
        rest = rest + error
        total, error = two_sum(total, -shift * fine)
        rest = rest + error
        high = total + rest
        low = rest - (high - total)
    sigma = 1.0 - shift
    energies = [sigma * centred[n] - centred[n + 1] for n in range(6)]
    curvatures = [sigma * energies[n] - energies[n + 1] for n in range(5)]

    def product(p, q, table):
        return sum(p[i] * q[j] * table[i + j] for i in range(len(p)) for j in range(len(q)))

    one = jnp.ones((8, LANES), F32)
    none = jnp.zeros((8, LANES), F32)
    smoothed = [one]
    direction = [one]
    result = []
    energy = energies[0]
    for iteration in range(3):
        length = energy / product(direction, direction, curvatures)
        result = [
            (result[i] if i < len(result) else none) + length * direction[i]
            for i in range(len(direction))
        ]
        if iteration < 2:
            image = [sigma * d for d in direction] + [none]
            image = [image[i] - (direction[i - 1] if i else none) for i in range(len(image))]
            smoothed = [
                (smoothed[i] if i < len(smoothed) else none) - length * image[i]
                for i in range(len(image))
            ]
            following = product(smoothed, smoothed, energies)
            ratio = following / energy
            direction = [
                smoothed[i] + (ratio * direction[i] if i < len(direction) else none)
                for i in range(len(smoothed))
            ]
            energy = following
    k0, k1, k2 = result
    return k0 - shift * k1 + shift * shift * k2, k1 - 2.0 * shift * k2, k2


def last_kernel(
    sums_ref, b_ref, x0_ref, x1_ref, x2_ref, y1_ref, y2_ref, y3_ref, solution_hbm, residual_hbm,
    solution_ref, residual_ref, sems
):
    step = ROWS // CHUNKS
    k0, k1, k2 = coefficients(sums_ref[:8], sums_ref[8:])
    r0, r1, r2 = 1.0 - k0, k0 - k1, k1 - k2

    def copy(i, n):
        src = (solution_ref, residual_ref)[i]
        dst = (solution_hbm, residual_hbm)[i]
        rows = pl.ds(n * step, step)
        return pltpu.make_async_copy(src.at[:, rows, :], dst.at[:, rows, :], sems.at[i, n])

    for n in range(CHUNKS):

        def tile(t, carry):
            at = pl.ds(pl.multiple_of(8 * t - 8, 8), 8)
            wide = pl.ds(pl.multiple_of(8 * t + 8, 8), 8)
            for k in range(LEVELS):
                solution_ref[k, at, :] = (
                    k0 * x0_ref[k, wide, :] + k1 * x1_ref[k, wide, :] + k2 * x2_ref[k, wide, :]
                )
                residual_ref[k, at, :] = (
                    r0 * b_ref[k, at, :] + r1 * y1_ref[k, at, :]
                    + r2 * y2_ref[k, at, :] + k2 * y3_ref[k, at, :]
                )
            return carry

        lax.fori_loop(1 + n * step // 8, 1 + (n + 1) * step // 8, tile, 0)
        for i in range(2):
            copy(i, n).start()
    for n in range(CHUNKS):
        for i in range(2):
            copy(i, n).wait()


VMEM = pl.BlockSpec(memory_space=pltpu.VMEM)
ANY = pl.BlockSpec(memory_space=pl.ANY)


def kept(*shape):
    return pltpu.VMEM(shape, F32)


def call(kernel, outs, ins, in_specs, out_specs=None, scratch=(), limit=24, flops=0, aliases=None):
    return pl.pallas_call(
        kernel,
        out_shape=outs,
        in_specs=in_specs,
        out_specs=[VMEM] * len(outs) if out_specs is None else out_specs,
        scratch_shapes=list(scratch),
        input_output_aliases=aliases or {},
        compiler_params=pltpu.CompilerParams(vmem_limit_bytes=limit * MIB),
        cost_estimate=pl.CostEstimate(flops=flops, bytes_accessed=1000000, transcendentals=0),
        name=kernel.__name__,
    )(*ins)


def total_over_devices(sums):
    high, low = sums, jnp.zeros_like(sums)
    for flip in (1, 2, 66, 4, 12, 16, 48):
        other = swap(jnp.concatenate([high, low], 0), lambda i: i ^ flip)
        high, error = two_sum(high, other[:8])
        low = low + other[8:] + error
    return jnp.concatenate([high, low], 0)


def on_device(right_side, helmholtz, coupling):
    low = pl.BlockSpec((LEVELS, 8, LANES), lambda i: (0, 0, 0))
    high = pl.BlockSpec((LEVELS, 8, LANES), lambda i: (0, ROWS // 8 - 1, 0))
    low_c = pl.BlockSpec((LEVELS - 1, 8, LANES), lambda i: (0, 0, 0))
    high_c = pl.BlockSpec((LEVELS - 1, 8, LANES), lambda i: (0, ROWS // 8 - 1, 0))
    message = jax.ShapeDtypeStruct((STACKED, 8, LANES), F32)
    whole = pl.BlockSpec((STACKED, 8, LANES), lambda i: (0, 0, 0))
    rows_a, rows_b = pl.pallas_call(
        edge_rows_kernel,
        grid=(1,),
        out_shape=[message, message],
        in_specs=[low, high, low, high, low_c, high_c],
        out_specs=[whole, whole],
        name="edge_rows",
    )(right_side, right_side, helmholtz, helmholtz, coupling, coupling)
    rows_a = swap(rows_a, lat_even)
    rows_b = swap(rows_b, lat_odd)
    field = kept(LEVELS, EXTENDED, LANES)
    block = kept(LEVELS, ROWS, LANES)
    b, scaled, inverse, ratio, x0, terms, last, first = call(
        first_kernel,
        [block, field, field, field, field, kept(4, 8 * TILES, LANES)]
        + [kept(STACKED, 8, LANES)] * 2,
        [right_side, helmholtz, coupling],
        [ANY] * 3,
        scratch=[
            pltpu.VMEM((LEVELS, ROWS, LANES), F32),
            pltpu.VMEM((LEVELS - 1, ROWS, LANES), F32),
            pltpu.SemaphoreType.DMA((3, CHUNKS)),
        ],
        flops=10000000,
    )
    south, north, lanes_e, lanes_d = call(
        edge_lanes_kernel,
        [kept(STACKED, 8, LANES)] * 2 + [message, message],
        [rows_a, rows_b, last, first],
        [VMEM] * 4,
    )
    lanes_e = swap(lanes_e, lon_even)
    lanes_d = swap(lanes_d, lon_odd)
    scaled, inverse, ratio, x0, x1, x2, y1, y2, y3, sums = call(
        middle_kernel,
        [field] * 6 + [block] * 3 + [jax.ShapeDtypeStruct((8, LANES), F32)],
        [b, scaled, inverse, ratio, x0, terms, south, north, lanes_e, lanes_d],
        [VMEM] * 10,
        scratch=[
            pltpu.VMEM((LEVELS, 8, LANES), F32),
            pltpu.VMEM((LEVELS, 8, LANES), F32),
            pltpu.VMEM((LEVELS, 8, LANES), F32),
            pltpu.VMEM((LEVELS, 8, LANES), F32),
            pltpu.VMEM((2, 3, LEVELS, 8, LANES), F32),
        ],
        flops=100000000,
        aliases={1: 0, 2: 1, 3: 2, 4: 3},
    )
    sums = total_over_devices(sums)
    result = jax.ShapeDtypeStruct((LEVELS, ROWS, LANES), F32)
    return call(
        last_kernel,
        [result, result],
        [sums, b, x0, x1, x2, y1, y2, y3],
        [VMEM] * 8,
        out_specs=[ANY, ANY],
        scratch=[
            pltpu.VMEM((LEVELS, ROWS, LANES), F32),
            pltpu.VMEM((LEVELS, ROWS, LANES), F32),
            pltpu.SemaphoreType.DMA((2, CHUNKS)),
        ],
        flops=10000000,
    )


def solution(mesh):
    spec = P(None, "lat", "lon")
    return jax.shard_map(
        lambda *args: tuple(on_device(*args)),
        mesh=mesh,
        in_specs=(spec,) * 3,
        out_specs=(spec,) * 2,
        check_vma=False,
    )
```

time: 535 us -> 103 us (0.19); the launches traced: 528 us -> 102 us
  blocking collectives: 320 us -> 0 us
  other arithmetic: 88.7 us -> 0.1 us
  local copies, waits for them, and re-layouts: 65.9 us -> 6.85 us
  Pallas kernels: 0 us -> 50.6 us
  waiting for transfers between devices: 0.04 us -> 27 us
  starting transfers between devices: 43.6 us -> 17.1 us
  between operations: 9.79 us -> 0.72 us
    psum x5 -> x0, blocking collectives: 320 us -> none  [the longest x3 192 us: energy_total(): return lax.psum(jnp.sum(smooth_field * smooth_image), ('lon', 'lat'))]
    pallas_call x0 -> x5, Pallas kernels: none -> 50.6 us  [the longest x4 48.6 us: call(): pl.pallas_call(kernel, out_shape=outs, in_specs=in_specs, out_specs=[VMEM...]
    slice x15 -> x0, local copies, waits for them, and re-layouts: 40 us -> none  [the longest x6 19.5 us: with_halo(): lax.slice_in_dim(block, 0, width, axis=dim)]
    ppermute x15 -> x11, waiting for transfers between devices: 0.04 us -> 27 us  [swap(): return lax.ppermute(x, AXES, [(i, partner(i)) for i in range(128)])]
    reduce_sum x5 -> x0, other arithmetic: 26.5 us -> none  [the longest x2 22.2 us: energy_total(): return lax.psum(jnp.sum(smooth_field * smooth_image), ('lon', 'lat'))]
    ppermute x15 -> x11, starting transfers between devices: 43.6 us -> 17.1 us  [swap(): return lax.ppermute(x, AXES, [(i, partner(i)) for i in range(128)])]
    add x5 -> x7, other arithmetic: 22.5 us -> 0.06 us  [the longest x6 0.05 us: total_over_devices(): low = low + other[8:] + error]
    mul x9 -> x0, other arithmetic: 21.9 us -> none  [the longest x3 10.4 us: combine(): vertical_flux = coupling * (field[:-1] - field[1:])]
  transfers between devices with their start and end apart: 15 -> 11, of which waited for: 0 -> 8; matrix products, arithmetic and copies ran while one was open for 11% -> 0% of each run, Pallas kernels for 0% -> 15%
where the time goes in v1:
time: 103 us; the launch traced here: 102 us
  Pallas kernels  50.6 us (49%)
  waiting for transfers between devices  27 us (26%)
  starting transfers between devices  17.1 us (17%)
  local copies, waits for them, and re-layouts  6.85 us (7%)
    pallas_call x4, Pallas kernels, call(): pl.pallas_call(kernel, out_shape=outs, in_specs=in_specs, out_specs=[VMEM...  48.6 us
    ppermute x11, waiting for transfers between devices, swap(): return lax.ppermute(x, AXES, [(i, partner(i)) for i in range(128)])  27 us
    ppermute x11, starting transfers between devices, swap(): return lax.ppermute(x, AXES, [(i, partner(i)) for i in range(128)])  17.1 us
    unnamed x10, local copies, waits for them, and re-layouts  6.85 us
  transfers between devices with their start and end apart: 11, of which 8 were waited for; matrix products, arithmetic and copies ran while one was open for 0% of the time, Pallas kernels for 15%

profile of v1, /device:TPU:0, one launch (start us, length us, event | category | flops | bytes accessed | tf_op | source)
XLA Modules:
  0.0 102.3 jit_solution(4533723464784589386)
XLA Ops:
  0.6 0.0 copy-start
  0.6 2.1 %edge_rows.1 = (f32[59,8,128]{2,1,0:T(8,128)}, f32[59,8,128]{2,1,0:T(8,128)}) custom-call(f32[20,256,128]{2,1,0:T(8,128)} %b_hi.1, f32[20,256,128]{2,1,0:T(8,128)} %b_hi.1, f32[20,256,128]{2,1,0:T(8,128)} %h_hi.1, f32[20,256,128]{2,1,0:T(8,128)} %h_hi.1, f32[19,256,128]{2,1,0:T(8,128)} %c_hi.1, f32[19,256,128]{2,1,0:T(8,128)} %c_hi.1), custom_call_target="tpu_custom_call" | custom-call | tf_op jit(solution)/shard_map/edge_rows/pallas_call | solution.py:550
  2.7 0.0 collective-permute-start
  2.7 3.1 %collective-permute-start.1 = (f32[59,8,128]{2,1,0:T(8,128)}, f32[59,8,128]{2,1,0:T(8,128)S(1)}, u32[]{:S(2)}, u32[]{:S(2)}) collective-permute-start(f32[59,8,128]{2,1,0:T(8,128)} %get-tuple-element.30), channel_id=1, source_target_pairs={{0,64},{1,2},{2,1},{3,67},{4,68},{5,6},{6,5},{7,71},{8,72},{9,10},... | collective-permute-start | bytes 725000 | tf_op jit(solution)/shard_map/ppermute | solution.py:28
  5.8 0.0 copy-done
  5.8 0.0 copy-start.1
  5.8 1.7 %copy-done.1 = f32[20,256,128]{2,1,0:T(8,128)S(1)} copy-done((f32[20,256,128]{2,1,0:T(8,128)S(1)}, f32[20,256,128]{2,1,0:T(8,128)}, u32[]{:S(2)}) %copy-start.1) | copy-done | bytes 2621464
  7.5 0.0 copy-start.2
  7.6 1.7 %copy-done.2 = f32[19,256,128]{2,1,0:T(8,128)S(1)} copy-done((f32[19,256,128]{2,1,0:T(8,128)S(1)}, f32[19,256,128]{2,1,0:T(8,128)}, u32[]{:S(2)}) %copy-start.2) | copy-done | bytes 2490392
  9.3 15.1 %first_kernel.1 = (f32[20,256,128]{2,1,0:T(8,128)S(1)}, f32[20,288,128]{2,1,0:T(8,128)S(1)}, f32[20,288,128]{2,1,0:T(8,128)S(1)}, f32[20,288,128]{2,1,0:T(8,128)...) custom-call(f32[20,256,128]{2,1,0:T(8,128)S(1)} %copy-done, ...), custom_call_target="tpu_custom_call" | custom-call | flops 10000000 | bytes 1000000 | tf_op jit(solution)/shard_map/first_kernel/pallas_call | solution.py:521
  24.4 0.0 copy-start.3
  24.4 1.6 %copy-done.3 = f32[20,288,128]{2,1,0:T(8,128)} copy-done((f32[20,288,128]{2,1,0:T(8,128)}, f32[20,288,128]{2,1,0:T(8,128)S(1)}, u32[]{:S(2)}) %copy-start.3) | copy-done | bytes 2949144
  26.0 0.0 collective-permute-done.a_ref
  26.0 0.0 collective-permute-done.1.o_ref
  26.0 4.4 %edge_lanes_kernel.1 = (f32[59,8,128]{2,1,0:T(8,128)S(1)}, f32[59,8,128]{2,1,0:T(8,128)S(1)}, f32[59,8,128]{2,1,0:T(8,128)S(1)}, f32[59,8,128]{2,1,0:T(8,128)S(1)}) custom-call(f32[59,8,128]{2,1,0:T(8,128)S(1)} %collective-permute-done.a_ref, f32[59,8,128]{2,1,0:T(8,128)S(1)} %collective-permute-done.1.o_ref, f32[59,8,128]{2,1,0:T(8,128)S(1)} %get-tuple-element.31.last_ref, ...), custom_call_target="tpu_custom_call" | custom-call | bytes 1000000 | tf_op jit(solution)/shard_map/edge_lanes_kernel/pallas_call | solution.py:521
  30.3 1.6 %collective-permute-start.2 = (f32[59,8,128]{2,1,0:T(8,128)S(1)}, f32[59,8,128]{2,1,0:T(8,128)S(1)}, u32[]{:S(2)}, u32[]{:S(2)}) collective-permute-start(f32[59,8,128]{2,1,0:T(8,128)S(1)} %get-tuple-element.35), channel_id=1, source_target_pairs={{0,4},{1,5},{2,6},{3,7},{4,0},{5,1},{6,2},{7,3},{8,12},{9,13},{10,... | collective-permute-start | bytes 725000 | tf_op jit(solution)/shard_map/ppermute | solution.py:28
  31.9 5.6 %collective-permute-start.3 = (f32[59,8,128]{2,1,0:T(8,128)S(1)}, f32[59,8,128]{2,1,0:T(8,128)S(1)}, u32[]{:S(2)}, u32[]{:S(2)}) collective-permute-start(f32[59,8,128]{2,1,0:T(8,128)S(1)} %get-tuple-element.36), channel_id=1, source_target_pairs={{0,124},{1,125},{2,126},{3,127},{4,8},{5,9},{6,10},{7,11},{8,4},{9... | collective-permute-start | bytes 725000 | tf_op jit(solution)/shard_map/ppermute | solution.py:28
  37.5 0.0 collective-permute-done.2.e_ref
  37.5 6.6 %collective-permute-done.3.d_ref = f32[59,8,128]{2,1,0:T(8,128)S(1)} collective-permute-done((f32[59,8,128]{2,1,0:T(8,128)S(1)}, f32[59,8,128]{2,1,0:T(8,128)S(1)}, u32[]{:S(2)}, u32[]{:S(2)}) %collective-permute-start.3) | collective-permute-done | bytes 241696 | tf_op jit(solution)/shard_map/ppermute | solution.py:28
  44.1 0.0 copy-start.4
  44.1 1.8 %copy-done.4 = f32[20,288,128]{2,1,0:T(8,128)S(1)} copy-done((f32[20,288,128]{2,1,0:T(8,128)S(1)}, f32[20,288,128]{2,1,0:T(8,128)}, u32[]{:S(2)}) %copy-start.4) | copy-done | bytes 2949144
  45.9 25.8 %middle_kernel.1 = (f32[20,288,128]{2,1,0:T(8,128)S(1)}, f32[20,288,128]{2,1,0:T(8,128)S(1)}, f32[20,288,128]{2,1,0:T(8,128)S(1)}, f32[20,288,128]{2,1,0:T(8,128...) custom-call(f32[20,256,128]{2,1,0:T(8,128)S(1)} %get-tuple-element.2, ...), custom_call_target="tpu_custom_call", output_to_operand_aliasing={{0}: (1, {}), {1}: (2, {}), {2}: (3, {}), {3}: (4, {})} | custom-call | flops 100000000 | bytes 1000000 | tf_op jit(solution)/shard_map/middle_kernel/pallas_call | solution.py:521
  71.7 0.1 collective-permute-start.4
  71.8 1.2 %collective-permute-done.4 = f32[16,128]{1,0:T(8,128)S(1)} collective-permute-done((f32[16,128]{1,0:T(8,128)S(1)}, f32[16,128]{1,0:T(8,128)S(1)}, u32[]{:S(2)}, u32[]{:S(2)}) %collective-permute-start.4) | collective-permute-done | bytes 8224 | tf_op jit(solution)/shard_map/ppermute | solution.py:28
  73.0 1.1 %collective-permute-start.5 = (f32[16,128]{1,0:T(8,128)S(1)}, f32[16,128]{1,0:T(8,128)S(1)}, u32[]{:S(2)}, u32[]{:S(2)}) collective-permute-start(f32[16,128]{1,0:T(8,128)S(1)} %pad_maximum_fusion), channel_id=1, source_target_pairs={{0,2},{1,3},{2,0},{3,1},{4,6},{5,7},{6,4},{7,5},{8,10},{9,11},{10,... | collective-permute-start | bytes 24584 | tf_op jit(solution)/shard_map/ppermute | solution.py:28
  74.1 2.6 %collective-permute-done.5 = f32[16,128]{1,0:T(8,128)S(1)} collective-permute-done((f32[16,128]{1,0:T(8,128)S(1)}, f32[16,128]{1,0:T(8,128)S(1)}, u32[]{:S(2)}, u32[]{:S(2)}) %collective-permute-start.5) | collective-permute-done | bytes 8224 | tf_op jit(solution)/shard_map/ppermute | solution.py:28
  76.7 2.5 %collective-permute-start.6 = (f32[16,128]{1,0:T(8,128)S(1)}, f32[16,128]{1,0:T(8,128)S(1)}, u32[]{:S(2)}, u32[]{:S(2)}) collective-permute-start(f32[16,128]{1,0:T(8,128)S(1)} %pad_maximum_fusion.1), channel_id=1, source_target_pairs={{0,66},{1,67},{2,64},{3,65},{4,70},{5,71},{6,68},{7,69},{8,74},{9,... | collective-permute-start | bytes 24584 | tf_op jit(solution)/shard_map/ppermute | solution.py:28
  79.3 2.4 %collective-permute-done.6 = f32[16,128]{1,0:T(8,128)S(1)} collective-permute-done((f32[16,128]{1,0:T(8,128)S(1)}, f32[16,128]{1,0:T(8,128)S(1)}, u32[]{:S(2)}, u32[]{:S(2)}) %collective-permute-start.6) | collective-permute-done | bytes 8224 | tf_op jit(solution)/shard_map/ppermute | solution.py:28
  81.7 0.1 collective-permute-start.7
  81.8 3.6 %collective-permute-done.7 = f32[16,128]{1,0:T(8,128)S(1)} collective-permute-done((f32[16,128]{1,0:T(8,128)S(1)}, f32[16,128]{1,0:T(8,128)S(1)}, u32[]{:S(2)}, u32[]{:S(2)}) %collective-permute-start.7) | collective-permute-done | bytes 8224 | tf_op jit(solution)/shard_map/ppermute | solution.py:28
  85.4 0.1 collective-permute-start.8
  85.5 4.8 %collective-permute-done.8 = f32[16,128]{1,0:T(8,128)S(1)} collective-permute-done((f32[16,128]{1,0:T(8,128)S(1)}, f32[16,128]{1,0:T(8,128)S(1)}, u32[]{:S(2)}, u32[]{:S(2)}) %collective-permute-start.8) | collective-permute-done | bytes 8224 | tf_op jit(solution)/shard_map/ppermute | solution.py:28
  90.4 0.1 collective-permute-start.9
  90.5 3.6 %collective-permute-done.9 = f32[16,128]{1,0:T(8,128)S(1)} collective-permute-done((f32[16,128]{1,0:T(8,128)S(1)}, f32[16,128]{1,0:T(8,128)S(1)}, u32[]{:S(2)}, u32[]{:S(2)}) %collective-permute-start.9) | collective-permute-done | bytes 8224 | tf_op jit(solution)/shard_map/ppermute | solution.py:28
  94.1 2.8 %collective-permute-start.10 = (f32[16,128]{1,0:T(8,128)S(1)}, f32[16,128]{1,0:T(8,128)S(1)}, u32[]{:S(2)}, u32[]{:S(2)}) collective-permute-start(f32[16,128]{1,0:T(8,128)S(1)} %pad_maximum_fusion.5), channel_id=1, source_target_pairs={{0,48},{1,49},{2,50},{3,51},{4,52},{5,53},{6,54},{7,55},{8,56},{9,... | collective-permute-start | bytes 24584 | tf_op jit(solution)/shard_map/ppermute | solution.py:28
  96.9 2.2 %collective-permute-done.10 = f32[16,128]{1,0:T(8,128)S(1)} collective-permute-done((f32[16,128]{1,0:T(8,128)S(1)}, f32[16,128]{1,0:T(8,128)S(1)}, u32[]{:S(2)}, u32[]{:S(2)}) %collective-permute-start.10) | collective-permute-done | bytes 8224 | tf_op jit(solution)/shard_map/ppermute | solution.py:28
  99.1 3.2 %last_kernel.1 = (f32[20,256,128]{2,1,0:T(8,128)}, f32[20,256,128]{2,1,0:T(8,128)}) custom-call(f32[16,128]{1,0:T(8,128)S(1)} %pad_maximum_fusion.6.sums_ref, f32[20,256,128]{2,1,0:T(8,128)S(1)} %get-tuple-element.23.b_ref, f32[20,288,128]{2,1,0:T(8,128)S(1)} %get-tuple-element.38.x0_ref, f32[20,288,128]{2,1,0:T(8,128)S(1)} %get-tuple-element.39.x1_ref, ...), custom_call_target="tpu_custom_call" | custom-call | flops 10000000 | bytes 1000000 | tf_op jit(solution)/shard_map/last_kernel/pallas_call | solution.py:521
  (15 shorter events, 0.1 us)
Async XLA Ops:
  0.6 5.2 %copy-start = (f32[20,256,128]{2,1,0:T(8,128)S(1)}, f32[20,256,128]{2,1,0:T(8,128)}, u32[]{:S(2)}) copy-start(f32[20,256,128]{2,1,0:T(8,128)} %b_hi.1) | copy-start | bytes 7864324
  2.7 23.3 %collective-permute-start = (f32[59,8,128]{2,1,0:T(8,128)}, f32[59,8,128]{2,1,0:T(8,128)S(1)}, u32[]{:S(2)}, u32[]{:S(2)}) collective-permute-start(f32[59,8,128]{2,1,0:T(8,128)} %get-tuple-element.29), channel_id=1, source_target_pairs={{0,1},{1,0},{2,3},{3,2},{4,5},{5,4},{6,7},{7,6},{8,9},{9,8},{10,11... | collective-permute-start | bytes 725000 | tf_op jit(solution)/shard_map/ppermute | solution.py:28
  2.7 23.3 %collective-permute-start.1 = (f32[59,8,128]{2,1,0:T(8,128)}, f32[59,8,128]{2,1,0:T(8,128)S(1)}, u32[]{:S(2)}, u32[]{:S(2)}) collective-permute-start(f32[59,8,128]{2,1,0:T(8,128)} %get-tuple-element.30), channel_id=1, source_target_pairs={{0,64},{1,2},{2,1},{3,67},{4,68},{5,6},{6,5},{7,71},{8,72},{9,10},... | collective-permute-start | bytes 725000 | tf_op jit(solution)/shard_map/ppermute | solution.py:28
  5.8 1.7 %copy-start.1 = (f32[20,256,128]{2,1,0:T(8,128)S(1)}, f32[20,256,128]{2,1,0:T(8,128)}, u32[]{:S(2)}) copy-start(f32[20,256,128]{2,1,0:T(8,128)} %h_hi.1) | copy-start | bytes 7864324
  7.5 1.7 %copy-start.2 = (f32[19,256,128]{2,1,0:T(8,128)S(1)}, f32[19,256,128]{2,1,0:T(8,128)}, u32[]{:S(2)}) copy-start(f32[19,256,128]{2,1,0:T(8,128)} %c_hi.1) | copy-start | bytes 7471108
  24.4 1.6 %copy-start.3 = (f32[20,288,128]{2,1,0:T(8,128)}, f32[20,288,128]{2,1,0:T(8,128)S(1)}, u32[]{:S(2)}) copy-start(f32[20,288,128]{2,1,0:T(8,128)S(1)} %get-tuple-element.24.scaled_in) | copy-start | bytes 8847364
  30.3 7.2 %collective-permute-start.2 = (f32[59,8,128]{2,1,0:T(8,128)S(1)}, f32[59,8,128]{2,1,0:T(8,128)S(1)}, u32[]{:S(2)}, u32[]{:S(2)}) collective-permute-start(f32[59,8,128]{2,1,0:T(8,128)S(1)} %get-tuple-element.35), channel_id=1, source_target_pairs={{0,4},{1,5},{2,6},{3,7},{4,0},{5,1},{6,2},{7,3},{8,12},{9,13},{10,... | collective-permute-start | bytes 725000 | tf_op jit(solution)/shard_map/ppermute | solution.py:28
  31.9 12.2 %collective-permute-start.3 = (f32[59,8,128]{2,1,0:T(8,128)S(1)}, f32[59,8,128]{2,1,0:T(8,128)S(1)}, u32[]{:S(2)}, u32[]{:S(2)}) collective-permute-start(f32[59,8,128]{2,1,0:T(8,128)S(1)} %get-tuple-element.36), channel_id=1, source_target_pairs={{0,124},{1,125},{2,126},{3,127},{4,8},{5,9},{6,10},{7,11},{8,4},{9... | collective-permute-start | bytes 725000 | tf_op jit(solution)/shard_map/ppermute | solution.py:28
  44.1 1.8 %copy-start.4 = (f32[20,288,128]{2,1,0:T(8,128)S(1)}, f32[20,288,128]{2,1,0:T(8,128)}, u32[]{:S(2)}) copy-start(f32[20,288,128]{2,1,0:T(8,128)} %copy-done.3) | copy-start | bytes 8847364
  71.7 1.3 %collective-permute-start.4 = (f32[16,128]{1,0:T(8,128)S(1)}, f32[16,128]{1,0:T(8,128)S(1)}, u32[]{:S(2)}, u32[]{:S(2)}) collective-permute-start(f32[16,128]{1,0:T(8,128)S(1)} %concatenate.24), channel_id=1, source_target_pairs={{0,1},{1,0},{2,3},{3,2},{4,5},{5,4},{6,7},{7,6},{8,9},{9,8},{10,11... | collective-permute-start | bytes 24584 | tf_op jit(solution)/shard_map/ppermute | solution.py:28
  73.0 3.7 %collective-permute-start.5 = (f32[16,128]{1,0:T(8,128)S(1)}, f32[16,128]{1,0:T(8,128)S(1)}, u32[]{:S(2)}, u32[]{:S(2)}) collective-permute-start(f32[16,128]{1,0:T(8,128)S(1)} %pad_maximum_fusion), channel_id=1, source_target_pairs={{0,2},{1,3},{2,0},{3,1},{4,6},{5,7},{6,4},{7,5},{8,10},{9,11},{10,... | collective-permute-start | bytes 24584 | tf_op jit(solution)/shard_map/ppermute | solution.py:28
  76.7 4.9 %collective-permute-start.6 = (f32[16,128]{1,0:T(8,128)S(1)}, f32[16,128]{1,0:T(8,128)S(1)}, u32[]{:S(2)}, u32[]{:S(2)}) collective-permute-start(f32[16,128]{1,0:T(8,128)S(1)} %pad_maximum_fusion.1), channel_id=1, source_target_pairs={{0,66},{1,67},{2,64},{3,65},{4,70},{5,71},{6,68},{7,69},{8,74},{9,... | collective-permute-start | bytes 24584 | tf_op jit(solution)/shard_map/ppermute | solution.py:28
  81.7 3.7 %collective-permute-start.7 = (f32[16,128]{1,0:T(8,128)S(1)}, f32[16,128]{1,0:T(8,128)S(1)}, u32[]{:S(2)}, u32[]{:S(2)}) collective-permute-start(f32[16,128]{1,0:T(8,128)S(1)} %pad_maximum_fusion.2), channel_id=1, source_target_pairs={{0,4},{1,5},{2,6},{3,7},{4,0},{5,1},{6,2},{7,3},{8,12},{9,13},{10,... | collective-permute-start | bytes 24584 | tf_op jit(solution)/shard_map/ppermute | solution.py:28
  85.4 4.9 %collective-permute-start.8 = (f32[16,128]{1,0:T(8,128)S(1)}, f32[16,128]{1,0:T(8,128)S(1)}, u32[]{:S(2)}, u32[]{:S(2)}) collective-permute-start(f32[16,128]{1,0:T(8,128)S(1)} %pad_maximum_fusion.3), channel_id=1, source_target_pairs={{0,12},{1,13},{2,14},{3,15},{4,8},{5,9},{6,10},{7,11},{8,4},{9,5},... | collective-permute-start | bytes 24584 | tf_op jit(solution)/shard_map/ppermute | solution.py:28
  90.4 3.7 %collective-permute-start.9 = (f32[16,128]{1,0:T(8,128)S(1)}, f32[16,128]{1,0:T(8,128)S(1)}, u32[]{:S(2)}, u32[]{:S(2)}) collective-permute-start(f32[16,128]{1,0:T(8,128)S(1)} %pad_maximum_fusion.4), channel_id=1, source_target_pairs={{0,16},{1,17},{2,18},{3,19},{4,20},{5,21},{6,22},{7,23},{8,24},{9,... | collective-permute-start | bytes 24584 | tf_op jit(solution)/shard_map/ppermute | solution.py:28
  94.1 4.9 %collective-permute-start.10 = (f32[16,128]{1,0:T(8,128)S(1)}, f32[16,128]{1,0:T(8,128)S(1)}, u32[]{:S(2)}, u32[]{:S(2)}) collective-permute-start(f32[16,128]{1,0:T(8,128)S(1)} %pad_maximum_fusion.5), channel_id=1, source_target_pairs={{0,48},{1,49},{2,50},{3,51},{4,52},{5,53},{6,54},{7,55},{8,56},{9,... | collective-permute-start | bytes 24584 | tf_op jit(solution)/shard_map/ppermute | solution.py:28

commit v2 on v1

v2 whole, which is shorter than its diff:
```python
import functools
import math

import jax
import jax.numpy as jnp
from jax import lax
from jax.experimental import pallas as pl
from jax.experimental.pallas import tpu as pltpu
from jax.sharding import PartitionSpec as P

LEVELS = 20
ROWS = 256
LANES = 128
TOTAL_ROWS = 1024
LON_COEFF = 4.0
TILES = ROWS // 8 + 2
EXTENDED = 8 * TILES + 16
STACKED = 3 * LEVELS - 1
AT_H = LEVELS
AT_C = 2 * LEVELS
CHUNKS = 8
GROUP = 4
PARTIALS = 16
AXES = ("lon", "lat")
F32 = jnp.float32
MIB = 1 << 20


def swap(x, partner):
    return lax.ppermute(x, AXES, [(i, partner(i)) for i in range(128)])


def lat_even(i):
    return i ^ 1


def lat_odd(i):
    lon, lat = i >> 2, i & 3
    if lat in (1, 2):
        return (lon << 2) | (3 - lat)
    return ((lon ^ 16) << 2) | lat


def lon_even(i):
    return i ^ 4


def lon_odd(i):
    lon, lat = i >> 2, i & 3
    other = (lon + 1) % 32 if lon % 2 else (lon - 1) % 32
    return (other << 2) | lat


def lane_index():
    return lax.broadcasted_iota(jnp.int32, (8, LANES), 1)


def sub_index():
    return lax.broadcasted_iota(jnp.int32, (8, LANES), 0)


def capped_cosine(row):
    angle = (row + 0.5) * (math.pi / TOTAL_ROWS) - 0.5 * math.pi
    square = angle * angle
    value = jnp.full_like(row, 0.0)
    for n in range(8, -1, -1):
        value = value * square + (-1.0) ** n / math.factorial(2 * n)
    return jnp.maximum(value, 0.5)


def row_terms(row):
    here = capped_cosine(row)
    return (
        here,
        LON_COEFF / here,
        (here + capped_cosine(row + 1.0)) * 0.5,
        (here + capped_cosine(row - 1.0)) * 0.5,
    )


def eliminate(tiles):
    count = len(tiles)
    below = [None] * count
    ratio = [None] * count
    value = [None] * count
    for k in range(LEVELS):
        for n, (terms, right, helm, coup, store, put, get) in enumerate(tiles):
            cosine, over, north, south = terms
            pivot = cosine * helm(k) + (2.0 * over + north + south)
            scaled = cosine * coup(k) if k < LEVELS - 1 else None
            if scaled is not None:
                pivot = pivot + scaled
            if k > 0:
                pivot = (pivot + below[n]) - below[n] * ratio[n]
            inverse = 1.0 / pivot
            carried = below[n] * inverse if k > 0 else None
            result = right(k) * inverse
            if k > 0:
                result = result + carried * value[n]
            value[n] = result
            put(k, result)
            ratio[n] = scaled * inverse if scaled is not None else None
            below[n] = scaled
            store(k, carried, inverse, ratio[n])
    for k in range(LEVELS - 2, -1, -1):
        for n, (terms, right, helm, coup, store, put, get) in enumerate(tiles):
            value[n] = get(0, k) + get(1, k) * value[n]
            put(k, value[n])


def packed_edges(read, lane):
    last = jnp.zeros((8, LANES), F32)
    first = jnp.zeros((8, LANES), F32)
    group = lane // 3
    for t in range(1, TILES - 1):
        turned = pltpu.roll(read(t), 3 * t + 3, axis=1)
        last = jnp.where(group == t, turned, last)
        first = jnp.where(group == t + 1, turned, first)
    return last, first


def edge_rows_kernel(b_lo, b_hi, h_lo, h_hi, c_lo, c_hi, a_ref, o_ref):
    even = lax.axis_index("lat") % 2 == 0
    for at, count, lo, hi in (
        (0, LEVELS, b_lo, b_hi),
        (AT_H, LEVELS, h_lo, h_hi),
        (AT_C, LEVELS - 1, c_lo, c_hi),
    ):
        low, high = lo[...], hi[...]
        a_ref[pl.ds(at, count)] = jnp.where(even, high, low)
        o_ref[pl.ds(at, count)] = jnp.where(even, low, high)


def pack_kernel(b_hbm, h_hbm, c_hbm, b_ref, h_ref, c_ref, last_ref, first_ref, sems):
    arrays = (
        (b_hbm, b_ref, 0, LEVELS),
        (h_hbm, h_ref, AT_H, LEVELS),
        (c_hbm, c_ref, AT_C, LEVELS - 1),
    )
    parts = []
    for i, (src, dst, at, count) in enumerate(arrays):
        for n in range(CHUNKS):
            lo, hi = count * n // CHUNKS, count * (n + 1) // CHUNKS
            levels = pl.ds(lo, hi - lo)
            copy = pltpu.make_async_copy(src.at[levels], dst.at[levels], sems.at[i, n])
            copy.start()
            parts.append((copy, dst, at, lo, hi))
    lane = lane_index()
    for copy, source, at, lo, hi in parts:
        copy.wait()

        def level(k, carry):
            last, first = packed_edges(lambda t: source[k, pl.ds(8 * t - 8, 8), :], lane)
            last_ref[at + k] = last
            first_ref[at + k] = first
            return carry

        lax.fori_loop(lo, hi, level, 0)


def first_kernel(
    b_ref, h_ref, c_ref, after_ref, carried_ref, inverse_ref, ratio_ref, x_ref, terms_ref, edge_ref,
    sum_ref
):
    del after_ref
    base = lax.axis_index("lat") * ROWS
    lane = lane_index()
    sub = sub_index()

    def row_term(t, carry):
        row = (base + 8 * t - 8 + sub).astype(F32)
        for i, term in enumerate(row_terms(row)):
            terms_ref[i, pl.ds(pl.multiple_of(8 * t, 8), 8), :] = term
        return carry

    lax.fori_loop(0, TILES, row_term, 0, unroll=2)

    def tiles(g, total):
        ats = [pl.ds(pl.multiple_of(32 * g + 8 * n, 8), 8) for n in range(GROUP)]
        wides = [pl.ds(pl.multiple_of(32 * g + 8 * n + 16, 8), 8) for n in range(GROUP)]
        work = []
        for n in range(GROUP):
            at, wide = ats[n], wides[n]
            terms = [
                terms_ref[i, pl.ds(pl.multiple_of(32 * g + 8 * n + 8, 8), 8), :] for i in range(4)
            ]

            def store(k, carried, inverse, ratio, wide=wide):
                inverse_ref[k, wide, :] = inverse
                if carried is not None:
                    carried_ref[k - 1, wide, :] = carried
                if ratio is not None:
                    ratio_ref[k, wide, :] = ratio

            def put(k, value, wide=wide):
                x_ref[k, wide, :] = value

            def get(which, k, wide=wide):
                return (x_ref, ratio_ref)[which][k, wide, :]

            work.append((
                terms,
                lambda k, at=at: b_ref[k, at, :],
                lambda k, at=at: h_ref[k, at, :],
                lambda k, at=at: c_ref[k, at, :],
                store,
                put,
                get,
            ))
        eliminate(work)
        for at, wide in zip(ats, wides):
            for k in range(LEVELS):
                total = total + x_ref[k, wide, :] * b_ref[k, at, :]
        return total

    sum_ref[...] = lax.fori_loop(0, ROWS // 8 // GROUP, tiles, jnp.zeros((8, LANES), F32))
    gather_edges(x_ref, edge_ref, range(1, TILES - 1), lane // 3)


def gather_edges(x_ref, edge_ref, tiles, group, keep=False):
    def level(k, carry):
        edge = edge_ref[k] if keep else jnp.zeros((8, LANES), F32)
        for t in tiles:
            turned = pltpu.roll(x_ref[k, pl.ds(8 * t + 8, 8), :], 3 * t + 2, axis=1)
            edge = jnp.where(group == t, turned, edge)
        edge_ref[k] = edge
        return carry

    lax.fori_loop(0, LEVELS, level, 0, unroll=4 if keep else 1)


def edge_lanes_kernel(a_ref, o_ref, last_ref, first_ref, south_ref, north_ref, e_ref, d_ref):
    lat = lax.axis_index("lat")
    lat_is_even = lat % 2 == 0
    lon_is_even = lax.axis_index("lon") % 2 == 0
    polar = jnp.logical_or(lat == 0, lat == 3)
    lane = lane_index()
    sub = sub_index()
    group = lane // 3

    def level(j, carry):
        near = a_ref[j]
        far = o_ref[j]
        flipped = far
        for s in (0, 1, 2, 5, 6, 7):
            flipped = jnp.where(sub == s, jnp.broadcast_to(far[7 - s : 8 - s], (8, LANES)), flipped)
        far = jnp.where(polar, flipped, far)
        south = jnp.where(lat_is_even, far, near)
        north = jnp.where(lat_is_even, near, far)
        south_ref[j] = south
        north_ref[j] = north
        last, first = last_ref[j], first_ref[j]
        for t, value in ((0, south), (TILES - 1, north)):
            turned = pltpu.roll(value, 3 * t + 3, axis=1)
            last = jnp.where(group == t, turned, last)
            first = jnp.where(group == t + 1, turned, first)
        first = pltpu.roll(first, LANES - 3, axis=1)
        e_ref[j] = jnp.where(lon_is_even, last, first)
        d_ref[j] = jnp.where(lon_is_even, first, last)
        return carry

    for j in range(STACKED):
        level(j, 0)


def middle_kernel(
    carried_in, inverse_in, ratio_in, x0_in, terms_ref, south_ref, north_ref, e_ref, d_ref,
    edge0_ref, sum_ref,
    carried_ref, inverse_ref, ratio_ref, x0_ref, x1_ref, x2_ref, y1_ref, y2_ref, y3_ref, sums_ref,
    left_ref, right_ref, joint_ref, edge_ref, strip_ref
):
    del carried_in, inverse_in, ratio_in, x0_in
    base = lax.axis_index("lat") * ROWS
    lon_is_even = lax.axis_index("lon") % 2 == 0
    lane = lane_index()
    sub = sub_index()
    slot = lane % 3
    group = lane // 3
    strip_terms = row_terms((base + 8 * group - 8 + sub).astype(F32))

    work = []
    for t, source in ((0, south_ref), (TILES - 1, north_ref)):
        wide = pl.ds(8 * t + 8, 8)

        def store(k, carried, inverse, ratio, wide=wide):
            inverse_ref[k, wide, :] = inverse
            if carried is not None:
                carried_ref[k - 1, wide, :] = carried
            if ratio is not None:
                ratio_ref[k, wide, :] = ratio

        def put(k, value, wide=wide):
            x0_ref[k, wide, :] = value

        def get(which, k, wide=wide):
            return (x0_ref, ratio_ref)[which][k, wide, :]

        work.append((
            [terms_ref[i, pl.ds(8 * t, 8), :] for i in range(4)],
            lambda k, source=source: source[k],
            lambda k, source=source: source[AT_H + k],
            lambda k, source=source: source[AT_C + k],
            store,
            put,
            get,
        ))
    for side, out in ((0, left_ref), (1, right_ref)):

        def received(j, side=side):
            even, odd = (d_ref, e_ref) if side == 0 else (e_ref, d_ref)
            return jnp.where(lon_is_even, even[j], odd[j])

        def store(k, carried, inverse, ratio, side=side):
            strip_ref[side, 1, k] = inverse
            if carried is not None:
                strip_ref[side, 0, k] = carried
            if ratio is not None:
                strip_ref[side, 2, k] = ratio

        def put(k, value, out=out):
            out[k] = value

        def get(which, k, side=side, out=out):
            return out[k] if which == 0 else strip_ref[side, 2, k]

        work.append((
            strip_terms,
            received,
            lambda k, received=received: received(AT_H + k),
            lambda k, received=received: received(AT_C + k),
            store,
            put,
            get,
        ))
    eliminate(work)
    for k in range(LEVELS):
        edge = edge0_ref[k]
        for t in (0, TILES - 1):
            turned = pltpu.roll(x0_ref[k, pl.ds(8 * t + 8, 8), :], 3 * t + 2, axis=1)
            edge = jnp.where(group == t, turned, edge)
        edge_ref[k] = edge

    def join_strips():
        for k in range(LEVELS):
            right = pltpu.roll(right_ref[k], 1, axis=1)
            joint_ref[k] = jnp.where(slot == 2, left_ref[k], right)

    def strip_step():
        _, over, north, south = strip_terms
        value = [None, None]
        for k in range(LEVELS):
            for side, ref in ((0, left_ref), (1, right_ref)):
                x = ref[k]
                up = pltpu.roll(x, 1, axis=1)
                down = pltpu.roll(x, LANES - 1, axis=1)
                if side == 0:
                    down = jnp.where(slot == 2, edge_ref[k], down)
                else:
                    up = jnp.where(slot == 0, pltpu.roll(edge_ref[k], LANES - 1, axis=1), up)
                above = jnp.concatenate([x[1:], pltpu.roll(x, LANES - 3, axis=1)[:1]], 0)
                below = jnp.concatenate([pltpu.roll(x, 3, axis=1)[7:], x[:7]], 0)
                y = over * (up + down) + north * above + south * below
                y = y * strip_ref[side, 1, k]
                if k > 0:
                    y = y + strip_ref[side, 0, k] * value[side]
                value[side] = y
                ref[k] = y
        for k in range(LEVELS - 2, -1, -1):
            for side, ref in ((0, left_ref), (1, right_ref)):
                value[side] = ref[k] + strip_ref[side, 2, k] * value[side]
                ref[k] = value[side]

    def step(tiles, x_ref, y_ref, out_ref, sums):
        starts = [pl.multiple_of(8 * t + 8, 8) for t in tiles]
        wides = [pl.ds(start, 8) for start in starts]
        ats = [pl.ds(pl.multiple_of(8 * t - 8, 8), 8) for t in tiles]
        terms = [
            [terms_ref[i, pl.ds(pl.multiple_of(8 * t, 8), 8), :] for i in range(1, 4)] for t in tiles
        ]
        zero = jnp.zeros((8, LANES), F32)
        cross = [zero] * len(tiles)
        own = [zero] * len(tiles)
        forward = [[] for _ in tiles]
        for k in range(LEVELS):
            for n, t in enumerate(tiles):
                over, north, south = terms[n]
                x = x_ref[k, wides[n], :]
                inject = pltpu.roll(joint_ref[k], 126 - 3 * t, axis=1)
                west = jnp.where(lane == 0, inject, pltpu.roll(x, 1, axis=1))
                east = jnp.where(lane == LANES - 1, inject, pltpu.roll(x, LANES - 1, axis=1))
                above = x_ref[k, pl.ds(starts[n] + 1, 8), :]
                below = x_ref[k, pl.ds(starts[n] - 1, 8), :]
                y = over * (west + east) + north * above + south * below
                if sums is not None:
                    y_ref[k, ats[n], :] = y
                    cross[n] = cross[n] + x * y
                y = y * inverse_ref[k, wides[n], :]
                if k > 0:
                    y = y + carried_ref[k - 1, wides[n], :] * forward[n][-1]
                forward[n].append(y)
        value = [f[-1] for f in forward]
        for k in range(LEVELS - 1, -1, -1):
            for n in range(len(tiles)):
                if k < LEVELS - 1:
                    value[n] = forward[n][k] + ratio_ref[k, wides[n], :] * value[n]
                if out_ref is not None:
                    out_ref[k, wides[n], :] = value[n]
                if sums is not None:
                    own[n] = own[n] + value[n] * y_ref[k, ats[n], :]
        if sums is not None:
            return sums[0] + sum(cross), sums[1] + sum(own)

    zero = jnp.zeros((8, LANES), F32)
    totals = [sum_ref[...]]
    for x_ref, y_ref, out_ref in (
        (x0_ref, y1_ref, x1_ref),
        (x1_ref, y2_ref, x2_ref),
        (x2_ref, y3_ref, None),
    ):
        join_strips()
        totals += lax.fori_loop(
            0,
            ROWS // 8 // GROUP,
            lambda g, sums: step(
                [GROUP * g + n + 1 for n in range(GROUP)], x_ref, y_ref, out_ref, sums
            ),
            (zero, zero),
        )
        if out_ref is not None:
            step([0, TILES - 1], x_ref, None, out_ref, None)
            strip_step()
            if x_ref is x0_ref:
                gather_edges(out_ref, edge_ref, range(TILES), group)
    row = zero[:1]
    for n, total in enumerate(totals):
        part = jnp.sum(total, axis=0, keepdims=True)
        for by in (64, 32, 16):
            part = part + pltpu.roll(part, by, axis=1)
        row = jnp.where(lane[:1] // PARTIALS == n, part, row)
    sums_ref[...] = jnp.broadcast_to(row, sums_ref.shape)


def two_sum(a, b):
    total = a + b
    part = total - a
    return total, (a - (total - part)) + (b - part)


def coefficients(parts):
    pairs = [(part, None) for part in parts]
    while len(pairs) > 1:
        joined = []
        for (a, a_low), (b, b_low) in zip(pairs[::2], pairs[1::2]):
            total, error = two_sum(a, b)
            joined.append((total, error if a_low is None else (a_low + b_low) + error))
        pairs = joined
    high, low = pairs[0]
    for axis, by in ((0, 4), (0, 2), (0, 1), (1, 8), (1, 4), (1, 2), (1, 1)):
        by = high.shape[axis] - by
        high, error = two_sum(high, pltpu.roll(high, by, axis=axis))
        low = (low + pltpu.roll(low, by, axis=axis)) + error
    spread = lambda x: jnp.concatenate(
        [jnp.broadcast_to(x[:1, PARTIALS * n : PARTIALS * n + 1], (1, LANES)) for n in range(8)], 0
    )
    high, low = spread(high), spread(low)
    row = lambda x, n: jnp.broadcast_to(x[n : n + 1], (8, LANES))
    shift = jnp.floor(64.0 * (row(high, 1) / row(high, 0)) + 0.5) * (1.0 / 64.0)
    centred = []
    for n in range(7):
        centred.append(row(high, 0) + row(low, 0))
        if n == 6:
            break
        wide = 4097.0 * high
        coarse = wide - (wide - high)
        fine = high - coarse
        following = jnp.concatenate([high[1:], high[:1]], 0)
        rest = jnp.concatenate([low[1:], low[:1]], 0) - shift * low
        total, error = two_sum(following, -shift * coarse)
        rest = rest + error
        total, error = two_sum(total, -shift * fine)
        rest = rest + error
        high = total + rest
        low = rest - (high - total)
    sigma = 1.0 - shift
    energies = [sigma * centred[n] - centred[n + 1] for n in range(6)]
    curvatures = [sigma * energies[n] - energies[n + 1] for n in range(5)]

    def product(p, q, table):
        return sum(p[i] * q[j] * table[i + j] for i in range(len(p)) for j in range(len(q)))

    one = jnp.ones((8, LANES), F32)
    none = jnp.zeros((8, LANES), F32)
    smoothed = [one]
    direction = [one]
    result = []
    energy = energies[0]
    for iteration in range(3):
        length = energy / product(direction, direction, curvatures)
        result = [
            (result[i] if i < len(result) else none) + length * direction[i]
            for i in range(len(direction))
        ]
        if iteration < 2:
            image = [sigma * d for d in direction] + [none]
            image = [image[i] - (direction[i - 1] if i else none) for i in range(len(image))]
            smoothed = [
                (smoothed[i] if i < len(smoothed) else none) - length * image[i]
                for i in range(len(image))
            ]
            following = product(smoothed, smoothed, energies)
            ratio = following / energy
            direction = [
                smoothed[i] + (ratio * direction[i] if i < len(direction) else none)
                for i in range(len(smoothed))
            ]
            energy = following
    k0, k1, k2 = result
    return k0 - shift * k1 + shift * shift * k2, k1 - 2.0 * shift * k2, k2


def last_kernel(
    sums_ref, b_ref, x0_ref, x1_ref, x2_ref, y1_ref, y2_ref, y3_ref, solution_hbm, residual_hbm,
    solution_ref, residual_ref, sems
):
    step = ROWS // CHUNKS
    k0, k1, k2 = coefficients([sums_ref[8 * n : 8 * n + 8] for n in range(16)])
    r0, r1, r2 = 1.0 - k0, k0 - k1, k1 - k2

    def copy(i, n):
        src = (solution_ref, residual_ref)[i]
        dst = (solution_hbm, residual_hbm)[i]
        rows = pl.ds(n * step, step)
        return pltpu.make_async_copy(src.at[:, rows, :], dst.at[:, rows, :], sems.at[i, n])

    for n in range(CHUNKS):

        def tile(t, carry):
            at = pl.ds(pl.multiple_of(8 * t - 8, 8), 8)
            wide = pl.ds(pl.multiple_of(8 * t + 8, 8), 8)
            for k in range(LEVELS):
                solution_ref[k, at, :] = (
                    k0 * x0_ref[k, wide, :] + k1 * x1_ref[k, wide, :] + k2 * x2_ref[k, wide, :]
                )
                residual_ref[k, at, :] = (
                    r0 * b_ref[k, at, :] + r1 * y1_ref[k, at, :]
                    + r2 * y2_ref[k, at, :] + k2 * y3_ref[k, at, :]
                )
            return carry

        lax.fori_loop(1 + n * step // 8, 1 + (n + 1) * step // 8, tile, 0)
        for i in range(2):
            copy(i, n).start()
    for n in range(CHUNKS):
        for i in range(2):
            copy(i, n).wait()


VMEM = pl.BlockSpec(memory_space=pltpu.VMEM)
ANY = pl.BlockSpec(memory_space=pl.ANY)
HBM = pl.BlockSpec(memory_space=pltpu.HBM)


def kept(*shape):
    return pltpu.VMEM(shape, F32)


def call(kernel, outs, ins, in_specs, out_specs=None, scratch=(), limit=8, flops=0, aliases=None):
    return pl.pallas_call(
        kernel,
        out_shape=outs,
        in_specs=in_specs,
        out_specs=[VMEM] * len(outs) if out_specs is None else out_specs,
        scratch_shapes=list(scratch),
        input_output_aliases=aliases or {},
        compiler_params=pltpu.CompilerParams(vmem_limit_bytes=limit * MIB),
        cost_estimate=pl.CostEstimate(flops=flops, bytes_accessed=1000000, transcendentals=0),
        name=kernel.__name__,
    )(*ins)


def on_device(right_side, helmholtz, coupling):
    right_side, helmholtz, coupling = [
        pltpu.with_memory_space_constraint(x, pltpu.HBM) for x in (right_side, helmholtz, coupling)
    ]
    low = pl.BlockSpec((LEVELS, 8, LANES), lambda i: (0, 0, 0))
    high = pl.BlockSpec((LEVELS, 8, LANES), lambda i: (0, ROWS // 8 - 1, 0))
    low_c = pl.BlockSpec((LEVELS - 1, 8, LANES), lambda i: (0, 0, 0))
    high_c = pl.BlockSpec((LEVELS - 1, 8, LANES), lambda i: (0, ROWS // 8 - 1, 0))
    message = jax.ShapeDtypeStruct((STACKED, 8, LANES), F32)
    whole = pl.BlockSpec((STACKED, 8, LANES), lambda i: (0, 0, 0))
    rows_a, rows_b = pl.pallas_call(
        edge_rows_kernel,
        grid=(1,),
        out_shape=[message, message],
        in_specs=[low, high, low, high, low_c, high_c],
        out_specs=[whole, whole],
        name="edge_rows",
    )(right_side, right_side, helmholtz, helmholtz, coupling, coupling)
    rows_a = swap(rows_a, lat_even)
    rows_b = swap(rows_b, lat_odd)
    field = kept(LEVELS, EXTENDED, LANES)
    block = kept(LEVELS, ROWS, LANES)
    stack = kept(STACKED, 8, LANES)
    edges = kept(LEVELS, 8, LANES)
    b, h, c, last, first = call(
        pack_kernel,
        [block, block, kept(LEVELS - 1, ROWS, LANES), stack, stack],
        [right_side, helmholtz, coupling],
        [HBM] * 3,
        scratch=[pltpu.SemaphoreType.DMA((3, CHUNKS))],
        flops=10000000,
    )
    south, north, lanes_e, lanes_d = call(
        edge_lanes_kernel,
        [stack, stack, message, message],
        [rows_a, rows_b, last, first],
        [VMEM] * 4,
    )
    carried, inverse, ratio, x0, terms, edge0, sum0 = call(
        first_kernel,
        [field] * 4 + [kept(4, 8 * TILES, LANES), edges, kept(8, LANES)],
        [b, h, c, lanes_d],
        [VMEM] * 3 + [ANY],
        flops=10000000,
    )
    lanes_e = swap(lanes_e, lon_even)
    lanes_d = swap(lanes_d, lon_odd)
    carried, inverse, ratio, x0, x1, x2, y1, y2, y3, sums = call(
        middle_kernel,
        [field] * 6 + [block] * 3 + [jax.ShapeDtypeStruct((128, LANES), F32)],
        [carried, inverse, ratio, x0, terms, south, north, lanes_e, lanes_d, edge0, sum0],
        [VMEM] * 11,
        scratch=[
            pltpu.VMEM((LEVELS, 8, LANES), F32),
            pltpu.VMEM((LEVELS, 8, LANES), F32),
            pltpu.VMEM((LEVELS, 8, LANES), F32),
            pltpu.VMEM((LEVELS, 8, LANES), F32),
            pltpu.VMEM((2, 3, LEVELS, 8, LANES), F32),
        ],
        flops=100000000,
        aliases={0: 0, 1: 1, 2: 2, 3: 3},
    )
    sums = lax.all_to_all(sums, AXES, 0, 0, tiled=True)
    result = jax.ShapeDtypeStruct((LEVELS, ROWS, LANES), F32)
    return call(
        last_kernel,
        [result, result],
        [sums, b, x0, x1, x2, y1, y2, y3],
        [VMEM] * 8,
        out_specs=[ANY, ANY],
        scratch=[
            pltpu.VMEM((LEVELS, ROWS, LANES), F32),
            pltpu.VMEM((LEVELS, ROWS, LANES), F32),
            pltpu.SemaphoreType.DMA((2, CHUNKS)),
        ],
        flops=10000000,
    )


def solution(mesh):
    spec = P(None, "lat", "lon")
    return jax.shard_map(
        lambda *args: tuple(on_device(*args)),
        mesh=mesh,
        in_specs=(spec,) * 3,
        out_specs=(spec,) * 2,
        check_vma=False,
    )
```

time: 103 us -> 64.5 us (0.63)
  waiting for transfers between devices: 27 us -> 0.8 us
  blocking collectives: 0 us -> 18.5 us
  Pallas kernels: 50.6 us -> 32.7 us
  local copies, waits for them, and re-layouts: 6.85 us -> 0 us
  starting transfers between devices: 17.1 us -> 10.9 us
    ppermute x11 -> x4, waiting for transfers between devices: 27 us -> 0.8 us  [swap(): return lax.ppermute(x, AXES, [(i, partner(i)) for i in range(128)])]
    all_to_all x0 -> x1, blocking collectives: none -> 18.5 us  [on_device(): sums = lax.all_to_all(sums, AXES, 0, 0, tiled=True)]
    pallas_call x4 -> x5, Pallas kernels: 48.6 us -> 30.8 us  [call(): pl.pallas_call(kernel, out_shape=outs, in_specs=in_specs, out_specs=[VMEM...]
    unnamed x10 -> x0, local copies, waits for them, and re-layouts: 6.85 us -> none
    ppermute x11 -> x4, starting transfers between devices: 17.1 us -> 10.9 us  [swap(): return lax.ppermute(x, AXES, [(i, partner(i)) for i in range(128)])]
  transfers between devices with their start and end apart: 11 -> 4, of which waited for: 8 -> 1; matrix products, arithmetic and copies ran while one was open for 0% -> 0% of each run, Pallas kernels for 15% -> 20%
where the time goes in v2:
time: 64.5 us; the launch traced here: 63.7 us
  Pallas kernels  32.7 us (51%)
  blocking collectives  18.5 us (29%)
  starting transfers between devices  10.9 us (17%)
  waiting for transfers between devices  0.8 us (1%)
  between operations  0.69 us (1%)
    pallas_call x5, Pallas kernels, call(): pl.pallas_call(kernel, out_shape=outs, in_specs=in_specs, out_specs=[VMEM...  30.8 us
    all_to_all x1, blocking collectives, on_device(): sums = lax.all_to_all(sums, AXES, 0, 0, tiled=True)  18.5 us
    ppermute x4, starting transfers between devices, swap(): return lax.ppermute(x, AXES, [(i, partner(i)) for i in range(128)])  10.9 us
    pallas_call x1, Pallas kernels, on_device(): pl.pallas_call(edge_rows_kernel, grid=(1,), out_shape=[message, message],...  1.91 us
  transfers between devices with their start and end apart: 4, of which 1 were waited for; matrix products, arithmetic and copies ran while one was open for 0% of the time, Pallas kernels for 20%

profile of v2, /device:TPU:0, one launch (start us, length us, event | category | flops | bytes accessed | tf_op | source)
XLA Modules:
  0.0 63.7 jit_solution(11552764711101690127)
XLA Ops:
  0.6 1.9 %edge_rows.1 = (f32[59,8,128]{2,1,0:T(8,128)}, f32[59,8,128]{2,1,0:T(8,128)}) custom-call(f32[20,256,128]{2,1,0:T(8,128)} %b_hi.1, f32[20,256,128]{2,1,0:T(8,128)} %b_hi.1, f32[20,256,128]{2,1,0:T(8,128)} %h_hi.1, f32[20,256,128]{2,1,0:T(8,128)} %h_hi.1, f32[19,256,128]{2,1,0:T(8,128)} %c_hi.1, f32[19,256,128]{2,1,0:T(8,128)} %c_hi.1), custom_call_target="tpu_custom_call" | custom-call | tf_op jit(solution)/shard_map/edge_rows/pallas_call | solution.py:591
  2.5 0.0 collective-permute-start
  2.5 3.1 %collective-permute-start.1 = (f32[59,8,128]{2,1,0:T(8,128)}, f32[59,8,128]{2,1,0:T(8,128)S(1)}, u32[]{:S(2)}, u32[]{:S(2)}) collective-permute-start(f32[59,8,128]{2,1,0:T(8,128)} %get-tuple-element.31), channel_id=1, source_target_pairs={{0,64},{1,2},{2,1},{3,67},{4,68},{5,6},{6,5},{7,71},{8,72},{9,10},... | collective-permute-start | bytes 725000 | tf_op jit(solution)/shard_map/ppermute | solution.py:30
  5.6 7.2 %pack_kernel.1 = (f32[20,256,128]{2,1,0:T(8,128)S(1)}, f32[20,256,128]{2,1,0:T(8,128)S(1)}, f32[19,256,128]{2,1,0:T(8,128)S(1)}, f32[59,8,128]{2,1,0:T(8,128)S(1)}, f32[59,8,128]{2,1,0:T(8,128)S(1)}) custom-call(f32[20,256,128]{2,1,0:T(8,128)} %b_hi.1, f32[20,256,128]{2,1,0:T(8,128)} %h_hi.1, f32[19,256,128]{2,1,0:T(8,128)} %c_hi.1), custom_call_target="tpu_custom_call" | custom-call | flops 10000000 | bytes 1000000 | tf_op jit(solution)/shard_map/pack_kernel/pallas_call | solution.py:568
  12.9 0.0 collective-permute-done.a_ref
  12.9 0.0 collective-permute-done.1.o_ref
  12.9 1.0 %edge_lanes_kernel.1 = (f32[59,8,128]{2,1,0:T(8,128)S(1)}, f32[59,8,128]{2,1,0:T(8,128)S(1)}, f32[59,8,128]{2,1,0:T(8,128)S(1)}, f32[59,8,128]{2,1,0:T(8,128)S(1)}) custom-call(f32[59,8,128]{2,1,0:T(8,128)S(1)} %collective-permute-done.a_ref, f32[59,8,128]{2,1,0:T(8,128)S(1)} %collective-permute-done.1.o_ref, f32[59,8,128]{2,1,0:T(8,128)S(1)} %get-tuple-element.32.last_ref, ...), custom_call_target="tpu_custom_call" | custom-call | bytes 1000000 | tf_op jit(solution)/shard_map/edge_lanes_kernel/pallas_call | solution.py:568
  13.9 1.7 %collective-permute-start.2 = (f32[59,8,128]{2,1,0:T(8,128)S(1)}, f32[59,8,128]{2,1,0:T(8,128)S(1)}, u32[]{:S(2)}, u32[]{:S(2)}) collective-permute-start(f32[59,8,128]{2,1,0:T(8,128)S(1)} %get-tuple-element.42), channel_id=1, source_target_pairs={{0,4},{1,5},{2,6},{3,7},{4,0},{5,1},{6,2},{7,3},{8,12},{9,13},{10,... | collective-permute-start | bytes 725000 | tf_op jit(solution)/shard_map/ppermute | solution.py:30
  15.7 6.1 %collective-permute-start.3 = (f32[59,8,128]{2,1,0:T(8,128)S(1)}, f32[59,8,128]{2,1,0:T(8,128)S(1)}, u32[]{:S(2)}, u32[]{:S(2)}) collective-permute-start(f32[59,8,128]{2,1,0:T(8,128)S(1)} %get-tuple-element.34.after_ref), channel_id=1, source_target_pairs={{0,124},{1,125},{2,126},{3,127},{4,8},{5,9},{6,10},{7,11},{8,4},{9... | collective-permute-start | bytes 725000 | tf_op jit(solution)/shard_map/ppermute | solution.py:30
  21.8 5.5 %first_kernel.1 = (f32[20,288,128]{2,1,0:T(8,128)S(1)}, f32[20,288,128]{2,1,0:T(8,128)S(1)}, f32[20,288,128]{2,1,0:T(8,128)S(1)}, f32[20,288,128]{2,1,0:T(8,128)...) custom-call(f32[20,256,128]{2,1,0:T(8,128)S(1)} %get-tuple-element.27.b_ref, ...), custom_call_target="tpu_custom_call" | custom-call | flops 10000000 | bytes 1000000 | tf_op jit(solution)/shard_map/first_kernel/pallas_call | solution.py:568
  27.3 0.0 collective-permute-done.2.e_ref
  27.3 0.8 %collective-permute-done.3.d_ref = f32[59,8,128]{2,1,0:T(8,128)S(1)} collective-permute-done((f32[59,8,128]{2,1,0:T(8,128)S(1)}, f32[59,8,128]{2,1,0:T(8,128)S(1)}, u32[]{:S(2)}, u32[]{:S(2)}) %collective-permute-start.3) | collective-permute-done | bytes 241696 | tf_op jit(solution)/shard_map/ppermute | solution.py:30
  28.1 14.0 %middle_kernel.1 = (f32[20,288,128]{2,1,0:T(8,128)S(1)}, f32[20,288,128]{2,1,0:T(8,128)S(1)}, f32[20,288,128]{2,1,0:T(8,128)S(1)}, f32[20,288,128]{2,1,0:T(8,128...) custom-call(f32[20,288,128]{2,1,0:T(8,128)S(1)} %get-tuple-element.3, ...), custom_call_target="tpu_custom_call", output_to_operand_aliasing={{0}: (0, {}), {1}: (1, {}), {2}: (2, {}), {3}: (3, {})} | custom-call | flops 100000000 | bytes 1000000 | tf_op jit(solution)/shard_map/middle_kernel/pallas_call | solution.py:568
  42.1 18.5 %all_to_all.11 = f32[128,1,128]{2,1,0:T(1,128)S(1)} all-to-all(f32[128,1,128]{2,1,0:T(1,128)S(1)} %bitcast.5), channel_id=1, replica_groups=mesh['lon'=32,'lat'=4] {'lon','lat'}, dimensions={0} | all-to-all | bytes 131072 | tf_op jit(solution)/shard_map/all_to_all | solution.py:643
  60.6 3.1 %last_kernel.1 = (f32[20,256,128]{2,1,0:T(8,128)}, f32[20,256,128]{2,1,0:T(8,128)}) custom-call(f32[128,128]{1,0:T(8,128)S(1)} %bitcast.4, f32[20,256,128]{2,1,0:T(8,128)S(1)} %get-tuple-element.27.b_ref, f32[20,288,128]{2,1,0:T(8,128)S(1)} %get-tuple-element.46.x0_ref, f32[20,288,128]{2,1,0:T(8,128)S(1)} %get-tuple-element.47.x1_ref, ...), custom_call_target="tpu_custom_call" | custom-call | flops 10000000 | bytes 1000000 | tf_op jit(solution)/shard_map/last_kernel/pallas_call | solution.py:568
Async XLA Ops:
  2.5 10.3 %collective-permute-start = (f32[59,8,128]{2,1,0:T(8,128)}, f32[59,8,128]{2,1,0:T(8,128)S(1)}, u32[]{:S(2)}, u32[]{:S(2)}) collective-permute-start(f32[59,8,128]{2,1,0:T(8,128)} %get-tuple-element.30), channel_id=1, source_target_pairs={{0,1},{1,0},{2,3},{3,2},{4,5},{5,4},{6,7},{7,6},{8,9},{9,8},{10,11... | collective-permute-start | bytes 725000 | tf_op jit(solution)/shard_map/ppermute | solution.py:30
  2.5 10.4 %collective-permute-start.1 = (f32[59,8,128]{2,1,0:T(8,128)}, f32[59,8,128]{2,1,0:T(8,128)S(1)}, u32[]{:S(2)}, u32[]{:S(2)}) collective-permute-start(f32[59,8,128]{2,1,0:T(8,128)} %get-tuple-element.31), channel_id=1, source_target_pairs={{0,64},{1,2},{2,1},{3,67},{4,68},{5,6},{6,5},{7,71},{8,72},{9,10},... | collective-permute-start | bytes 725000 | tf_op jit(solution)/shard_map/ppermute | solution.py:30
  13.9 13.3 %collective-permute-start.2 = (f32[59,8,128]{2,1,0:T(8,128)S(1)}, f32[59,8,128]{2,1,0:T(8,128)S(1)}, u32[]{:S(2)}, u32[]{:S(2)}) collective-permute-start(f32[59,8,128]{2,1,0:T(8,128)S(1)} %get-tuple-element.42), channel_id=1, source_target_pairs={{0,4},{1,5},{2,6},{3,7},{4,0},{5,1},{6,2},{7,3},{8,12},{9,13},{10,... | collective-permute-start | bytes 725000 | tf_op jit(solution)/shard_map/ppermute | solution.py:30
  15.7 12.4 %collective-permute-start.3 = (f32[59,8,128]{2,1,0:T(8,128)S(1)}, f32[59,8,128]{2,1,0:T(8,128)S(1)}, u32[]{:S(2)}, u32[]{:S(2)}) collective-permute-start(f32[59,8,128]{2,1,0:T(8,128)S(1)} %get-tuple-element.34.after_ref), channel_id=1, source_target_pairs={{0,124},{1,125},{2,126},{3,127},{4,8},{5,9},{6,10},{7,11},{8,4},{9... | collective-permute-start | bytes 725000 | tf_op jit(solution)/shard_map/ppermute | solution.py:30

commit v3 on v2

v3 whole, which is shorter than its diff:
```python
import functools
import math

import jax
import jax.numpy as jnp
from jax import lax
from jax.experimental import pallas as pl
from jax.experimental.pallas import tpu as pltpu
from jax.sharding import PartitionSpec as P

LEVELS = 20
ROWS = 256
LANES = 128
TOTAL_ROWS = 1024
LON_COEFF = 4.0
TILES = ROWS // 8 + 2
EXTENDED = 8 * TILES + 16
STACKED = 3 * LEVELS - 1
AT_H = LEVELS
AT_C = 2 * LEVELS
CHUNKS = 8
GROUP = 8
PARTIALS = 16
PAD = 8
LANE_MESSAGE = LEVELS + (2 * LEVELS + 1) // 3
AXES = ("lon", "lat")
F32 = jnp.float32
MIB = 1 << 20


def swap(x, partner):
    return lax.ppermute(x, AXES, [(i, partner(i)) for i in range(128)])


def lat_even(i):
    return i ^ 1


def lat_odd(i):
    lon, lat = i >> 2, i & 3
    if lat in (1, 2):
        return (lon << 2) | (3 - lat)
    return ((lon ^ 16) << 2) | lat


def lon_even(i):
    return i ^ 4


def lon_odd(i):
    lon, lat = i >> 2, i & 3
    other = (lon + 1) % 32 if lon % 2 else (lon - 1) % 32
    return (other << 2) | lat


def lane_index():
    return lax.broadcasted_iota(jnp.int32, (8, LANES), 1)


def sub_index():
    return lax.broadcasted_iota(jnp.int32, (8, LANES), 0)


def capped_cosine(row):
    angle = (row + 0.5) * (math.pi / TOTAL_ROWS) - 0.5 * math.pi
    square = angle * angle
    value = jnp.full_like(row, 0.0)
    for n in range(8, -1, -1):
        value = value * square + (-1.0) ** n / math.factorial(2 * n)
    return jnp.maximum(value, 0.5)


def row_terms(row):
    here = capped_cosine(row)
    return (
        here,
        LON_COEFF / here,
        (here + capped_cosine(row + 1.0)) * 0.5,
        (here + capped_cosine(row - 1.0)) * 0.5,
    )


def eliminate(tiles):
    count = len(tiles)
    below = [None] * count
    ratio = [None] * count
    value = [None] * count
    total = [None] * count
    for k in range(LEVELS):
        for n, (terms, right, helm, coup, store, put, get) in enumerate(tiles):
            cosine, over, north, south = terms
            pivot = cosine * helm(k) + (2.0 * over + north + south)
            scaled = cosine * coup(k) if k < LEVELS - 1 else None
            if scaled is not None:
                pivot = pivot + scaled
            if k > 0:
                pivot = (pivot + below[n]) - below[n] * ratio[n]
            inverse = 1.0 / pivot
            summed = right(k)
            if k > 0:
                summed = summed + below[n] * value[n]
            value[n] = summed * inverse
            total[n] = summed * value[n] if k == 0 else total[n] + summed * value[n]
            put(k, value[n])
            ratio[n] = scaled * inverse if scaled is not None else None
            below[n] = scaled
            store(k, scaled, inverse, ratio[n])
    for k in range(LEVELS - 2, -1, -1):
        for n, (terms, right, helm, coup, store, put, get) in enumerate(tiles):
            value[n] = get(0, k) + get(1, k) * value[n]
            put(k, value[n])
    return total


def rows_beside(x):
    above = jnp.concatenate([x[1:], pltpu.roll(x, LANES - 3, axis=1)[:1]], 0)
    below = jnp.concatenate([pltpu.roll(x, 3, axis=1)[7:], x[:7]], 0)
    return above, below


def packed_edges(read, lane):
    last = jnp.zeros((8, LANES), F32)
    first = jnp.zeros((8, LANES), F32)
    group = lane // 3
    for t in range(1, TILES - 1):
        turned = pltpu.roll(read(t), 3 * t + 3, axis=1)
        last = jnp.where(group == t, turned, last)
        first = jnp.where(group == t + 1, turned, first)
    return last, first


def edge_rows_kernel(b_lo, b_hi, h_lo, h_hi, c_lo, c_hi, a_ref, o_ref):
    lat = lax.axis_index("lat")
    even = lat % 2 == 0
    levels = [
        (at + k, lo, hi, k)
        for at, count, lo, hi in (
            (0, LEVELS, b_lo, b_hi),
            (AT_H, LEVELS, h_lo, h_hi),
            (AT_C, LEVELS - 1, c_lo, c_hi),
        )
        for k in range(count)
    ]

    def put_high(ref):
        for j, lo, hi, k in reversed(levels):
            ref[pl.ds(PAD + 3 * j - 5, 8), :] = hi[k]

    def put_low(ref):
        for j, lo, hi, k in levels:
            ref[pl.ds(PAD + 3 * j, 8), :] = lo[k]

    @pl.when(even)
    def _():
        put_high(a_ref)

    @pl.when(jnp.logical_not(even))
    def _():
        put_low(a_ref)

    @pl.when(lat == 0)
    def _():
        for j, lo, hi, k in levels:
            for i in range(3):
                o_ref[pl.ds(PAD + 3 * j + i, 1), :] = lo[k, pl.ds(2 - i, 1), :]

    @pl.when(lat == 1)
    def _():
        put_high(o_ref)

    @pl.when(lat == 2)
    def _():
        put_low(o_ref)

    @pl.when(lat == 3)
    def _():
        for j, lo, hi, k in levels:
            for i in range(3):
                o_ref[pl.ds(PAD + 3 * j + i, 1), :] = hi[k, pl.ds(7 - i, 1), :]


def pack_kernel(b_hbm, h_hbm, c_hbm, b_ref, h_ref, c_ref, last_ref, first_ref, sems):
    arrays = (
        (b_hbm, b_ref, 0, LEVELS),
        (h_hbm, h_ref, AT_H, LEVELS),
        (c_hbm, c_ref, AT_C, LEVELS - 1),
    )
    parts = []
    for i, (src, dst, at, count) in enumerate(arrays):
        for n in range(CHUNKS):
            lo, hi = count * n // CHUNKS, count * (n + 1) // CHUNKS
            levels = pl.ds(lo, hi - lo)
            copy = pltpu.make_async_copy(src.at[levels], dst.at[levels], sems.at[i, n])
            copy.start()
            parts.append((copy, dst, at, lo, hi))
    lane = lane_index()
    for copy, source, at, lo, hi in parts:
        copy.wait()

        for k in range(lo, hi):
            last, first = packed_edges(lambda t: source[k, pl.ds(8 * t - 8, 8), :], lane)
            last_ref[at + k] = last
            first_ref[at + k] = first


def first_kernel(
    b_ref, h_ref, c_ref, halo_ref, scaled_ref, inverse_ref, ratio_ref, x_ref, terms_ref, edge_ref,
    sum_ref, y_ref
):
    base = lax.axis_index("lat") * ROWS
    lane = lane_index()
    sub = sub_index()

    def row_term(t, carry):
        row = (base + 8 * t - 8 + sub).astype(F32)
        for i, term in enumerate(row_terms(row)):
            terms_ref[i, pl.ds(pl.multiple_of(8 * t, 8), 8), :] = term
        return carry

    lax.fori_loop(0, TILES, row_term, 0, unroll=2)
    for n, t in ((0, 0), (1, TILES - 1)):
        for k in range(LEVELS):
            wide = pl.ds(8 * t + 8, 8)
            x_ref[k, wide, :] = halo_ref[n, 0, k]
            inverse_ref[k, wide, :] = halo_ref[n, 2, k]
            if k < LEVELS - 1:
                scaled_ref[k, wide, :] = halo_ref[n, 1, k]
                ratio_ref[k, wide, :] = halo_ref[n, 3, k]

    def tiles(g, total):
        work = []
        for n in range(4):
            at = pl.ds(pl.multiple_of(32 * g + 8 * n, 8), 8)
            wide = pl.ds(pl.multiple_of(32 * g + 8 * n + 16, 8), 8)
            terms = [
                terms_ref[i, pl.ds(pl.multiple_of(32 * g + 8 * n + 8, 8), 8), :] for i in range(4)
            ]

            def store(k, scaled, inverse, ratio, wide=wide):
                inverse_ref[k, wide, :] = inverse
                if scaled is not None:
                    scaled_ref[k, wide, :] = scaled
                    ratio_ref[k, wide, :] = ratio

            def put(k, value, wide=wide):
                x_ref[k, wide, :] = value

            def get(which, k, wide=wide):
                return (x_ref, ratio_ref)[which][k, wide, :]

            work.append((
                terms,
                lambda k, at=at: b_ref[k, at, :],
                lambda k, at=at: h_ref[k, at, :],
                lambda k, at=at: c_ref[k, at, :],
                store,
                put,
                get,
            ))
        return total + sum(eliminate(work))

    sum_ref[...] = lax.fori_loop(0, ROWS // 32, tiles, jnp.zeros((8, LANES), F32))
    gather_edges(x_ref, edge_ref, range(TILES), lane // 3)

    def neighbours(g, carry):
        for n in range(4):
            start = pl.multiple_of(32 * g + 8 * n + 16, 8)
            here = pl.ds(pl.multiple_of(32 * g + 8 * n + 8, 8), 8)
            over, north, south = [terms_ref[i, here, :] for i in range(1, 4)]
            for k in range(LEVELS):
                x = x_ref[k, pl.ds(start, 8), :]
                west = jnp.where(lane == 0, 0.0, pltpu.roll(x, 1, axis=1))
                east = jnp.where(lane == LANES - 1, 0.0, pltpu.roll(x, LANES - 1, axis=1))
                above = x_ref[k, pl.ds(start + 1, 8), :]
                below = x_ref[k, pl.ds(start - 1, 8), :]
                y_ref[k, pl.ds(pl.multiple_of(32 * g + 8 * n, 8), 8), :] = (
                    over * (west + east) + north * above + south * below
                )
        return carry

    lax.fori_loop(0, ROWS // 32, neighbours, 0)


def gather_edges(x_ref, edge_ref, tiles, group):
    def level(k, carry):
        edge = jnp.zeros((8, LANES), F32)
        for t in tiles:
            turned = pltpu.roll(x_ref[k, pl.ds(8 * t + 8, 8), :], 3 * t + 2, axis=1)
            edge = jnp.where(group == t, turned, edge)
        edge_ref[k] = edge
        return carry

    lax.fori_loop(0, LEVELS, level, 0, unroll=2)


def edge_lanes_kernel(
    a_ref, o_ref, last_ref, first_ref, halo_ref, e_ref, d_ref, raw_ref, strip_ref, part_ref
):
    even = lax.axis_index("lat") % 2 == 0
    lon_is_even = lax.axis_index("lon") % 2 == 0
    base = lax.axis_index("lat") * ROWS
    lane = lane_index()
    sub = sub_index()
    group = lane // 3
    slot = lane % 3
    for j in range(STACKED):
        low, high = pl.ds(PAD + 3 * j - 5, 8), pl.ds(PAD + 3 * j, 8)
        south = jnp.where(even, o_ref[low, :], a_ref[low, :])
        north = jnp.where(even, a_ref[high, :], o_ref[high, :])
        raw_ref[0, j] = south
        raw_ref[1, j] = north
        last, first = last_ref[j], first_ref[j]
        for t, value in ((0, south), (TILES - 1, north)):
            turned = pltpu.roll(value, 3 * t + 3, axis=1)
            last = jnp.where(group == t, turned, last)
            first = jnp.where(group == t + 1, turned, first)
        raw_ref[2, j] = last
        raw_ref[3, j] = pltpu.roll(first, LANES - 3, axis=1)
    strip_terms = row_terms((base + 8 * group - 8 + sub).astype(F32))
    work = []
    for n in range(4):
        if n < 2:
            terms = row_terms((base + (TILES - 1) * 8 * n - 8 + sub).astype(F32))
            keep = halo_ref.at[n]
        else:
            terms = strip_terms
            keep = strip_ref.at[n - 2]

        def store(k, scaled, inverse, ratio, keep=keep):
            keep[2, k] = inverse
            if scaled is not None:
                keep[1, k] = scaled
                keep[3, k] = ratio

        def put(k, value, keep=keep):
            keep[0, k] = value

        def get(which, k, keep=keep):
            return keep[3 * which, k]

        work.append((
            terms,
            lambda k, n=n: raw_ref[n, k],
            lambda k, n=n: raw_ref[n, AT_H + k],
            lambda k, n=n: raw_ref[n, AT_C + k],
            store,
            put,
            get,
        ))
    eliminate(work)
    _, over, north, south = strip_terms
    value = [None, None]
    for k in range(LEVELS):
        for side in (0, 1):
            x = strip_ref[side, 0, k]
            up = pltpu.roll(x, 1, axis=1)
            down = pltpu.roll(x, LANES - 1, axis=1)
            if side == 0:
                down = jnp.where(slot == 2, 0.0, down)
            else:
                up = jnp.where(slot == 0, 0.0, up)
            above, below = rows_beside(x)
            y = over * (up + down) + north * above + south * below
            part_ref[side, 0, k] = y
            if k > 0:
                y = y + strip_ref[side, 1, k - 1] * value[side]
            value[side] = y * strip_ref[side, 2, k]
            part_ref[side, 1, k] = value[side]
    for k in range(LEVELS - 1, -1, -1):
        messages = []
        for side in (0, 1):
            if k < LEVELS - 1:
                value[side] = part_ref[side, 1, k] + strip_ref[side, 3, k] * value[side]
            outer = 2 - 2 * side
            known = pltpu.roll(part_ref[side, 0, k], (2 - 2 * outer) % LANES, axis=1)
            message = jnp.where(slot == outer, strip_ref[side, 0, k], known)
            messages.append(jnp.where(slot == 1, value[side], message))
        last, first = messages
        e_ref[k] = jnp.where(lon_is_even, last, first)
        d_ref[k] = jnp.where(lon_is_even, first, last)
    for m in range(LEVELS, LANE_MESSAGE):
        messages = []
        for side in (0, 1):
            outer = 2 - 2 * side
            message = jnp.zeros((8, LANES), F32)
            for q in range(3):
                at = 3 * (m - LEVELS) + q
                source = strip_ref[side, 2, at] if at < LEVELS else strip_ref[side, 1, at - LEVELS]
                message = jnp.where(slot == q, pltpu.roll(source, (q - outer) % LANES, axis=1), message)
            messages.append(message)
        last, first = messages
        e_ref[m] = jnp.where(lon_is_even, last, first)
        d_ref[m] = jnp.where(lon_is_even, first, last)


def middle_kernel(
    scaled_ref, inverse_ref, ratio_ref, x0_ref, y1_in, terms_ref, e_ref, d_ref, edge0_ref, sum_ref,
    y1_ref, x1_ref, x2_ref, y2_ref, y3_ref, sums_ref, strip0_ref, strip_ref, further_ref, edge_ref,
    factor_ref
):
    del y1_in
    base = lax.axis_index("lat") * ROWS
    lon_is_even = lax.axis_index("lon") % 2 == 0
    lane = lane_index()
    sub = sub_index()
    slot = lane % 3
    group = lane // 3
    _, strip_over, strip_north, strip_south = row_terms((base + 8 * group - 8 + sub).astype(F32))

    def turned(x, by):
        return pltpu.roll(x, by % LANES, axis=1) if by % LANES else x

    def arrived(m):
        e, d = e_ref[m], d_ref[m]
        return jnp.where(lon_is_even, d, e), jnp.where(lon_is_even, e, d)

    for m in range(LEVELS, LANE_MESSAGE):
        left, right = arrived(m)
        for q in range(3):
            at = 3 * (m - LEVELS) + q
            value = jnp.where(slot == 2, turned(left, 2 - q), turned(right, 1 - q))
            if at < LEVELS:
                factor_ref[1, at] = value
            else:
                factor_ref[0, at - LEVELS] = value
    for k in range(LEVELS - 1):
        factor_ref[2, k] = factor_ref[0, k] * factor_ref[1, k]

    def solve_strip(right, out_ref):
        value = None
        for k in range(LEVELS):
            y = right(k)
            if k > 0:
                y = y + factor_ref[0, k - 1] * value
            value = y * factor_ref[1, k]
            out_ref[k] = value
        for k in range(LEVELS - 2, -1, -1):
            value = out_ref[k] + factor_ref[2, k] * value
            out_ref[k] = value

    def first_right(k):
        left, right = arrived(k)
        strip0_ref[k] = jnp.where(slot == 2, left, turned(right, 1))
        further_ref[k] = jnp.where(slot == 2, turned(left, 1), right)
        known = jnp.where(slot == 2, turned(left, 2), turned(right, -1))
        return known + strip_over * edge0_ref[k]

    def second_right(k):
        above, below = rows_beside(strip_ref[k])
        beside = further_ref[k] + edge_ref[k]
        return strip_over * beside + strip_north * above + strip_south * below

    def step(tiles, x_ref, y_ref, out_ref, halo_ref, sums, begun=False):
        starts = [pl.multiple_of(8 * t + 8, 8) for t in tiles]
        wides = [pl.ds(start, 8) for start in starts]
        ats = [pl.ds(pl.multiple_of(8 * t - 8, 8), 8) for t in tiles]
        terms = [
            [terms_ref[i, pl.ds(pl.multiple_of(8 * t, 8), 8), :] for i in range(1, 4)] for t in tiles
        ]
        zero = jnp.zeros((8, LANES), F32)
        cross = [zero] * len(tiles)
        own = [zero] * len(tiles)
        forward = [[] for _ in tiles]
        for k in range(LEVELS):
            for n, t in enumerate(tiles):
                over, north, south = terms[n]
                x = x_ref[k, wides[n], :]
                inject = pltpu.roll(halo_ref[k], 126 - 3 * t, axis=1)
                if begun:
                    inject = jnp.where((lane == 0) | (lane == LANES - 1), inject, 0.0)
                    y = y_ref[k, ats[n], :] + over * inject
                else:
                    west = jnp.where(lane == 0, inject, pltpu.roll(x, 1, axis=1))
                    east = jnp.where(lane == LANES - 1, inject, pltpu.roll(x, LANES - 1, axis=1))
                    above = x_ref[k, pl.ds(starts[n] + 1, 8), :]
                    below = x_ref[k, pl.ds(starts[n] - 1, 8), :]
                    y = over * (west + east) + north * above + south * below
                if sums is not None:
                    y_ref[k, ats[n], :] = y
                    cross[n] = cross[n] + x * y
                if k > 0:
                    y = y + scaled_ref[k - 1, wides[n], :] * forward[n][-1]
                value = y * inverse_ref[k, wides[n], :]
                if sums is not None:
                    own[n] = own[n] + y * value
                forward[n].append(value)
        if out_ref is not None:
            value = [f[-1] for f in forward]
            for k in range(LEVELS - 1, -1, -1):
                for n in range(len(tiles)):
                    if k < LEVELS - 1:
                        value[n] = forward[n][k] + ratio_ref[k, wides[n], :] * value[n]
                    out_ref[k, wides[n], :] = value[n]
        if sums is not None:
            return sums[0] + sum(cross), sums[1] + sum(own)

    zero = jnp.zeros((8, LANES), F32)
    totals = [sum_ref[...]]
    solve_strip(first_right, strip_ref)
    for x_ref, y_ref, out_ref, halo_ref in (
        (x0_ref, y1_ref, x1_ref, strip0_ref),
        (x1_ref, y2_ref, x2_ref, strip_ref),
        (x2_ref, y3_ref, None, strip_ref),
    ):
        totals += lax.fori_loop(
            0,
            ROWS // 8 // GROUP,
            lambda g, sums: step(
                [GROUP * g + n + 1 for n in range(GROUP)], x_ref, y_ref, out_ref, halo_ref, sums,
                x_ref is x0_ref
            ),
            (zero, zero),
        )
        if out_ref is not None:
            step([0, TILES - 1], x_ref, None, out_ref, halo_ref, None)
        if x_ref is x0_ref:
            gather_edges(out_ref, edge_ref, range(TILES), group)
        elif x_ref is x1_ref:
            solve_strip(second_right, strip_ref)
    row = zero[:1]
    for n, total in enumerate(totals):
        part = jnp.sum(total, axis=0, keepdims=True)
        for by in (64, 32, 16):
            part = part + pltpu.roll(part, by, axis=1)
        row = jnp.where(lane[:1] // PARTIALS == n, part, row)
    sums_ref[...] = jnp.broadcast_to(row, sums_ref.shape)


def two_sum(a, b):
    total = a + b
    part = total - a
    return total, (a - (total - part)) + (b - part)


def coefficients(parts):
    pairs = [(part, None) for part in parts]
    while len(pairs) > 1:
        joined = []
        for (a, a_low), (b, b_low) in zip(pairs[::2], pairs[1::2]):
            total, error = two_sum(a, b)
            joined.append((total, error if a_low is None else (a_low + b_low) + error))
        pairs = joined
    high, low = pairs[0]
    for axis, by in ((0, 4), (0, 2), (0, 1), (1, 8), (1, 4), (1, 2), (1, 1)):
        by = high.shape[axis] - by
        high, error = two_sum(high, pltpu.roll(high, by, axis=axis))
        low = (low + pltpu.roll(low, by, axis=axis)) + error
    spread = lambda x: jnp.concatenate(
        [jnp.broadcast_to(x[:1, PARTIALS * n : PARTIALS * n + 1], (1, LANES)) for n in range(8)], 0
    )
    high, low = spread(high), spread(low)
    row = lambda x, n: jnp.broadcast_to(x[n : n + 1], (8, LANES))
    shift = jnp.floor(64.0 * (row(high, 1) / row(high, 0)) + 0.5) * (1.0 / 64.0)
    centred = []
    for n in range(7):
        centred.append(row(high, 0) + row(low, 0))
        if n == 6:
            break
        wide = 4097.0 * high
        coarse = wide - (wide - high)
        fine = high - coarse
        following = jnp.concatenate([high[1:], high[:1]], 0)
        rest = jnp.concatenate([low[1:], low[:1]], 0) - shift * low
        total, error = two_sum(following, -shift * coarse)
        rest = rest + error
        total, error = two_sum(total, -shift * fine)
        rest = rest + error
        high = total + rest
        low = rest - (high - total)
    sigma = 1.0 - shift
    energies = [sigma * centred[n] - centred[n + 1] for n in range(6)]
    curvatures = [sigma * energies[n] - energies[n + 1] for n in range(5)]

    def product(p, q, table):
        return sum(p[i] * q[j] * table[i + j] for i in range(len(p)) for j in range(len(q)))

    one = jnp.ones((8, LANES), F32)
    none = jnp.zeros((8, LANES), F32)
    smoothed = [one]
    direction = [one]
    result = []
    energy = energies[0]
    for iteration in range(3):
        length = energy / product(direction, direction, curvatures)
        result = [
            (result[i] if i < len(result) else none) + length * direction[i]
            for i in range(len(direction))
        ]
        if iteration < 2:
            image = [sigma * d for d in direction] + [none]
            image = [image[i] - (direction[i - 1] if i else none) for i in range(len(image))]
            smoothed = [
                (smoothed[i] if i < len(smoothed) else none) - length * image[i]
                for i in range(len(image))
            ]
            following = product(smoothed, smoothed, energies)
            ratio = following / energy
            direction = [
                smoothed[i] + (ratio * direction[i] if i < len(direction) else none)
                for i in range(len(smoothed))
            ]
            energy = following
    k0, k1, k2 = result
    return k0 - shift * k1 + shift * shift * k2, k1 - 2.0 * shift * k2, k2


def last_kernel(
    sums_ref, b_ref, x0_ref, x1_ref, x2_ref, y1_ref, y2_ref, y3_ref, solution_hbm, residual_hbm,
    solution_ref, residual_ref, sems
):
    step = ROWS // CHUNKS
    k0, k1, k2 = coefficients([sums_ref[8 * n : 8 * n + 8] for n in range(16)])
    r0, r1, r2 = 1.0 - k0, k0 - k1, k1 - k2

    def copy(i, n):
        src = (solution_ref, residual_ref)[i]
        dst = (solution_hbm, residual_hbm)[i]
        rows = pl.ds(n * step, step)
        return pltpu.make_async_copy(src.at[:, rows, :], dst.at[:, rows, :], sems.at[i, n])

    for n in range(CHUNKS):

        def tile(t, carry):
            at = pl.ds(pl.multiple_of(8 * t - 8, 8), 8)
            wide = pl.ds(pl.multiple_of(8 * t + 8, 8), 8)
            for k in range(LEVELS):
                solution_ref[k, at, :] = (
                    k0 * x0_ref[k, wide, :] + k1 * x1_ref[k, wide, :] + k2 * x2_ref[k, wide, :]
                )
                residual_ref[k, at, :] = (
                    r0 * b_ref[k, at, :] + r1 * y1_ref[k, at, :]
                    + r2 * y2_ref[k, at, :] + k2 * y3_ref[k, at, :]
                )
            return carry

        lax.fori_loop(1 + n * step // 8, 1 + (n + 1) * step // 8, tile, 0)
        for i in range(2):
            copy(i, n).start()
    for n in range(CHUNKS):
        for i in range(2):
            copy(i, n).wait()


VMEM = pl.BlockSpec(memory_space=pltpu.VMEM)
ANY = pl.BlockSpec(memory_space=pl.ANY)
HBM = pl.BlockSpec(memory_space=pltpu.HBM)


def kept(*shape):
    return pltpu.VMEM(shape, F32)


def call(kernel, outs, ins, in_specs, out_specs=None, scratch=(), limit=8, flops=0, aliases=None):
    return pl.pallas_call(
        kernel,
        out_shape=outs,
        in_specs=in_specs,
        out_specs=[VMEM] * len(outs) if out_specs is None else out_specs,
        scratch_shapes=list(scratch),
        input_output_aliases=aliases or {},
        compiler_params=pltpu.CompilerParams(vmem_limit_bytes=limit * MIB),
        cost_estimate=pl.CostEstimate(flops=flops, bytes_accessed=1000000, transcendentals=0),
        name=kernel.__name__,
    )(*ins)


def on_device(right_side, helmholtz, coupling):
    right_side, helmholtz, coupling = [
        pltpu.with_memory_space_constraint(x, pltpu.HBM) for x in (right_side, helmholtz, coupling)
    ]
    low = pl.BlockSpec((LEVELS, 8, LANES), lambda i: (0, 0, 0))
    high = pl.BlockSpec((LEVELS, 8, LANES), lambda i: (0, ROWS // 8 - 1, 0))
    low_c = pl.BlockSpec((LEVELS - 1, 8, LANES), lambda i: (0, 0, 0))
    high_c = pl.BlockSpec((LEVELS - 1, 8, LANES), lambda i: (0, ROWS // 8 - 1, 0))
    message_rows = -(-(PAD + 3 * STACKED + 5) // 8) * 8
    rows_a, rows_b = pl.pallas_call(
        edge_rows_kernel,
        grid=(1,),
        out_shape=[kept(message_rows, LANES)] * 2,
        in_specs=[low, high, low, high, low_c, high_c],
        out_specs=[pl.BlockSpec((message_rows, LANES), lambda i: (0, 0))] * 2,
        name="edge_rows",
    )(right_side, right_side, helmholtz, helmholtz, coupling, coupling)
    rows_a = swap(rows_a, lat_even)
    rows_b = swap(rows_b, lat_odd)
    field = kept(LEVELS, EXTENDED, LANES)
    block = kept(LEVELS, ROWS, LANES)
    stack = kept(STACKED, 8, LANES)
    edges = kept(LEVELS, 8, LANES)
    message = kept(LANE_MESSAGE, 8, LANES)
    tile_scratch = lambda *n: pltpu.VMEM((*n, 8, LANES), F32)
    b, h, c, last, first = call(
        pack_kernel,
        [block, block, kept(LEVELS - 1, ROWS, LANES), stack, stack],
        [right_side, helmholtz, coupling],
        [HBM] * 3,
        scratch=[pltpu.SemaphoreType.DMA((3, CHUNKS))],
        flops=10000000,
    )
    halo, lanes_e, lanes_d = call(
        edge_lanes_kernel,
        [kept(2, 4, LEVELS, 8, LANES), message, message],
        [rows_a, rows_b, last, first],
        [VMEM] * 4,
        scratch=[tile_scratch(4, STACKED), tile_scratch(2, 4, LEVELS), tile_scratch(2, 2, LEVELS)],
    )
    scaled, inverse, ratio, x0, terms, edge0, sum0, y1 = call(
        first_kernel,
        [field] * 4 + [kept(4, 8 * TILES, LANES), edges, kept(8, LANES), block],
        [b, h, c, halo],
        [VMEM] * 4,
        flops=10000000,
    )
    lanes_e = swap(lanes_e, lon_even)
    lanes_d = swap(lanes_d, lon_odd)
    y1, x1, x2, y2, y3, sums = call(
        middle_kernel,
        [block, field, field, block, block, kept(128, LANES)],
        [scaled, inverse, ratio, x0, y1, terms, lanes_e, lanes_d, edge0, sum0],
        [VMEM] * 10,
        scratch=[tile_scratch(LEVELS)] * 4 + [tile_scratch(3, LEVELS)],
        flops=100000000,
        aliases={4: 0},
    )
    sums = lax.all_to_all(sums, AXES, 0, 0, tiled=True)
    result = jax.ShapeDtypeStruct((LEVELS, ROWS, LANES), F32)
    return call(
        last_kernel,
        [result, result],
        [sums, b, x0, x1, x2, y1, y2, y3],
        [VMEM] * 8,
        out_specs=[ANY, ANY],
        scratch=[
            pltpu.VMEM((LEVELS, ROWS, LANES), F32),
            pltpu.VMEM((LEVELS, ROWS, LANES), F32),
            pltpu.SemaphoreType.DMA((2, CHUNKS)),
        ],
        flops=10000000,
    )


def solution(mesh):
    spec = P(None, "lat", "lon")
    return jax.shard_map(
        lambda *args: tuple(on_device(*args)),
        mesh=mesh,
        in_specs=(spec,) * 3,
        out_specs=(spec,) * 2,
        check_vma=False,
    )
```

time: 64.5 us -> 57.1 us (0.89)
  Pallas kernels: 32.7 us -> 28.3 us
  blocking collectives: 18.5 us -> 15.9 us
  waiting for transfers between devices: 0.8 us -> 0.01 us
    pallas_call x5, Pallas kernels: 30.8 us -> 27.1 us  [call(): pl.pallas_call(kernel, out_shape=outs, in_specs=in_specs, out_specs=[VMEM...]
    all_to_all x1, blocking collectives: 18.5 us -> 15.9 us  [on_device(): sums = lax.all_to_all(sums, AXES, 0, 0, tiled=True)]
    ppermute x4, waiting for transfers between devices: 0.8 us -> 0.01 us  [swap(): return lax.ppermute(x, AXES, [(i, partner(i)) for i in range(128)])]
    pallas_call x1, Pallas kernels: 1.91 us -> 1.21 us  [on_device(): pl.pallas_call(edge_rows_kernel, grid=(1,), out_shape=[kept(message_rows,...]
  transfers between devices with their start and end apart: 4 -> 4, of which waited for: 1 -> 0; matrix products, arithmetic and copies ran while one was open for 0% -> 0% of each run, Pallas kernels for 20% -> 19%
where the time goes in v3:
time: 57.1 us; the launch traced here: 56.2 us
  Pallas kernels  28.3 us (50%)
  blocking collectives  15.9 us (28%)
  starting transfers between devices  11.3 us (20%)
  between operations  0.71 us (1%)
    pallas_call x5, Pallas kernels, call(): pl.pallas_call(kernel, out_shape=outs, in_specs=in_specs, out_specs=[VMEM...  27.1 us
    all_to_all x1, blocking collectives, on_device(): sums = lax.all_to_all(sums, AXES, 0, 0, tiled=True)  15.9 us
    ppermute x4, starting transfers between devices, swap(): return lax.ppermute(x, AXES, [(i, partner(i)) for i in range(128)])  11.3 us
    pallas_call x1, Pallas kernels, on_device(): pl.pallas_call(edge_rows_kernel, grid=(1,), out_shape=[kept(message_rows,...  1.21 us
  transfers between devices with their start and end apart: 4, of which 0 were waited for; matrix products, arithmetic and copies ran while one was open for 0% of the time, Pallas kernels for 19%

profile of v3, /device:TPU:0, one launch (start us, length us, event | category | flops | bytes accessed | tf_op | source)
XLA Modules:
  0.0 56.2 jit_solution(4360948467564038179)
XLA Ops:
  0.6 1.2 %edge_rows.1 = (f32[192,128]{1,0:T(8,128)S(1)}, f32[192,128]{1,0:T(8,128)S(1)}) custom-call(f32[20,256,128]{2,1,0:T(8,128)} %b_hi.1, f32[20,256,128]{2,1,0:T(8,128)} %b_hi.1, f32[20,256,128]{2,1,0:T(8,128)} %h_hi.1, f32[20,256,128]{2,1,0:T(8,128)} %h_hi.1, f32[19,256,128]{2,1,0:T(8,128)} %c_hi.1, f32[19,256,128]{2,1,0:T(8,128)} %c_hi.1), custom_call_target="tpu_custom_call" | custom-call | tf_op jit(solution)/shard_map/edge_rows/pallas_call | solution.py:676
  1.8 0.1 collective-permute-start
  1.9 3.2 %collective-permute-start.1 = (f32[192,128]{1,0:T(8,128)S(1)}, f32[192,128]{1,0:T(8,128)S(1)}, u32[]{:S(2)}, u32[]{:S(2)}) collective-permute-start(f32[192,128]{1,0:T(8,128)S(1)} %get-tuple-element.30), channel_id=1, source_target_pairs={{0,64},{1,2},{2,1},{3,67},{4,68},{5,6},{6,5},{7,71},{8,72},{9,10},... | collective-permute-start | bytes 294920 | tf_op jit(solution)/shard_map/ppermute | solution.py:32
  5.1 4.8 %pack_kernel.1 = (f32[20,256,128]{2,1,0:T(8,128)S(1)}, f32[20,256,128]{2,1,0:T(8,128)S(1)}, f32[19,256,128]{2,1,0:T(8,128)S(1)}, f32[59,8,128]{2,1,0:T(8,128)S(1)}, f32[59,8,128]{2,1,0:T(8,128)S(1)}) custom-call(f32[20,256,128]{2,1,0:T(8,128)} %b_hi.1, f32[20,256,128]{2,1,0:T(8,128)} %h_hi.1, f32[19,256,128]{2,1,0:T(8,128)} %c_hi.1), custom_call_target="tpu_custom_call" | custom-call | flops 10000000 | bytes 1000000 | tf_op jit(solution)/shard_map/pack_kernel/pallas_call | solution.py:654
  9.9 0.0 collective-permute-done.a_ref
  9.9 0.0 collective-permute-done.1.o_ref
  10.0 1.5 %edge_lanes_kernel.1 = (f32[2,4,20,8,128]{4,3,2,1,0:T(8,128)S(1)}, f32[33,8,128]{2,1,0:T(8,128)S(1)}, f32[33,8,128]{2,1,0:T(8,128)S(1)}) custom-call(f32[192,128]{1,0:T(8,128)S(1)} %collective-permute-done.a_ref, f32[192,128]{1,0:T(8,128)S(1)} %collective-permute-done.1.o_ref, f32[59,8,128]{2,1,0:T(8,128)S(1)} %get-tuple-element.31.last_ref, ...), custom_call_target="tpu_custom_call" | custom-call | bytes 1000000 | tf_op jit(solution)/shard_map/edge_lanes_kernel/pallas_call | solution.py:654
  11.5 1.7 %collective-permute-start.2 = (f32[33,8,128]{2,1,0:T(8,128)S(1)}, f32[33,8,128]{2,1,0:T(8,128)S(1)}, u32[]{:S(2)}, u32[]{:S(2)}) collective-permute-start(f32[33,8,128]{2,1,0:T(8,128)S(1)} %get-tuple-element.40), channel_id=1, source_target_pairs={{0,4},{1,5},{2,6},{3,7},{4,0},{5,1},{6,2},{7,3},{8,12},{9,13},{10,... | collective-permute-start | bytes 405512 | tf_op jit(solution)/shard_map/ppermute | solution.py:32
  13.1 6.4 %collective-permute-start.3 = (f32[33,8,128]{2,1,0:T(8,128)S(1)}, f32[33,8,128]{2,1,0:T(8,128)S(1)}, u32[]{:S(2)}, u32[]{:S(2)}) collective-permute-start(f32[33,8,128]{2,1,0:T(8,128)S(1)} %get-tuple-element.41), channel_id=1, source_target_pairs={{0,124},{1,125},{2,126},{3,127},{4,8},{5,9},{6,10},{7,11},{8,4},{9... | collective-permute-start | bytes 405512 | tf_op jit(solution)/shard_map/ppermute | solution.py:32
  19.5 6.0 %first_kernel.1 = (f32[20,288,128]{2,1,0:T(8,128)S(1)}, f32[20,288,128]{2,1,0:T(8,128)S(1)}, f32[20,288,128]{2,1,0:T(8,128)S(1)}, f32[20,288,128]{2,1,0:T(8,128)...) custom-call(f32[20,256,128]{2,1,0:T(8,128)S(1)} %get-tuple-element.2, ...), custom_call_target="tpu_custom_call" | custom-call | flops 10000000 | bytes 1000000 | tf_op jit(solution)/shard_map/first_kernel/pallas_call | solution.py:654
  25.5 0.0 collective-permute-done.2.e_ref
  25.5 0.0 collective-permute-done.3.d_ref
  25.6 11.6 %middle_kernel.1 = (f32[20,256,128]{2,1,0:T(8,128)S(1)}, f32[20,288,128]{2,1,0:T(8,128)S(1)}, f32[20,288,128]{2,1,0:T(8,128)S(1)}, f32[20,256,128]{2,1,0:T(8,128...) custom-call(f32[20,288,128]{2,1,0:T(8,128)S(1)} %get-tuple-element.34.scaled_ref, ...), custom_call_target="tpu_custom_call", output_to_operand_aliasing={{0}: (4, {})} | custom-call | flops 100000000 | bytes 1000000 | tf_op jit(solution)/shard_map/middle_kernel/pallas_call | solution.py:654
  37.2 15.9 %all_to_all.11 = f32[128,1,128]{2,1,0:T(1,128)S(1)} all-to-all(f32[128,1,128]{2,1,0:T(1,128)S(1)} %bitcast.5), channel_id=1, replica_groups=mesh['lon'=32,'lat'=4] {'lon','lat'}, dimensions={0} | all-to-all | bytes 131072 | tf_op jit(solution)/shard_map/all_to_all | solution.py:725
  53.1 3.1 %last_kernel.1 = (f32[20,256,128]{2,1,0:T(8,128)}, f32[20,256,128]{2,1,0:T(8,128)}) custom-call(f32[128,128]{1,0:T(8,128)S(1)} %bitcast.4, f32[20,256,128]{2,1,0:T(8,128)S(1)} %get-tuple-element.26.b_ref, f32[20,288,128]{2,1,0:T(8,128)S(1)} %get-tuple-element.37.x0_ref, f32[20,288,128]{2,1,0:T(8,128)S(1)} %get-tuple-element.45.x1_ref, ...), custom_call_target="tpu_custom_call" | custom-call | flops 10000000 | bytes 1000000 | tf_op jit(solution)/shard_map/last_kernel/pallas_call | solution.py:654
Async XLA Ops:
  1.8 8.1 %collective-permute-start = (f32[192,128]{1,0:T(8,128)S(1)}, f32[192,128]{1,0:T(8,128)S(1)}, u32[]{:S(2)}, u32[]{:S(2)}) collective-permute-start(f32[192,128]{1,0:T(8,128)S(1)} %get-tuple-element.29), channel_id=1, source_target_pairs={{0,1},{1,0},{2,3},{3,2},{4,5},{5,4},{6,7},{7,6},{8,9},{9,8},{10,11... | collective-permute-start | bytes 294920 | tf_op jit(solution)/shard_map/ppermute | solution.py:32
  1.9 8.0 %collective-permute-start.1 = (f32[192,128]{1,0:T(8,128)S(1)}, f32[192,128]{1,0:T(8,128)S(1)}, u32[]{:S(2)}, u32[]{:S(2)}) collective-permute-start(f32[192,128]{1,0:T(8,128)S(1)} %get-tuple-element.30), channel_id=1, source_target_pairs={{0,64},{1,2},{2,1},{3,67},{4,68},{5,6},{6,5},{7,71},{8,72},{9,10},... | collective-permute-start | bytes 294920 | tf_op jit(solution)/shard_map/ppermute | solution.py:32
  11.5 14.1 %collective-permute-start.2 = (f32[33,8,128]{2,1,0:T(8,128)S(1)}, f32[33,8,128]{2,1,0:T(8,128)S(1)}, u32[]{:S(2)}, u32[]{:S(2)}) collective-permute-start(f32[33,8,128]{2,1,0:T(8,128)S(1)} %get-tuple-element.40), channel_id=1, source_target_pairs={{0,4},{1,5},{2,6},{3,7},{4,0},{5,1},{6,2},{7,3},{8,12},{9,13},{10,... | collective-permute-start | bytes 405512 | tf_op jit(solution)/shard_map/ppermute | solution.py:32
  13.1 12.4 %collective-permute-start.3 = (f32[33,8,128]{2,1,0:T(8,128)S(1)}, f32[33,8,128]{2,1,0:T(8,128)S(1)}, u32[]{:S(2)}, u32[]{:S(2)}) collective-permute-start(f32[33,8,128]{2,1,0:T(8,128)S(1)} %get-tuple-element.41), channel_id=1, source_target_pairs={{0,124},{1,125},{2,126},{3,127},{4,8},{5,9},{6,10},{7,11},{8,4},{9... | collective-permute-start | bytes 405512 | tf_op jit(solution)/shard_map/ppermute | solution.py:32

commit v4 on v3

--- a/solution.py
+++ b/solution.py
@@ -129,7 +129,7 @@
     return last, first
 
 
-def edge_rows_kernel(b_lo, b_hi, h_lo, h_hi, c_lo, c_hi, a_ref, o_ref):
+def edge_rows_kernel(b_lo, b_hi, h_lo, h_hi, c_lo, c_hi, o_ref, a_ref):
     lat = lax.axis_index("lat")
     even = lat % 2 == 0
     levels = [
@@ -227,7 +227,11 @@
                 scaled_ref[k, wide, :] = halo_ref[n, 1, k]
                 ratio_ref[k, wide, :] = halo_ref[n, 3, k]
 
-    def tiles(g, total):
+    group = lane // 3
+    for k in range(LEVELS):
+        edge_ref[k] = jnp.zeros((8, LANES), F32)
+
+    def eliminated(g):
         work = []
         for n in range(4):
             at = pl.ds(pl.multiple_of(32 * g + 8 * n, 8), 8)
@@ -257,44 +261,37 @@
                 put,
                 get,
             ))
-        return total + sum(eliminate(work))
-
-    sum_ref[...] = lax.fori_loop(0, ROWS // 32, tiles, jnp.zeros((8, LANES), F32))
-    gather_edges(x_ref, edge_ref, range(TILES), lane // 3)
-
-    def neighbours(g, carry):
-        for n in range(4):
-            start = pl.multiple_of(32 * g + 8 * n + 16, 8)
-            here = pl.ds(pl.multiple_of(32 * g + 8 * n + 8, 8), 8)
-            over, north, south = [terms_ref[i, here, :] for i in range(1, 4)]
-            for k in range(LEVELS):
-                x = x_ref[k, pl.ds(start, 8), :]
+        return sum(eliminate(work))
+
+    def neighbours(tiles):
+        terms = [
+            [terms_ref[i, pl.ds(pl.multiple_of(8 * t, 8), 8), :] for i in range(1, 4)] for t in tiles
+        ]
+        for k in range(LEVELS):
+            edge = edge_ref[k]
+            for t, (over, north, south) in zip(tiles, terms):
+                start = pl.multiple_of(8 * t + 8, 8)
+                wide = pl.ds(start, 8)
+                x = x_ref[k, wide, :]
                 west = jnp.where(lane == 0, 0.0, pltpu.roll(x, 1, axis=1))
                 east = jnp.where(lane == LANES - 1, 0.0, pltpu.roll(x, LANES - 1, axis=1))
                 above = x_ref[k, pl.ds(start + 1, 8), :]
                 below = x_ref[k, pl.ds(start - 1, 8), :]
-                y_ref[k, pl.ds(pl.multiple_of(32 * g + 8 * n, 8), 8), :] = (
-                    over * (west + east) + north * above + south * below
-                )
-        return carry
-
-    lax.fori_loop(0, ROWS // 32, neighbours, 0)
-
-
-def gather_edges(x_ref, edge_ref, tiles, group):
-    def level(k, carry):
-        edge = jnp.zeros((8, LANES), F32)
-        for t in tiles:
-            turned = pltpu.roll(x_ref[k, pl.ds(8 * t + 8, 8), :], 3 * t + 2, axis=1)
-            edge = jnp.where(group == t, turned, edge)
-        edge_ref[k] = edge
-        return carry
-
-    lax.fori_loop(0, LEVELS, level, 0, unroll=2)
+                y_ref[k, wide, :] = over * (west + east) + north * above + south * below
+                edge = jnp.where(group == t, pltpu.roll(x, 3 * t + 2, axis=1), edge)
+            edge_ref[k] = edge
+
+    def both(g, total):
+        total = total + eliminated(g)
+        neighbours([4 * g - 4 + n for n in range(4)])
+        return total
+
+    sum_ref[...] = lax.fori_loop(1, ROWS // 32, both, eliminated(0))
+    neighbours(range(TILES - 6, TILES))
 
 
 def edge_lanes_kernel(
-    a_ref, o_ref, last_ref, first_ref, halo_ref, e_ref, d_ref, raw_ref, strip_ref, part_ref
+    o_ref, a_ref, last_ref, first_ref, halo_ref, d_ref, e_ref, raw_ref, strip_ref, part_ref
 ):
     even = lax.axis_index("lat") % 2 == 0
     lon_is_even = lax.axis_index("lon") % 2 == 0
@@ -394,7 +391,7 @@
 
 
 def middle_kernel(
-    scaled_ref, inverse_ref, ratio_ref, x0_ref, y1_in, terms_ref, e_ref, d_ref, edge0_ref, sum_ref,
+    scaled_ref, inverse_ref, ratio_ref, x0_ref, y1_in, terms_ref, d_ref, e_ref, edge0_ref, sum_ref,
     y1_ref, x1_ref, x2_ref, y2_ref, y3_ref, sums_ref, strip0_ref, strip_ref, further_ref, edge_ref,
     factor_ref
 ):
@@ -453,7 +450,7 @@
     def step(tiles, x_ref, y_ref, out_ref, halo_ref, sums, begun=False):
         starts = [pl.multiple_of(8 * t + 8, 8) for t in tiles]
         wides = [pl.ds(start, 8) for start in starts]
-        ats = [pl.ds(pl.multiple_of(8 * t - 8, 8), 8) for t in tiles]
+        ats = wides if begun else [pl.ds(pl.multiple_of(8 * t - 8, 8), 8) for t in tiles]
         terms = [
             [terms_ref[i, pl.ds(pl.multiple_of(8 * t, 8), 8), :] for i in range(1, 4)] for t in tiles
         ]
@@ -487,15 +484,22 @@
         if out_ref is not None:
             value = [f[-1] for f in forward]
             for k in range(LEVELS - 1, -1, -1):
-                for n in range(len(tiles)):
+                edge = edge_ref[k] if begun else None
+                for n, t in enumerate(tiles):
                     if k < LEVELS - 1:
                         value[n] = forward[n][k] + ratio_ref[k, wides[n], :] * value[n]
                     out_ref[k, wides[n], :] = value[n]
+                    if begun:
+                        edge = jnp.where(group == t, pltpu.roll(value[n], 3 * t + 2, axis=1), edge)
+                if begun:
+                    edge_ref[k] = edge
         if sums is not None:
             return sums[0] + sum(cross), sums[1] + sum(own)
 
     zero = jnp.zeros((8, LANES), F32)
     totals = [sum_ref[...]]
+    for k in range(LEVELS):
+        edge_ref[k] = zero
     solve_strip(first_right, strip_ref)
     for x_ref, y_ref, out_ref, halo_ref in (
         (x0_ref, y1_ref, x1_ref, strip0_ref),
@@ -512,10 +516,9 @@
             (zero, zero),
         )
         if out_ref is not None:
-            step([0, TILES - 1], x_ref, None, out_ref, halo_ref, None)
-        if x_ref is x0_ref:
-            gather_edges(out_ref, edge_ref, range(TILES), group)
-        elif x_ref is x1_ref:
+            begun = x_ref is x0_ref
+            step([0, TILES - 1], x_ref, y_ref, out_ref, halo_ref, None, begun)
+        if x_ref is x1_ref:
             solve_strip(second_right, strip_ref)
     row = zero[:1]
     for n, total in enumerate(totals):
@@ -628,7 +631,7 @@
                     k0 * x0_ref[k, wide, :] + k1 * x1_ref[k, wide, :] + k2 * x2_ref[k, wide, :]
                 )
                 residual_ref[k, at, :] = (
-                    r0 * b_ref[k, at, :] + r1 * y1_ref[k, at, :]
+                    r0 * b_ref[k, at, :] + r1 * y1_ref[k, wide, :]
                     + r2 * y2_ref[k, at, :] + k2 * y3_ref[k, at, :]
                 )
             return carry
@@ -673,7 +676,7 @@
     low_c = pl.BlockSpec((LEVELS - 1, 8, LANES), lambda i: (0, 0, 0))
     high_c = pl.BlockSpec((LEVELS - 1, 8, LANES), lambda i: (0, ROWS // 8 - 1, 0))
     message_rows = -(-(PAD + 3 * STACKED + 5) // 8) * 8
-    rows_a, rows_b = pl.pallas_call(
+    rows_b, rows_a = pl.pallas_call(
         edge_rows_kernel,
         grid=(1,),
         out_shape=[kept(message_rows, LANES)] * 2,
@@ -681,8 +684,8 @@
         out_specs=[pl.BlockSpec((message_rows, LANES), lambda i: (0, 0))] * 2,
         name="edge_rows",
     )(right_side, right_side, helmholtz, helmholtz, coupling, coupling)
+    rows_b = swap(rows_b, lat_odd)
     rows_a = swap(rows_a, lat_even)
-    rows_b = swap(rows_b, lat_odd)
     field = kept(LEVELS, EXTENDED, LANES)
     block = kept(LEVELS, ROWS, LANES)
     stack = kept(STACKED, 8, LANES)
@@ -697,26 +700,26 @@
         scratch=[pltpu.SemaphoreType.DMA((3, CHUNKS))],
         flops=10000000,
     )
-    halo, lanes_e, lanes_d = call(
+    halo, lanes_d, lanes_e = call(
         edge_lanes_kernel,
         [kept(2, 4, LEVELS, 8, LANES), message, message],
-        [rows_a, rows_b, last, first],
+        [rows_b, rows_a, last, first],
         [VMEM] * 4,
         scratch=[tile_scratch(4, STACKED), tile_scratch(2, 4, LEVELS), tile_scratch(2, 2, LEVELS)],
     )
     scaled, inverse, ratio, x0, terms, edge0, sum0, y1 = call(
         first_kernel,
-        [field] * 4 + [kept(4, 8 * TILES, LANES), edges, kept(8, LANES), block],
+        [field] * 4 + [kept(4, 8 * TILES, LANES), edges, kept(8, LANES), field],
         [b, h, c, halo],
         [VMEM] * 4,
         flops=10000000,
     )
+    lanes_d = swap(lanes_d, lon_odd)
     lanes_e = swap(lanes_e, lon_even)
-    lanes_d = swap(lanes_d, lon_odd)
     y1, x1, x2, y2, y3, sums = call(
         middle_kernel,
-        [block, field, field, block, block, kept(128, LANES)],
-        [scaled, inverse, ratio, x0, y1, terms, lanes_e, lanes_d, edge0, sum0],
+        [field, field, field, block, block, kept(128, LANES)],
+        [scaled, inverse, ratio, x0, y1, terms, lanes_d, lanes_e, edge0, sum0],
         [VMEM] * 10,
         scratch=[tile_scratch(LEVELS)] * 4 + [tile_scratch(3, LEVELS)],
         flops=100000000,

time: 57.1 us -> 53.4 us (0.935)
  Pallas kernels: 28.3 us -> 24.2 us
  blocking collectives: 15.9 us -> 17 us
  starting transfers between devices: 11.3 us -> 10.5 us
    pallas_call x5, Pallas kernels: 27.1 us -> 23 us  [call(): pl.pallas_call(kernel, out_shape=outs, in_specs=in_specs, out_specs=[VMEM...]
    all_to_all x1, blocking collectives: 15.9 us -> 17 us  [on_device(): sums = lax.all_to_all(sums, AXES, 0, 0, tiled=True)]
    ppermute x4, starting transfers between devices: 11.3 us -> 10.5 us  [swap(): return lax.ppermute(x, AXES, [(i, partner(i)) for i in range(128)])]
  transfers between devices with their start and end apart: 4 -> 4, of which waited for: 0 -> 1; matrix products, arithmetic and copies ran while one was open for 0% -> 0% of each run, Pallas kernels for 19% -> 19%
where the time goes in v4:
time: 53.4 us; the launch traced here: 52.6 us
  Pallas kernels  24.2 us (45%)
  blocking collectives  17 us (32%)
  starting transfers between devices  10.5 us (20%)
  between operations  0.69 us (1%)
    pallas_call x5, Pallas kernels, call(): pl.pallas_call(kernel, out_shape=outs, in_specs=in_specs, out_specs=[VMEM...  23 us
    all_to_all x1, blocking collectives, on_device(): sums = lax.all_to_all(sums, AXES, 0, 0, tiled=True)  17 us
    ppermute x4, starting transfers between devices, swap(): return lax.ppermute(x, AXES, [(i, partner(i)) for i in range(128)])  10.5 us
    pallas_call x1, Pallas kernels, on_device(): pl.pallas_call(edge_rows_kernel, grid=(1,), out_shape=[kept(message_rows,...  1.21 us
  transfers between devices with their start and end apart: 4, of which 1 were waited for; matrix products, arithmetic and copies ran while one was open for 0% of the time, Pallas kernels for 19%

profile of v4, /device:TPU:0, one launch (start us, length us, event | category | flops | bytes accessed | tf_op | source)
XLA Modules:
  0.0 52.6 jit_solution(8723662318979546244)
XLA Ops:
  0.6 1.2 %edge_rows.1 = (f32[192,128]{1,0:T(8,128)S(1)}, f32[192,128]{1,0:T(8,128)S(1)}) custom-call(f32[20,256,128]{2,1,0:T(8,128)} %b_hi.1, f32[20,256,128]{2,1,0:T(8,128)} %b_hi.1, f32[20,256,128]{2,1,0:T(8,128)} %h_hi.1, f32[20,256,128]{2,1,0:T(8,128)} %h_hi.1, f32[19,256,128]{2,1,0:T(8,128)} %c_hi.1, f32[19,256,128]{2,1,0:T(8,128)} %c_hi.1), custom_call_target="tpu_custom_call" | custom-call | tf_op jit(solution)/shard_map/edge_rows/pallas_call | solution.py:679
  1.8 3.2 %collective-permute-start = (f32[192,128]{1,0:T(8,128)S(1)}, f32[192,128]{1,0:T(8,128)S(1)}, u32[]{:S(2)}, u32[]{:S(2)}) collective-permute-start(f32[192,128]{1,0:T(8,128)S(1)} %get-tuple-element.29), channel_id=1, source_target_pairs={{0,64},{1,2},{2,1},{3,67},{4,68},{5,6},{6,5},{7,71},{8,72},{9,10},... | collective-permute-start | bytes 294920 | tf_op jit(solution)/shard_map/ppermute | solution.py:32
  5.0 0.0 collective-permute-start.1
  5.0 4.8 %pack_kernel.1 = (f32[20,256,128]{2,1,0:T(8,128)S(1)}, f32[20,256,128]{2,1,0:T(8,128)S(1)}, f32[19,256,128]{2,1,0:T(8,128)S(1)}, f32[59,8,128]{2,1,0:T(8,128)S(1)}, f32[59,8,128]{2,1,0:T(8,128)S(1)}) custom-call(f32[20,256,128]{2,1,0:T(8,128)} %b_hi.1, f32[20,256,128]{2,1,0:T(8,128)} %h_hi.1, f32[19,256,128]{2,1,0:T(8,128)} %c_hi.1), custom_call_target="tpu_custom_call" | custom-call | flops 10000000 | bytes 1000000 | tf_op jit(solution)/shard_map/pack_kernel/pallas_call | solution.py:657
  9.8 0.0 collective-permute-done.o_ref
  9.9 0.0 collective-permute-done.1.a_ref
  9.9 1.5 %edge_lanes_kernel.1 = (f32[2,4,20,8,128]{4,3,2,1,0:T(8,128)S(1)}, f32[33,8,128]{2,1,0:T(8,128)S(1)}, f32[33,8,128]{2,1,0:T(8,128)S(1)}) custom-call(f32[192,128]{1,0:T(8,128)S(1)} %collective-permute-done.o_ref, f32[192,128]{1,0:T(8,128)S(1)} %collective-permute-done.1.a_ref, f32[59,8,128]{2,1,0:T(8,128)S(1)} %get-tuple-element.31.last_ref, ...), custom_call_target="tpu_custom_call" | custom-call | bytes 1000000 | tf_op jit(solution)/shard_map/edge_lanes_kernel/pallas_call | solution.py:657
  11.4 7.3 %collective-permute-start.2 = (f32[33,8,128]{2,1,0:T(8,128)S(1)}, f32[33,8,128]{2,1,0:T(8,128)S(1)}, u32[]{:S(2)}, u32[]{:S(2)}) collective-permute-start(f32[33,8,128]{2,1,0:T(8,128)S(1)} %get-tuple-element.40), channel_id=1, source_target_pairs={{0,124},{1,125},{2,126},{3,127},{4,8},{5,9},{6,10},{7,11},{8,4},{9... | collective-permute-start | bytes 405512 | tf_op jit(solution)/shard_map/ppermute | solution.py:32
  18.7 0.0 collective-permute-start.3
  18.7 4.9 %first_kernel.1 = (f32[20,288,128]{2,1,0:T(8,128)S(1)}, f32[20,288,128]{2,1,0:T(8,128)S(1)}, f32[20,288,128]{2,1,0:T(8,128)S(1)}, f32[20,288,128]{2,1,0:T(8,128)...) custom-call(f32[20,256,128]{2,1,0:T(8,128)S(1)} %get-tuple-element.2, ...), custom_call_target="tpu_custom_call" | custom-call | flops 10000000 | bytes 1000000 | tf_op jit(solution)/shard_map/first_kernel/pallas_call | solution.py:657
  23.6 0.0 collective-permute-done.2.d_ref
  23.6 0.2 collective-permute-done.3.e_ref
  23.9 8.6 %middle_kernel.1 = (f32[20,288,128]{2,1,0:T(8,128)S(1)}, f32[20,288,128]{2,1,0:T(8,128)S(1)}, f32[20,288,128]{2,1,0:T(8,128)S(1)}, f32[20,256,128]{2,1,0:T(8,128...) custom-call(f32[20,288,128]{2,1,0:T(8,128)S(1)} %get-tuple-element.34.scaled_ref, ...), custom_call_target="tpu_custom_call", output_to_operand_aliasing={{0}: (4, {})} | custom-call | flops 100000000 | bytes 1000000 | tf_op jit(solution)/shard_map/middle_kernel/pallas_call | solution.py:657
  32.5 17.0 %all_to_all.11 = f32[128,1,128]{2,1,0:T(1,128)S(1)} all-to-all(f32[128,1,128]{2,1,0:T(1,128)S(1)} %bitcast.5), channel_id=1, replica_groups=mesh['lon'=32,'lat'=4] {'lon','lat'}, dimensions={0} | all-to-all | bytes 131072 | tf_op jit(solution)/shard_map/all_to_all | solution.py:728
  49.5 3.1 %last_kernel.1 = (f32[20,256,128]{2,1,0:T(8,128)}, f32[20,256,128]{2,1,0:T(8,128)}) custom-call(f32[128,128]{1,0:T(8,128)S(1)} %bitcast.4, f32[20,256,128]{2,1,0:T(8,128)S(1)} %get-tuple-element.26.b_ref, f32[20,288,128]{2,1,0:T(8,128)S(1)} %get-tuple-element.37.x0_ref, f32[20,288,128]{2,1,0:T(8,128)S(1)} %get-tuple-element.45.x1_ref, ...), custom_call_target="tpu_custom_call" | custom-call | flops 10000000 | bytes 1000000 | tf_op jit(solution)/shard_map/last_kernel/pallas_call | solution.py:657
Async XLA Ops:
  1.8 8.0 %collective-permute-start = (f32[192,128]{1,0:T(8,128)S(1)}, f32[192,128]{1,0:T(8,128)S(1)}, u32[]{:S(2)}, u32[]{:S(2)}) collective-permute-start(f32[192,128]{1,0:T(8,128)S(1)} %get-tuple-element.29), channel_id=1, source_target_pairs={{0,64},{1,2},{2,1},{3,67},{4,68},{5,6},{6,5},{7,71},{8,72},{9,10},... | collective-permute-start | bytes 294920 | tf_op jit(solution)/shard_map/ppermute | solution.py:32
  5.0 4.8 %collective-permute-start.1 = (f32[192,128]{1,0:T(8,128)S(1)}, f32[192,128]{1,0:T(8,128)S(1)}, u32[]{:S(2)}, u32[]{:S(2)}) collective-permute-start(f32[192,128]{1,0:T(8,128)S(1)} %get-tuple-element.30), channel_id=1, source_target_pairs={{0,1},{1,0},{2,3},{3,2},{4,5},{5,4},{6,7},{7,6},{8,9},{9,8},{10,11... | collective-permute-start | bytes 294920 | tf_op jit(solution)/shard_map/ppermute | solution.py:32
  11.4 12.3 %collective-permute-start.2 = (f32[33,8,128]{2,1,0:T(8,128)S(1)}, f32[33,8,128]{2,1,0:T(8,128)S(1)}, u32[]{:S(2)}, u32[]{:S(2)}) collective-permute-start(f32[33,8,128]{2,1,0:T(8,128)S(1)} %get-tuple-element.40), channel_id=1, source_target_pairs={{0,124},{1,125},{2,126},{3,127},{4,8},{5,9},{6,10},{7,11},{8,4},{9... | collective-permute-start | bytes 405512 | tf_op jit(solution)/shard_map/ppermute | solution.py:32
  18.7 5.2 %collective-permute-start.3 = (f32[33,8,128]{2,1,0:T(8,128)S(1)}, f32[33,8,128]{2,1,0:T(8,128)S(1)}, u32[]{:S(2)}, u32[]{:S(2)}) collective-permute-start(f32[33,8,128]{2,1,0:T(8,128)S(1)} %get-tuple-element.41), channel_id=1, source_target_pairs={{0,4},{1,5},{2,6},{3,7},{4,0},{5,1},{6,2},{7,3},{8,12},{9,13},{10,... | collective-permute-start | bytes 405512 | tf_op jit(solution)/shard_map/ppermute | solution.py:32

commit v5 on v4

--- a/solution.py
+++ b/solution.py
@@ -19,7 +19,8 @@
 AT_H = LEVELS
 AT_C = 2 * LEVELS
 CHUNKS = 8
-GROUP = 8
+PACKS = 2
+GROUP = 16
 PARTIALS = 16
 PAD = 8
 LANE_MESSAGE = LEVELS + (2 * LEVELS + 1) // 3
@@ -179,7 +180,7 @@
                 o_ref[pl.ds(PAD + 3 * j + i, 1), :] = hi[k, pl.ds(7 - i, 1), :]
 
 
-def pack_kernel(b_hbm, h_hbm, c_hbm, b_ref, h_ref, c_ref, last_ref, first_ref, sems):
+def pack_kernel(b_hbm, h_hbm, c_hbm, b_ref, h_ref, c_ref, last_ref, first_ref, terms_ref, sems):
     arrays = (
         (b_hbm, b_ref, 0, LEVELS),
         (h_hbm, h_ref, AT_H, LEVELS),
@@ -187,16 +188,20 @@
     )
     parts = []
     for i, (src, dst, at, count) in enumerate(arrays):
-        for n in range(CHUNKS):
-            lo, hi = count * n // CHUNKS, count * (n + 1) // CHUNKS
+        for n in range(PACKS):
+            lo, hi = count * n // PACKS, count * (n + 1) // PACKS
             levels = pl.ds(lo, hi - lo)
             copy = pltpu.make_async_copy(src.at[levels], dst.at[levels], sems.at[i, n])
             copy.start()
             parts.append((copy, dst, at, lo, hi))
     lane = lane_index()
-    for copy, source, at, lo, hi in parts:
+    sub = sub_index()
+    base = lax.axis_index("lat") * ROWS
+    for n, (copy, source, at, lo, hi) in enumerate(parts):
         copy.wait()
-
+        for t in range(n, TILES, len(parts)):
+            for i, term in enumerate(row_terms((base + 8 * t - 8 + sub).astype(F32))):
+                terms_ref[i, pl.ds(8 * t, 8), :] = term
         for k in range(lo, hi):
             last, first = packed_edges(lambda t: source[k, pl.ds(8 * t - 8, 8), :], lane)
             last_ref[at + k] = last
@@ -204,20 +209,10 @@
 
 
 def first_kernel(
-    b_ref, h_ref, c_ref, halo_ref, scaled_ref, inverse_ref, ratio_ref, x_ref, terms_ref, edge_ref,
+    b_ref, h_ref, c_ref, halo_ref, terms_ref, scaled_ref, inverse_ref, ratio_ref, x_ref, edge_ref,
     sum_ref, y_ref
 ):
-    base = lax.axis_index("lat") * ROWS
     lane = lane_index()
-    sub = sub_index()
-
-    def row_term(t, carry):
-        row = (base + 8 * t - 8 + sub).astype(F32)
-        for i, term in enumerate(row_terms(row)):
-            terms_ref[i, pl.ds(pl.multiple_of(8 * t, 8), 8), :] = term
-        return carry
-
-    lax.fori_loop(0, TILES, row_term, 0, unroll=2)
     for n, t in ((0, 0), (1, TILES - 1)):
         for k in range(LEVELS):
             wide = pl.ds(8 * t + 8, 8)
@@ -392,8 +387,8 @@
 
 def middle_kernel(
     scaled_ref, inverse_ref, ratio_ref, x0_ref, y1_in, terms_ref, d_ref, e_ref, edge0_ref, sum_ref,
-    y1_ref, x1_ref, x2_ref, y2_ref, y3_ref, sums_ref, strip0_ref, strip_ref, further_ref, edge_ref,
-    factor_ref
+    y1_ref, x1_ref, x2_ref, y2_ref, y3_ref, sums_ref, strip0_ref, strip_ref, strip2_ref, further_ref,
+    edge_ref, factor_ref
 ):
     del y1_in
     base = lax.axis_index("lat") * ROWS
@@ -504,22 +499,21 @@
     for x_ref, y_ref, out_ref, halo_ref in (
         (x0_ref, y1_ref, x1_ref, strip0_ref),
         (x1_ref, y2_ref, x2_ref, strip_ref),
-        (x2_ref, y3_ref, None, strip_ref),
+        (x2_ref, y3_ref, None, strip2_ref),
     ):
+        begun = x_ref is x0_ref
+        if out_ref is not None:
+            step([0, TILES - 1], x_ref, y_ref, out_ref, halo_ref, None, begun)
+        if x_ref is x1_ref:
+            solve_strip(second_right, strip2_ref)
         totals += lax.fori_loop(
             0,
             ROWS // 8 // GROUP,
             lambda g, sums: step(
-                [GROUP * g + n + 1 for n in range(GROUP)], x_ref, y_ref, out_ref, halo_ref, sums,
-                x_ref is x0_ref
+                [GROUP * g + n + 1 for n in range(GROUP)], x_ref, y_ref, out_ref, halo_ref, sums, begun
             ),
             (zero, zero),
         )
-        if out_ref is not None:
-            begun = x_ref is x0_ref
-            step([0, TILES - 1], x_ref, y_ref, out_ref, halo_ref, None, begun)
-        if x_ref is x1_ref:
-            solve_strip(second_right, strip_ref)
     row = zero[:1]
     for n, total in enumerate(totals):
         part = jnp.sum(total, axis=0, keepdims=True)
@@ -692,12 +686,12 @@
     edges = kept(LEVELS, 8, LANES)
     message = kept(LANE_MESSAGE, 8, LANES)
     tile_scratch = lambda *n: pltpu.VMEM((*n, 8, LANES), F32)
-    b, h, c, last, first = call(
+    b, h, c, last, first, terms = call(
         pack_kernel,
-        [block, block, kept(LEVELS - 1, ROWS, LANES), stack, stack],
+        [block, block, kept(LEVELS - 1, ROWS, LANES), stack, stack, kept(4, 8 * TILES, LANES)],
         [right_side, helmholtz, coupling],
         [HBM] * 3,
-        scratch=[pltpu.SemaphoreType.DMA((3, CHUNKS))],
+        scratch=[pltpu.SemaphoreType.DMA((3, PACKS))],
         flops=10000000,
     )
     halo, lanes_d, lanes_e = call(
@@ -707,11 +701,11 @@
         [VMEM] * 4,
         scratch=[tile_scratch(4, STACKED), tile_scratch(2, 4, LEVELS), tile_scratch(2, 2, LEVELS)],
     )
-    scaled, inverse, ratio, x0, terms, edge0, sum0, y1 = call(
+    scaled, inverse, ratio, x0, edge0, sum0, y1 = call(
         first_kernel,
-        [field] * 4 + [kept(4, 8 * TILES, LANES), edges, kept(8, LANES), field],
-        [b, h, c, halo],
-        [VMEM] * 4,
+        [field] * 4 + [edges, kept(8, LANES), field],
+        [b, h, c, halo, terms],
+        [VMEM] * 5,
         flops=10000000,
     )
     lanes_d = swap(lanes_d, lon_odd)
@@ -721,7 +715,7 @@
         [field, field, field, block, block, kept(128, LANES)],
         [scaled, inverse, ratio, x0, y1, terms, lanes_d, lanes_e, edge0, sum0],
         [VMEM] * 10,
-        scratch=[tile_scratch(LEVELS)] * 4 + [tile_scratch(3, LEVELS)],
+        scratch=[tile_scratch(LEVELS)] * 5 + [tile_scratch(3, LEVELS)],
         flops=100000000,
         aliases={4: 0},
     )

time: 53.4 us -> 52.7 us (0.987)
  Pallas kernels: 24.2 us -> 22.3 us
  starting transfers between devices: 10.5 us -> 11.4 us
    pallas_call x5, Pallas kernels: 23 us -> 21.1 us  [call(): pl.pallas_call(kernel, out_shape=outs, in_specs=in_specs, out_specs=[VMEM...]
    ppermute x4, starting transfers between devices: 10.5 us -> 11.4 us  [swap(): return lax.ppermute(x, AXES, [(i, partner(i)) for i in range(128)])]
  transfers between devices with their start and end apart: 4 -> 4, of which waited for: 1 -> 2; matrix products, arithmetic and copies ran while one was open for 0% -> 0% of each run, Pallas kernels for 19% -> 16%
where the time goes in v5:
time: 52.7 us; the launch traced here: 51.9 us
  Pallas kernels  22.3 us (42%)
  blocking collectives  16.8 us (32%)
  starting transfers between devices  11.4 us (22%)
  waiting for transfers between devices  0.73 us (1%)
  between operations  0.68 us (1%)
    pallas_call x5, Pallas kernels, call(): pl.pallas_call(kernel, out_shape=outs, in_specs=in_specs, out_specs=[VMEM...  21.1 us
    all_to_all x1, blocking collectives, on_device(): sums = lax.all_to_all(sums, AXES, 0, 0, tiled=True)  16.8 us
    ppermute x4, starting transfers between devices, swap(): return lax.ppermute(x, AXES, [(i, partner(i)) for i in range(128)])  11.4 us
    pallas_call x1, Pallas kernels, on_device(): pl.pallas_call(edge_rows_kernel, grid=(1,), out_shape=[kept(message_rows,...  1.21 us
  transfers between devices with their start and end apart: 4, of which 2 were waited for; matrix products, arithmetic and copies ran while one was open for 0% of the time, Pallas kernels for 16%

profile of v5, /device:TPU:0, one launch (start us, length us, event | category | flops | bytes accessed | tf_op | source)
XLA Modules:
  0.0 51.9 jit_solution(17814716454830573814)
XLA Ops:
  0.6 1.2 %edge_rows.1 = (f32[192,128]{1,0:T(8,128)S(1)}, f32[192,128]{1,0:T(8,128)S(1)}) custom-call(f32[20,256,128]{2,1,0:T(8,128)} %b_hi.1, f32[20,256,128]{2,1,0:T(8,128)} %b_hi.1, f32[20,256,128]{2,1,0:T(8,128)} %h_hi.1, f32[20,256,128]{2,1,0:T(8,128)} %h_hi.1, f32[19,256,128]{2,1,0:T(8,128)} %c_hi.1, f32[19,256,128]{2,1,0:T(8,128)} %c_hi.1), custom_call_target="tpu_custom_call" | custom-call | tf_op jit(solution)/shard_map/edge_rows/pallas_call | solution.py:673
  1.8 3.2 %collective-permute-start = (f32[192,128]{1,0:T(8,128)S(1)}, f32[192,128]{1,0:T(8,128)S(1)}, u32[]{:S(2)}, u32[]{:S(2)}) collective-permute-start(f32[192,128]{1,0:T(8,128)S(1)} %get-tuple-element.29), channel_id=1, source_target_pairs={{0,64},{1,2},{2,1},{3,67},{4,68},{5,6},{6,5},{7,71},{8,72},{9,10},... | collective-permute-start | bytes 294920 | tf_op jit(solution)/shard_map/ppermute | solution.py:33
  5.0 0.0 collective-permute-start.1
  5.0 3.8 %pack_kernel.1 = (f32[20,256,128]{2,1,0:T(8,128)S(1)}, f32[20,256,128]{2,1,0:T(8,128)S(1)}, f32[19,256,128]{2,1,0:T(8,128)S(1)}, f32[59,8,128]{2,1,0:T(8,128)S(1...) custom-call(f32[20,256,128]{2,1,0:T(8,128)} %b_hi.1, f32[20,256,128]{2,1,0:T(8,128)} %h_hi.1, f32[19,256,128]{2,1,0:T(8,128)} %c_hi.1), custom_call_target="tpu_custom_call" | custom-call | flops 10000000 | bytes 1000000 | tf_op jit(solution)/shard_map/pack_kernel/pallas_call | solution.py:651
  8.9 0.1 collective-permute-done.o_ref
  8.9 0.0 collective-permute-done.1.a_ref
  8.9 1.5 %edge_lanes_kernel.1 = (f32[2,4,20,8,128]{4,3,2,1,0:T(8,128)S(1)}, f32[33,8,128]{2,1,0:T(8,128)S(1)}, f32[33,8,128]{2,1,0:T(8,128)S(1)}) custom-call(f32[192,128]{1,0:T(8,128)S(1)} %collective-permute-done.o_ref, f32[192,128]{1,0:T(8,128)S(1)} %collective-permute-done.1.a_ref, f32[59,8,128]{2,1,0:T(8,128)S(1)} %get-tuple-element.31.last_ref, ...), custom_call_target="tpu_custom_call" | custom-call | bytes 1000000 | tf_op jit(solution)/shard_map/edge_lanes_kernel/pallas_call | solution.py:651
  10.5 8.2 %collective-permute-start.2 = (f32[33,8,128]{2,1,0:T(8,128)S(1)}, f32[33,8,128]{2,1,0:T(8,128)S(1)}, u32[]{:S(2)}, u32[]{:S(2)}) collective-permute-start(f32[33,8,128]{2,1,0:T(8,128)S(1)} %get-tuple-element.40), channel_id=1, source_target_pairs={{0,124},{1,125},{2,126},{3,127},{4,8},{5,9},{6,10},{7,11},{8,4},{9... | collective-permute-start | bytes 405512 | tf_op jit(solution)/shard_map/ppermute | solution.py:33
  18.7 0.0 collective-permute-start.3
  18.7 4.3 %first_kernel.1 = (f32[20,288,128]{2,1,0:T(8,128)S(1)}, f32[20,288,128]{2,1,0:T(8,128)S(1)}, f32[20,288,128]{2,1,0:T(8,128)S(1)}, f32[20,288,128]{2,1,0:T(8,128)...) custom-call(f32[20,256,128]{2,1,0:T(8,128)S(1)} %get-tuple-element.26.b_ref, ...), custom_call_target="tpu_custom_call" | custom-call | flops 10000000 | bytes 1000000 | tf_op jit(solution)/shard_map/first_kernel/pallas_call | solution.py:651
  23.0 0.0 collective-permute-done.2.d_ref
  23.0 0.6 %collective-permute-done.3.e_ref = f32[33,8,128]{2,1,0:T(8,128)S(1)} collective-permute-done((f32[33,8,128]{2,1,0:T(8,128)S(1)}, f32[33,8,128]{2,1,0:T(8,128)S(1)}, u32[]{:S(2)}, u32[]{:S(2)}) %collective-permute-start.3) | collective-permute-done | bytes 135200 | tf_op jit(solution)/shard_map/ppermute | solution.py:33
  23.7 8.3 %middle_kernel.1 = (f32[20,288,128]{2,1,0:T(8,128)S(1)}, f32[20,288,128]{2,1,0:T(8,128)S(1)}, f32[20,288,128]{2,1,0:T(8,128)S(1)}, f32[20,256,128]{2,1,0:T(8,128...) custom-call(f32[20,288,128]{2,1,0:T(8,128)S(1)} %get-tuple-element.35.scaled_ref, ...), custom_call_target="tpu_custom_call", output_to_operand_aliasing={{0}: (4, {})} | custom-call | flops 100000000 | bytes 1000000 | tf_op jit(solution)/shard_map/middle_kernel/pallas_call | solution.py:651
  32.0 16.8 %all_to_all.11 = f32[128,1,128]{2,1,0:T(1,128)S(1)} all-to-all(f32[128,1,128]{2,1,0:T(1,128)S(1)} %bitcast.5), channel_id=1, replica_groups=mesh['lon'=32,'lat'=4] {'lon','lat'}, dimensions={0} | all-to-all | bytes 131072 | tf_op jit(solution)/shard_map/all_to_all | solution.py:722
  48.7 3.1 %last_kernel.1 = (f32[20,256,128]{2,1,0:T(8,128)}, f32[20,256,128]{2,1,0:T(8,128)}) custom-call(f32[128,128]{1,0:T(8,128)S(1)} %bitcast.4, f32[20,256,128]{2,1,0:T(8,128)S(1)} %get-tuple-element.26.b_ref, f32[20,288,128]{2,1,0:T(8,128)S(1)} %get-tuple-element.38.x0_ref, f32[20,288,128]{2,1,0:T(8,128)S(1)} %get-tuple-element.45.x1_ref, ...), custom_call_target="tpu_custom_call" | custom-call | flops 10000000 | bytes 1000000 | tf_op jit(solution)/shard_map/last_kernel/pallas_call | solution.py:651
Async XLA Ops:
  1.8 7.1 %collective-permute-start = (f32[192,128]{1,0:T(8,128)S(1)}, f32[192,128]{1,0:T(8,128)S(1)}, u32[]{:S(2)}, u32[]{:S(2)}) collective-permute-start(f32[192,128]{1,0:T(8,128)S(1)} %get-tuple-element.29), channel_id=1, source_target_pairs={{0,64},{1,2},{2,1},{3,67},{4,68},{5,6},{6,5},{7,71},{8,72},{9,10},... | collective-permute-start | bytes 294920 | tf_op jit(solution)/shard_map/ppermute | solution.py:33
  5.0 3.9 %collective-permute-start.1 = (f32[192,128]{1,0:T(8,128)S(1)}, f32[192,128]{1,0:T(8,128)S(1)}, u32[]{:S(2)}, u32[]{:S(2)}) collective-permute-start(f32[192,128]{1,0:T(8,128)S(1)} %get-tuple-element.30), channel_id=1, source_target_pairs={{0,1},{1,0},{2,3},{3,2},{4,5},{5,4},{6,7},{7,6},{8,9},{9,8},{10,11... | collective-permute-start | bytes 294920 | tf_op jit(solution)/shard_map/ppermute | solution.py:33
  10.5 12.6 %collective-permute-start.2 = (f32[33,8,128]{2,1,0:T(8,128)S(1)}, f32[33,8,128]{2,1,0:T(8,128)S(1)}, u32[]{:S(2)}, u32[]{:S(2)}) collective-permute-start(f32[33,8,128]{2,1,0:T(8,128)S(1)} %get-tuple-element.40), channel_id=1, source_target_pairs={{0,124},{1,125},{2,126},{3,127},{4,8},{5,9},{6,10},{7,11},{8,4},{9... | collective-permute-start | bytes 405512 | tf_op jit(solution)/shard_map/ppermute | solution.py:33
  18.7 5.0 %collective-permute-start.3 = (f32[33,8,128]{2,1,0:T(8,128)S(1)}, f32[33,8,128]{2,1,0:T(8,128)S(1)}, u32[]{:S(2)}, u32[]{:S(2)}) collective-permute-start(f32[33,8,128]{2,1,0:T(8,128)S(1)} %get-tuple-element.41), channel_id=1, source_target_pairs={{0,4},{1,5},{2,6},{3,7},{4,0},{5,1},{6,2},{7,3},{8,12},{9,13},{10,... | collective-permute-start | bytes 405512 | tf_op jit(solution)/shard_map/ppermute | solution.py:33

commit v6 on v5

--- a/solution.py
+++ b/solution.py
@@ -19,7 +19,7 @@
 AT_H = LEVELS
 AT_C = 2 * LEVELS
 CHUNKS = 8
-PACKS = 2
+PACKS = 3
 GROUP = 16
 PARTIALS = 16
 PAD = 8
@@ -130,9 +130,18 @@
     return last, first
 
 
-def edge_rows_kernel(b_lo, b_hi, h_lo, h_hi, c_lo, c_hi, o_ref, a_ref):
+def edge_rows_kernel(
+    b_hbm, h_hbm, c_hbm, o_ref, a_ref, b_lo, b_hi, h_lo, h_hi, c_lo, c_hi, sems
+):
+    copies = []
+    for i, (src, low, high) in enumerate(((b_hbm, b_lo, b_hi), (h_hbm, h_lo, h_hi), (c_hbm, c_lo, c_hi))):
+        for n, (dst, at) in enumerate(((low, 0), (high, ROWS - 8))):
+            copies.append(pltpu.make_async_copy(src.at[:, pl.ds(at, 8), :], dst, sems.at[i, n]))
+            copies[-1].start()
     lat = lax.axis_index("lat")
     even = lat % 2 == 0
+    for copy in copies:
+        copy.wait()
     levels = [
         (at + k, lo, hi, k)
         for at, count, lo, hi in (
@@ -188,8 +197,8 @@
     )
     parts = []
     for i, (src, dst, at, count) in enumerate(arrays):
-        for n in range(PACKS):
-            lo, hi = count * n // PACKS, count * (n + 1) // PACKS
+        cuts = (0, 3, count // 2, count) if i == 0 else (0, count // 2, count)
+        for n, (lo, hi) in enumerate(zip(cuts, cuts[1:])):
             levels = pl.ds(lo, hi - lo)
             copy = pltpu.make_async_copy(src.at[levels], dst.at[levels], sems.at[i, n])
             copy.start()
@@ -665,19 +674,17 @@
     right_side, helmholtz, coupling = [
         pltpu.with_memory_space_constraint(x, pltpu.HBM) for x in (right_side, helmholtz, coupling)
     ]
-    low = pl.BlockSpec((LEVELS, 8, LANES), lambda i: (0, 0, 0))
-    high = pl.BlockSpec((LEVELS, 8, LANES), lambda i: (0, ROWS // 8 - 1, 0))
-    low_c = pl.BlockSpec((LEVELS - 1, 8, LANES), lambda i: (0, 0, 0))
-    high_c = pl.BlockSpec((LEVELS - 1, 8, LANES), lambda i: (0, ROWS // 8 - 1, 0))
     message_rows = -(-(PAD + 3 * STACKED + 5) // 8) * 8
-    rows_b, rows_a = pl.pallas_call(
+    tile_scratch = lambda *n: pltpu.VMEM((*n, 8, LANES), F32)
+    rows_b, rows_a = call(
         edge_rows_kernel,
-        grid=(1,),
-        out_shape=[kept(message_rows, LANES)] * 2,
-        in_specs=[low, high, low, high, low_c, high_c],
-        out_specs=[pl.BlockSpec((message_rows, LANES), lambda i: (0, 0))] * 2,
-        name="edge_rows",
-    )(right_side, right_side, helmholtz, helmholtz, coupling, coupling)
+        [kept(message_rows, LANES)] * 2,
+        [right_side, helmholtz, coupling],
+        [HBM] * 3,
+        scratch=[tile_scratch(LEVELS)] * 4
+        + [tile_scratch(LEVELS - 1)] * 2
+        + [pltpu.SemaphoreType.DMA((3, 2))],
+    )
     rows_b = swap(rows_b, lat_odd)
     rows_a = swap(rows_a, lat_even)
     field = kept(LEVELS, EXTENDED, LANES)
@@ -685,7 +692,6 @@
     stack = kept(STACKED, 8, LANES)
     edges = kept(LEVELS, 8, LANES)
     message = kept(LANE_MESSAGE, 8, LANES)
-    tile_scratch = lambda *n: pltpu.VMEM((*n, 8, LANES), F32)
     b, h, c, last, first, terms = call(
         pack_kernel,
         [block, block, kept(LEVELS - 1, ROWS, LANES), stack, stack, kept(4, 8 * TILES, LANES)],

time: 52.7 us -> 52.7 us (level)
    pallas_call x5 -> x6, Pallas kernels: 21.1 us -> 22.3 us  [call(): pl.pallas_call(kernel, out_shape=outs, in_specs=in_specs, out_specs=[VMEM...]
    pallas_call x1 -> x0, Pallas kernels: 1.21 us -> none  [on_device(): pl.pallas_call(edge_rows_kernel, grid=(1,), out_shape=[kept(message_rows,...]
where the time goes in v6:
time: 52.7 us; the launch traced here: 51.9 us
  Pallas kernels  22.3 us (42%)
  blocking collectives  16.8 us (32%)
  starting transfers between devices  11.4 us (22%)
  waiting for transfers between devices  0.72 us (1%)
  between operations  0.68 us (1%)
    pallas_call x6, Pallas kernels, call(): pl.pallas_call(kernel, out_shape=outs, in_specs=in_specs, out_specs=[VMEM...  22.3 us
    all_to_all x1, blocking collectives, on_device(): sums = lax.all_to_all(sums, AXES, 0, 0, tiled=True)  16.8 us
    ppermute x4, starting transfers between devices, swap(): return lax.ppermute(x, AXES, [(i, partner(i)) for i in range(128)])  11.4 us
  transfers between devices with their start and end apart: 4, of which 2 were waited for; matrix products, arithmetic and copies ran while one was open for 0% of the time, Pallas kernels for 16%

profile of v6, /device:TPU:0, one launch (start us, length us, event | category | flops | bytes accessed | tf_op | source)
XLA Modules:
  0.0 51.9 jit_solution(9867912854259810935)
XLA Ops:
  0.6 1.3 %edge_rows_kernel.1 = (f32[192,128]{1,0:T(8,128)S(1)}, f32[192,128]{1,0:T(8,128)S(1)}) custom-call(f32[20,256,128]{2,1,0:T(8,128)} %b_hbm.3, f32[20,256,128]{2,1,0:T(8,128)} %h_hbm.3, f32[19,256,128]{2,1,0:T(8,128)} %c_hbm.3), custom_call_target="tpu_custom_call" | custom-call | bytes 1000000 | tf_op jit(solution)/shard_map/edge_rows_kernel/pallas_call | solution.py:660
  1.9 3.2 %collective-permute-start = (f32[192,128]{1,0:T(8,128)S(1)}, f32[192,128]{1,0:T(8,128)S(1)}, u32[]{:S(2)}, u32[]{:S(2)}) collective-permute-start(f32[192,128]{1,0:T(8,128)S(1)} %get-tuple-element.29), channel_id=1, source_target_pairs={{0,64},{1,2},{2,1},{3,67},{4,68},{5,6},{6,5},{7,71},{8,72},{9,10},... | collective-permute-start | bytes 294920 | tf_op jit(solution)/shard_map/ppermute | solution.py:33
  5.1 0.0 collective-permute-start.1
  5.1 3.8 %pack_kernel.1 = (f32[20,256,128]{2,1,0:T(8,128)S(1)}, f32[20,256,128]{2,1,0:T(8,128)S(1)}, f32[19,256,128]{2,1,0:T(8,128)S(1)}, f32[59,8,128]{2,1,0:T(8,128)S(1...) custom-call(f32[20,256,128]{2,1,0:T(8,128)} %b_hbm.3, f32[20,256,128]{2,1,0:T(8,128)} %h_hbm.3, ...), custom_call_target="tpu_custom_call" | custom-call | flops 10000000 | bytes 1000000 | tf_op jit(solution)/shard_map/pack_kernel/pallas_call | solution.py:660
  8.9 0.1 collective-permute-done.o_ref
  9.0 0.0 collective-permute-done.1.a_ref
  9.0 1.5 %edge_lanes_kernel.1 = (f32[2,4,20,8,128]{4,3,2,1,0:T(8,128)S(1)}, f32[33,8,128]{2,1,0:T(8,128)S(1)}, f32[33,8,128]{2,1,0:T(8,128)S(1)}) custom-call(f32[192,128]{1,0:T(8,128)S(1)} %collective-permute-done.o_ref, f32[192,128]{1,0:T(8,128)S(1)} %collective-permute-done.1.a_ref, f32[59,8,128]{2,1,0:T(8,128)S(1)} %get-tuple-element.31.last_ref, ...), custom_call_target="tpu_custom_call" | custom-call | bytes 1000000 | tf_op jit(solution)/shard_map/edge_lanes_kernel/pallas_call | solution.py:660
  10.5 8.2 %collective-permute-start.2 = (f32[33,8,128]{2,1,0:T(8,128)S(1)}, f32[33,8,128]{2,1,0:T(8,128)S(1)}, u32[]{:S(2)}, u32[]{:S(2)}) collective-permute-start(f32[33,8,128]{2,1,0:T(8,128)S(1)} %get-tuple-element.40), channel_id=1, source_target_pairs={{0,124},{1,125},{2,126},{3,127},{4,8},{5,9},{6,10},{7,11},{8,4},{9... | collective-permute-start | bytes 405512 | tf_op jit(solution)/shard_map/ppermute | solution.py:33
  18.7 0.0 collective-permute-start.3
  18.7 4.3 %first_kernel.1 = (f32[20,288,128]{2,1,0:T(8,128)S(1)}, f32[20,288,128]{2,1,0:T(8,128)S(1)}, f32[20,288,128]{2,1,0:T(8,128)S(1)}, f32[20,288,128]{2,1,0:T(8,128)...) custom-call(f32[20,256,128]{2,1,0:T(8,128)S(1)} %get-tuple-element.26.b_ref, ...), custom_call_target="tpu_custom_call" | custom-call | flops 10000000 | bytes 1000000 | tf_op jit(solution)/shard_map/first_kernel/pallas_call | solution.py:660
  23.1 0.0 collective-permute-done.2.d_ref
  23.1 0.6 %collective-permute-done.3.e_ref = f32[33,8,128]{2,1,0:T(8,128)S(1)} collective-permute-done((f32[33,8,128]{2,1,0:T(8,128)S(1)}, f32[33,8,128]{2,1,0:T(8,128)S(1)}, u32[]{:S(2)}, u32[]{:S(2)}) %collective-permute-start.3) | collective-permute-done | bytes 135200 | tf_op jit(solution)/shard_map/ppermute | solution.py:33
  23.7 8.3 %middle_kernel.1 = (f32[20,288,128]{2,1,0:T(8,128)S(1)}, f32[20,288,128]{2,1,0:T(8,128)S(1)}, f32[20,288,128]{2,1,0:T(8,128)S(1)}, f32[20,256,128]{2,1,0:T(8,128...) custom-call(f32[20,288,128]{2,1,0:T(8,128)S(1)} %get-tuple-element.35.scaled_ref, ...), custom_call_target="tpu_custom_call", output_to_operand_aliasing={{0}: (4, {})} | custom-call | flops 100000000 | bytes 1000000 | tf_op jit(solution)/shard_map/middle_kernel/pallas_call | solution.py:660
  32.0 16.8 %all_to_all.11 = f32[128,1,128]{2,1,0:T(1,128)S(1)} all-to-all(f32[128,1,128]{2,1,0:T(1,128)S(1)} %bitcast.5), channel_id=1, replica_groups=mesh['lon'=32,'lat'=4] {'lon','lat'}, dimensions={0} | all-to-all | bytes 131072 | tf_op jit(solution)/shard_map/all_to_all | solution.py:728
  48.8 3.1 %last_kernel.1 = (f32[20,256,128]{2,1,0:T(8,128)}, f32[20,256,128]{2,1,0:T(8,128)}) custom-call(f32[128,128]{1,0:T(8,128)S(1)} %bitcast.4, f32[20,256,128]{2,1,0:T(8,128)S(1)} %get-tuple-element.26.b_ref, f32[20,288,128]{2,1,0:T(8,128)S(1)} %get-tuple-element.38.x0_ref, f32[20,288,128]{2,1,0:T(8,128)S(1)} %get-tuple-element.45.x1_ref, ...), custom_call_target="tpu_custom_call" | custom-call | flops 10000000 | bytes 1000000 | tf_op jit(solution)/shard_map/last_kernel/pallas_call | solution.py:660
Async XLA Ops:
  1.9 7.1 %collective-permute-start = (f32[192,128]{1,0:T(8,128)S(1)}, f32[192,128]{1,0:T(8,128)S(1)}, u32[]{:S(2)}, u32[]{:S(2)}) collective-permute-start(f32[192,128]{1,0:T(8,128)S(1)} %get-tuple-element.29), channel_id=1, source_target_pairs={{0,64},{1,2},{2,1},{3,67},{4,68},{5,6},{6,5},{7,71},{8,72},{9,10},... | collective-permute-start | bytes 294920 | tf_op jit(solution)/shard_map/ppermute | solution.py:33
  5.1 3.9 %collective-permute-start.1 = (f32[192,128]{1,0:T(8,128)S(1)}, f32[192,128]{1,0:T(8,128)S(1)}, u32[]{:S(2)}, u32[]{:S(2)}) collective-permute-start(f32[192,128]{1,0:T(8,128)S(1)} %get-tuple-element.30), channel_id=1, source_target_pairs={{0,1},{1,0},{2,3},{3,2},{4,5},{5,4},{6,7},{7,6},{8,9},{9,8},{10,11... | collective-permute-start | bytes 294920 | tf_op jit(solution)/shard_map/ppermute | solution.py:33
  10.5 12.6 %collective-permute-start.2 = (f32[33,8,128]{2,1,0:T(8,128)S(1)}, f32[33,8,128]{2,1,0:T(8,128)S(1)}, u32[]{:S(2)}, u32[]{:S(2)}) collective-permute-start(f32[33,8,128]{2,1,0:T(8,128)S(1)} %get-tuple-element.40), channel_id=1, source_target_pairs={{0,124},{1,125},{2,126},{3,127},{4,8},{5,9},{6,10},{7,11},{8,4},{9... | collective-permute-start | bytes 405512 | tf_op jit(solution)/shard_map/ppermute | solution.py:33
  18.7 5.0 %collective-permute-start.3 = (f32[33,8,128]{2,1,0:T(8,128)S(1)}, f32[33,8,128]{2,1,0:T(8,128)S(1)}, u32[]{:S(2)}, u32[]{:S(2)}) collective-permute-start(f32[33,8,128]{2,1,0:T(8,128)S(1)} %get-tuple-element.41), channel_id=1, source_target_pairs={{0,4},{1,5},{2,6},{3,7},{4,0},{5,1},{6,2},{7,3},{8,12},{9,13},{10,... | collective-permute-start | bytes 405512 | tf_op jit(solution)/shard_map/ppermute | solution.py:33
